TPU v7x, 512 devices: a whole 4x8x8 slice. The times are simulated.
512 devices in a mesh: ctx: 64 (over y, z), head: 8 (over x, core).
Axes of the slice: x: 4, y: 8, z: 8, core: 2. Of those that a mesh axis runs over, the one named last changes fastest.
Arguments:
- queries: bfloat16 [8192, 4096], P('ctx', 'head'), may hold values from -6 to 6
- keys: bfloat16 [8192, 4096], P('ctx', 'head'), may hold values from -6 to 6
- values: bfloat16 [8192, 4096], P('ctx', 'head'), may hold values from -6 to 6
- out_weight: bfloat16 [4096, 4096], P('head', 'ctx'), may hold values from -0.25 to 0.25
- grad_out: bfloat16 [8192, 4096], P('ctx', 'head'), may hold values from -6 to 6
Outputs:
- mixed: bfloat16 [8192, 4096], P('ctx', 'head')
- grad_queries: bfloat16 [8192, 4096], P('ctx', 'head')
- grad_keys: bfloat16 [8192, 4096], P('ctx', 'head')
- grad_values: bfloat16 [8192, 4096], P('ctx', 'head')
All inputs are finite; a program needn't handle non-finite values.
Results may differ from a plain program's by a relative error of at most 0.017.
Values may be sent and summed in bfloat16 or wider, within the bound.
No kernel may reach another device: no remote copies, remote signals or barrier semaphores. Data moves between devices by JAX's collectives and lax.ppermute only.
A program may use at most 64 MiB of HBM per device.

v0:
```python
import jax
import jax.numpy as jnp
from jax import lax
from jax.sharding import PartitionSpec as P

HEAD_DIM = 128


epsilon = 1e-06


def carried_in(value, axis, combine, identity):
    size, place = (lax.axis_size(axis), lax.axis_index(axis))
    everything = lax.all_gather(value, axis)
    start = jnp.broadcast_to(jnp.asarray(identity, value.dtype), value.shape)

    def lap(k, before):
        reached = k < place
        new = combine(before, everything[k])
        return jnp.where(reached, new, before)

    return lax.fori_loop(0, size, lap, start)


def carried_in_2(value, axis, join, neutral):
    count = lax.axis_size(axis)
    place = lax.axis_index(axis)
    ahead = count - 1 - place
    gathered = lax.all_gather(value.astype(jnp.bfloat16), axis)
    state = jnp.zeros_like(value) + jnp.asarray(neutral, value.dtype)

    def one(lap, state):
        source = count - 1 - lap
        return join(state, lax.dynamic_index_in_dim(gathered, source, 0, False).astype(value.dtype))

    return lax.fori_loop(0, ahead, one, state)


def add_states(earlier, later):
    return earlier + later


def local(queries, keys, values, out_weight, grad_out):
    length = queries.shape[0]
    heads = queries.shape[1] // HEAD_DIM
    highest = lax.Precision.HIGHEST
    query_heads = queries.reshape(length, heads, HEAD_DIM)
    key_heads = keys.reshape(length, heads, HEAD_DIM)
    value_heads = values.reshape(length, heads, HEAD_DIM)
    causal = jnp.tril(jnp.ones((length, length), dtype=bool))[None]
    scores = jnp.einsum("ihe,jhe->hij", query_heads, key_heads, preferred_element_type=jnp.float32)
    attn_weights = jnp.where(causal, scores, 0.0).astype(jnp.bfloat16)
    local_state = jnp.einsum(
        "ihd,ihe->hde", key_heads, value_heads, preferred_element_type=jnp.float32
    )
    before = carried_in(local_state, "ctx", add_states, jnp.zeros_like(local_state))
    query_float = query_heads.astype(jnp.float32)
    within = jnp.einsum(
        "hij,jhe->ihe", attn_weights, value_heads, preferred_element_type=jnp.float32
    )
    carried = jnp.einsum("ihd,hde->ihe", query_float, before, precision=highest)
    attended = within + carried
    scale_rows = lax.rsqrt(jnp.mean(attended * attended, axis=-1, keepdims=True) + epsilon)
    normed = attended * scale_rows
    flat_normed = normed.astype(jnp.bfloat16).reshape(length, heads * HEAD_DIM)
    full_weight = lax.all_gather(out_weight, "ctx", axis=1, tiled=True)
    partial_value = jnp.dot(flat_normed, full_weight, preferred_element_type=jnp.float32)
    mixed = lax.psum_scatter(
        partial_value.astype(jnp.bfloat16), "head", scatter_dimension=1, tiled=True
    )
    grad_full = lax.all_gather(grad_out, "head", axis=1, tiled=True)
    contract_last = (((1,), (1,)), ((), ()))
    grad_normed = lax.dot_general(
        grad_full, full_weight, contract_last, preferred_element_type=jnp.float32
    )
    grad_normed = grad_normed.reshape(length, heads, HEAD_DIM)
    grad_attended = scale_rows * (
        grad_normed - normed * jnp.mean(grad_normed * normed, axis=-1, keepdims=True)
    )
    grad_heads = grad_attended.astype(jnp.bfloat16)
    local_grad = jnp.einsum(
        "ihd,ihe->hde", query_heads, grad_heads, preferred_element_type=jnp.float32
    )
    after = carried_in_2(local_grad, "ctx", add_states, jnp.zeros_like(local_grad))
    grad_scores = jnp.einsum(
        "ihe,jhe->hij", grad_heads, value_heads, preferred_element_type=jnp.float32
    )
    grad_scores = jnp.where(causal, grad_scores, 0.0).astype(jnp.bfloat16)
    grad_query = jnp.einsum(
        "hij,jhd->ihd", grad_scores, key_heads, preferred_element_type=jnp.float32
    )
    grad_query = grad_query + jnp.einsum(
        "ihe,hde->ihd", grad_heads.astype(jnp.float32), before, precision=highest
    )
    grad_key = jnp.einsum(
        "hij,ihd->jhd", grad_scores, query_heads, preferred_element_type=jnp.float32
    )
    grad_key = grad_key + jnp.einsum(
        "jhe,hde->jhd", value_heads.astype(jnp.float32), after, precision=highest
    )
    grad_value = jnp.einsum(
        "hij,ihe->jhe", attn_weights, grad_heads, preferred_element_type=jnp.float32
    )
    grad_value = grad_value + jnp.einsum(
        "jhd,hde->jhe", key_heads.astype(jnp.float32), after, precision=highest
    )
    width = heads * HEAD_DIM
    return (
        mixed,
        grad_query.astype(jnp.bfloat16).reshape(length, width),
        grad_key.astype(jnp.bfloat16).reshape(length, width),
        grad_value.astype(jnp.bfloat16).reshape(length, width),
    )


def solution(mesh):
    return jax.shard_map(
        local,
        mesh=mesh,
        in_specs=(
            P("ctx", "head"),
            P("ctx", "head"),
            P("ctx", "head"),
            P("head", "ctx"),
            P("ctx", "head"),
        ),
        out_specs=(P("ctx", "head"), P("ctx", "head"), P("ctx", "head"), P("ctx", "head")),
        check_vma=False,
    )
```

profile of v0, /device:TPU:6, one launch (start us, length us, event | category | flops | bytes accessed | tf_op | source)
XLA Modules:
  0.0 447.7 jit_solution(2987400718012066501)
XLA Ops:
  7.2 1.1 copy.99
  8.3 1.8 fusion.12
  11.7 1.1 fusion.3
  12.8 1.1 convolution_bitcast_fusion.5
  14.0 141.7 %all-gather.11.cloned.1.call-done = f32[256,128,128]{2,1,0:T(8,128)} async-done(((f32[4,128,128]{2,1,0:T(8,128)}), f32[256,128,128]{2,1,0:T(8,128)}) %all-gather.11.cloned.1.call-update) | async-done | bytes 16777232 | tf_op jit(solution)/shard_map/all_gather | solution.py:14
  155.7 68.1 %while.27 = (s32[]{:T(128)}, f32[4,128,128]{2,1,0:T(8,128)S(1)}, s32[]{:T(128)}, f32[64,4,128,128]{3,2,1,0:T(8,128)}, s32[]{:T(128)}, /*index=5*/s32[]{:T(128)}) while((s32[]{:T(128)}, f32[4,128,128]{2,1,0:T(8,128)S(1)}, s32[]{:T(128)}, f32[64,4,128,128]{3,2,1,0:T(8,128)}, s32[]{:T(128)}, /*index=5*/s32[]{:T(128)}) %tuple.79), condition=%wide.region_1.2_spmd.clone, body=%wide.region_0.1_spmd.clone.sunk | while | flops 196612 | bytes 786525 | solution.py:22
  156.7 1.0 add_select_fusion.2
  158.9 1.0 add_select_fusion.2
  161.0 1.0 add_select_fusion.2
  169.5 1.0 add_select_fusion.2
  173.8 1.0 add_select_fusion.2
  174.8 1.0 add_select_fusion.2
  179.1 1.0 add_select_fusion.2
  182.3 1.0 add_select_fusion.2
  201.4 1.0 add_select_fusion.2
  202.5 1.0 add_select_fusion.2
  208.9 1.0 add_select_fusion.2
  217.4 1.0 add_select_fusion.2
  220.6 1.0 add_select_fusion.2
  224.3 50.5 %all-gather.7.cloned.1.call-done = bf16[512,4096]{0,1:T(8,128)(2,1)} async-done(((bf16[512,64]{0,1:T(8,128)(2,1)}), bf16[512,4096]{0,1:T(8,128)(2,1)}) %all-gather.7.cloned.1.call-update) | async-done | bytes 4194320 | tf_op jit(solution)/shard_map/all_gather | solution.py:66
  274.7 4.3 multiply_reduce_fusion
  280.6 4.7 %convolution_convert_fusion = bf16[128,4096]{1,0:T(8,128)(2,1)} fusion(bf16[128,512]{0,1:T(8,128)(2,1)S(1)} %bitcast.126, bf16[512,4096]{0,1:T(8,128)(2,1)} %all-gather.7.cloned.1.call-done), kind=kOutput, calls=%fused_computation.2 | convolution fusion | flops 537395200 | bytes 5373952 | tf_op jit(solution)/shard_map/dot_general | solution.py:67
  286.8 89.5 %all-gather.13.cloned.1.call-done = bf16[256,128,128]{2,1,0:T(8,128)(2,1)} async-done(((bf16[4,128,128]{2,1,0:T(8,128)(2,1)}), bf16[256,128,128]{2,1,0:T(8,128)(2,1)}) %all-gather.13.cloned.1.call-update) | async-done | bytes 8388624 | tf_op jit(solution)/shard_map/all_gather | solution.py:29
  376.3 62.5 %while.26 = (s32[]{:T(128)}, f32[4,128,128]{2,1,0:T(8,128)S(1)}, s32[]{:T(128)}, bf16[64,4,128,128]{3,2,1,0:T(8,128)(2,1)}, s32[]{:T(128)}, /*index=5*/s32[]{:T(128)}, s32[]{:T(128)}, s32[]{:T(128)}) while((s32[]{:T(128)}, f32[4,128,128]{2,1,0:T(8,128)S(1)}, s32[]{:T(128)}, bf16[64,4,128,128]{3,2,1,0:T(8,128)(2,1)}, s32[]{:T(128)}, ...), condition=%wide.region_6.7_spmd, body=%wide.region_5.6_spmd.sunk | while | flops 131078 | bytes 655495 | solution.py:36
  (151 shorter events, 121.1 us)
Async XLA Ops:
  7.2 4.5 %copy-start = (bf16[128,512]{1,0:T(8,128)(2,1)S(1)}, bf16[128,512]{1,0:T(8,128)(2,1)}, u32[]{:S(2)}) copy-start(bf16[128,512]{1,0:T(8,128)(2,1)} %param.9) | copy-start | bytes 393220
  7.2 148.5 %all-gather.11.cloned.1.call-start = ((), (), s32[]{:S(2)}) async-start(), calls=%async_computation.4 | async-start | bytes 17039360 | tf_op jit(solution)/shard_map/all_gather | solution.py:14
  10.1 214.1 %all-gather.9.cloned.1.call-start = ((), (), s32[]{:S(2)}) async-start(), calls=%async_computation.3 | async-start | bytes 1179648 | tf_op jit(solution)/shard_map/all_gather | solution.py:71
  10.9 263.9 %all-gather.7.cloned.1.call-start = ((), (), s32[]{:S(2)}) async-start(), calls=%async_computation.1 | async-start | bytes 4259840 | tf_op jit(solution)/shard_map/all_gather | solution.py:66
  11.6 364.7 %all-gather.13.cloned.1.call-start = ((), (), s32[]{:S(2)}) async-start(), calls=%async_computation.5 | async-start | bytes 8519680 | tf_op jit(solution)/shard_map/all_gather | solution.py:29
  223.8 56.3 %copy-start.1 = (bf16[128,512]{1,0:T(8,128)(2,1)S(1)}, bf16[128,512]{1,0:T(8,128)(2,1)}, u32[]{:S(2)}) copy-start(bf16[128,512]{1,0:T(8,128)(2,1)} %param.11) | copy-start | bytes 393220
  280.0 161.1 %reduce-scatter.2.cloned.1.call-start = ((), (), s32[]{:S(2)}) async-start(), calls=%async_computation.2 | async-start | bytes 1179648 | tf_op jit(solution)/shard_map/reduce_scatter | solution.py:68
  285.3 153.5 %copy-start.2 = (bf16[128,512]{1,0:T(8,128)(2,1)S(1)}, bf16[128,512]{1,0:T(8,128)(2,1)}, u32[]{:S(2)}) copy-start(bf16[128,512]{1,0:T(8,128)(2,1)} %param.10) | copy-start | bytes 393220
Sparse Core Ops, SparseCore 0:
  11.0 144.5 all-gather.10
  157.8 25.5 all-gather.8
  186.4 88.2 all-gather.6
  280.2 96.0 all-gather.12
  379.5 32.1 reduce-scatter.1
where the time goes:
time: 452 us; the launch traced here: 448 us
  waiting for transfers between devices  283 us (63%)
  other arithmetic  127 us (28%)
  matrix products  15.5 us (3%)
  between operations  14 us (3%)
    all_gather x1, waiting for transfers between devices, carried_in(): everything = lax.all_gather(value, axis)  142 us
    all_gather x1, waiting for transfers between devices, carried_in_2(): gathered = lax.all_gather(value.astype(jnp.bfloat16), axis)  89.5 us
    select_n x64, other arithmetic, lap(): return jnp.where(reached, new, before)  66.6 us
    add x63, other arithmetic, add_states(): return earlier + later  60.7 us
    all_gather x1, waiting for transfers between devices, local(): full_weight = lax.all_gather(out_weight, 'ctx', axis=1, tiled=True)  50.5 us
  transfers between devices with their start and end apart: 5, of which 3 were waited for; matrix products, arithmetic and copies ran while one was open for 31% of the time, Pallas kernels for 0%

commit v1 on v0

v1 whole, which is shorter than its diff:
```python
import functools

import jax
import jax.numpy as jnp
from jax import lax
from jax.experimental import pallas as pl
from jax.experimental.pallas import tpu as pltpu
from jax.sharding import Mesh, PartitionSpec as P

HEAD_DIM = 128
HEADS_DEV = 4
TOK = 128
WIDTH = HEADS_DEV * HEAD_DIM
EPSILON = 1e-06
F32 = jnp.float32
BF16 = jnp.bfloat16
Z = ("z",)
CTX = ("y", "z")

NN = (((1,), (0,)), ((), ()))
NT = (((1,), (1,)), ((), ()))
TN = (((0,), (0,)), ((), ()))


def mm(a, b, dims):
    return lax.dot_general(a, b, dims, preferred_element_type=F32)


def head(h):
    return slice(h * HEAD_DIM, (h + 1) * HEAD_DIM)


def causal():
    rows = lax.broadcasted_iota(jnp.int32, (TOK, TOK), 0)
    cols = lax.broadcasted_iota(jnp.int32, (TOK, TOK), 1)
    return rows >= cols


def cost(flops, nbytes):
    return pl.CostEstimate(flops=flops, bytes_accessed=nbytes, transcendentals=0)


def state_kernel(k_ref, v_ref, out_ref):
    for h in range(HEADS_DEV):
        out_ref[head(h), :] = mm(k_ref[:, head(h)], v_ref[:, head(h)], TN).astype(out_ref.dtype)


def local_state(keys, values):
    return pl.pallas_call(
        state_kernel,
        out_shape=jax.ShapeDtypeStruct((WIDTH, HEAD_DIM), BF16),
        cost_estimate=cost(2 * TOK * WIDTH * HEAD_DIM, 400000),
        name="local_state",
    )(keys, values)


def scan_kernel(reverse, in_ref, out_ref):
    pairs = in_ref.shape[0] // 16
    total = jnp.zeros((8, HEAD_DIM), F32)
    order = range(pairs - 1, -1, -1) if reverse else range(pairs)
    for i in order:
        rows = slice(16 * i, 16 * i + 16)
        both = in_ref[rows, :].astype(F32)
        low, high = both[:8], both[8:]
        if reverse:
            then = total + high
            out_ref[rows, :] = jnp.concatenate([then, total], axis=0).astype(out_ref.dtype)
            total = then + low
        else:
            then = total + low
            out_ref[rows, :] = jnp.concatenate([total, then], axis=0).astype(out_ref.dtype)
            total = then + high


def exclusive_scan(pieces, reverse):
    return pl.pallas_call(
        functools.partial(scan_kernel, reverse),
        out_shape=jax.ShapeDtypeStruct(pieces.shape, pieces.dtype),
        cost_estimate=cost(WIDTH * HEAD_DIM, 300000),
        name="scan_states",
    )(pieces)


def carried(state, reverse):
    pieces = lax.all_to_all(state.reshape(64, 8, HEAD_DIM), CTX, 0, 0)
    sums = exclusive_scan(pieces.reshape(WIDTH, HEAD_DIM), reverse)
    back = lax.all_to_all(sums.reshape(64, 8, HEAD_DIM), CTX, 0, 0)
    return back.reshape(WIDTH, HEAD_DIM)


def attend_kernel(q_ref, k_ref, v_ref, s_ref, flat_ref, normed_ref, scale_ref, p_ref):
    keep = causal()
    for h in range(HEADS_DEV):
        q, k, v = q_ref[:, head(h)], k_ref[:, head(h)], v_ref[:, head(h)]
        weights = jnp.where(keep, mm(q, k, NT), 0.0).astype(BF16)
        p_ref[:, head(h)] = weights
        attended = mm(weights, v, NN) + mm(q, s_ref[head(h), :], NN)
        scale = lax.rsqrt(jnp.mean(attended * attended, axis=-1, keepdims=True) + EPSILON)
        normed = attended * scale
        flat_ref[:, head(h)] = normed.astype(BF16)
        normed_ref[:, head(h)] = normed
        scale_ref[:, head(h)] = jnp.broadcast_to(scale, (TOK, HEAD_DIM))


def attend(queries, keys, values, before):
    flat = jax.ShapeDtypeStruct((TOK, WIDTH), BF16)
    wide = jax.ShapeDtypeStruct((TOK, WIDTH), F32)
    return pl.pallas_call(
        attend_kernel,
        out_shape=(flat, wide, wide, flat),
        cost_estimate=cost(6 * TOK * WIDTH * HEAD_DIM, 1500000),
        name="attend",
    )(queries, keys, values, before)


def project_kernel(go_ref, w_ref, flat_ref, normed_ref, scale_ref, q_ref, part_ref, ga_ref, state_ref, gn_ref):
    step = pl.program_id(0)
    weight = w_ref[...]
    part_ref[0] = mm(flat_ref[...], weight, NT).astype(BF16)
    grad = mm(go_ref[0], weight, NN)

    @pl.when(step == 0)
    def _():
        gn_ref[...] = grad

    @pl.when(step > 0)
    def _():
        gn_ref[...] += grad

    @pl.when(step == pl.num_programs(0) - 1)
    def _():
        for h in range(HEADS_DEV):
            grad_normed, normed = gn_ref[:, head(h)], normed_ref[:, head(h)]
            mean = jnp.mean(grad_normed * normed, axis=-1, keepdims=True)
            ga = (scale_ref[:, head(h)] * (grad_normed - normed * mean)).astype(BF16)
            ga_ref[:, head(h)] = ga
            state_ref[head(h), :] = mm(q_ref[:, head(h)], ga, TN).astype(BF16)


def project(grad_full, weight, flat, normed, scale, queries):
    def group(j):
        return 2 * (j % 4) + j // 4

    whole = pl.BlockSpec((TOK, WIDTH), lambda j: (0, 0))
    return pl.pallas_call(
        project_kernel,
        grid=(8,),
        in_specs=[
            pl.BlockSpec((1, TOK, 512), lambda j: (j, 0, 0)),
            pl.BlockSpec((512, WIDTH), lambda j: (group(j), 0)),
            whole, whole, whole, whole,
        ],
        out_specs=(
            pl.BlockSpec((1, TOK, 512), lambda j: (group(j), 0, 0)),
            whole,
            pl.BlockSpec((WIDTH, HEAD_DIM), lambda j: (0, 0)),
        ),
        out_shape=(
            jax.ShapeDtypeStruct((8, TOK, 512), BF16),
            jax.ShapeDtypeStruct((TOK, WIDTH), BF16),
            jax.ShapeDtypeStruct((WIDTH, HEAD_DIM), BF16),
        ),
        scratch_shapes=[pltpu.VMEM((TOK, WIDTH), F32)],
        compiler_params=pltpu.CompilerParams(vmem_limit_bytes=24 * 1024 * 1024),
        cost_estimate=cost(4 * TOK * WIDTH * 4096, 8000000),
        name="project",
    )(grad_full, weight, flat, normed, scale, queries)


def grads_kernel(q_ref, k_ref, v_ref, p_ref, ga_ref, s_ref, g_ref, gq_ref, gk_ref, gv_ref):
    keep = causal()
    for h in range(HEADS_DEV):
        q, k, v, ga = q_ref[:, head(h)], k_ref[:, head(h)], v_ref[:, head(h)], ga_ref[:, head(h)]
        before, after = s_ref[head(h), :], g_ref[head(h), :]
        scores = jnp.where(keep, mm(ga, v, NT), 0.0).astype(BF16)
        gq_ref[:, head(h)] = (mm(scores, k, NN) + mm(ga, before, NT)).astype(BF16)
        gk_ref[:, head(h)] = (mm(scores, q, TN) + mm(v, after, NT)).astype(BF16)
        gv_ref[:, head(h)] = (mm(p_ref[:, head(h)], ga, TN) + mm(k, after, NN)).astype(BF16)


def grads(queries, keys, values, weights, ga, before, after):
    flat = jax.ShapeDtypeStruct((TOK, WIDTH), BF16)
    return pl.pallas_call(
        grads_kernel,
        out_shape=(flat, flat, flat),
        cost_estimate=cost(14 * TOK * WIDTH * HEAD_DIM, 1500000),
        name="grads",
    )(queries, keys, values, weights, ga, before, after)


def tied(first, second):
    return lax.optimization_barrier((first, second))


def local(queries, keys, values, out_weight, grad_out):
    mine = out_weight.T
    rows = lax.all_to_all(jnp.broadcast_to(mine, (8,) + mine.shape), Z, 0, 0)
    state = local_state(keys, values)
    rows, state = tied(rows, state)
    weight = lax.all_gather(rows.reshape(512, WIDTH), "y").reshape(4096, WIDTH)
    before = carried(state, False)
    flat, normed, scale, weights = attend(queries, keys, values, before)
    grad_out, flat = tied(grad_out, flat)
    along_x = lax.all_to_all(jnp.broadcast_to(grad_out, (4,) + grad_out.shape), "x", 0, 0)
    grad_full = lax.all_to_all(jnp.broadcast_to(along_x, (2,) + along_x.shape), "core", 0, 0)
    parts, ga, grad_state = project(
        grad_full.reshape(8, TOK, 512), weight, flat, normed, scale, queries
    )
    mixed = lax.psum_scatter(parts, ("x", "core"), scatter_dimension=0, tiled=False)
    after = carried(grad_state, True)
    grad_query, grad_key, grad_value = grads(queries, keys, values, weights, ga, before, after)
    return mixed, grad_query, grad_key, grad_value


def solution(mesh):
    finer = Mesh(mesh.devices.reshape(8, 8, 4, 2), ("y", "z", "x", "core"))
    spec = P(CTX, ("x", "core"))
    return jax.shard_map(
        local,
        mesh=finer,
        in_specs=(spec, spec, spec, P(("x", "core"), CTX), spec),
        out_specs=(spec, spec, spec, spec),
        check_vma=False,
    )
```

time: 452 us -> 156 us (0.35)
  waiting for transfers between devices: 283 us -> 15.6 us
  other arithmetic: 127 us -> 0 us
  blocking collectives: 0 us -> 92.7 us
  matrix products: 15.5 us -> 0 us
  Pallas kernels: 0 us -> 15.4 us
  starting transfers between devices: 0.2 us -> 10.5 us
    all_gather x4 -> x1, waiting for transfers between devices: 282 us -> 0.01 us  [local(): weight = lax.all_gather(rows.reshape(512, WIDTH), 'y').reshape(4096, WIDTH)]
    all_to_all x0 -> x6, blocking collectives: none -> 92.7 us  [the longest x2 40.3 us: carried(): pieces = lax.all_to_all(state.reshape(64, 8, HEAD_DIM), CTX, 0, 0)]
    select_n x64 -> x0, other arithmetic: 66.6 us -> none  [lap(): return jnp.where(reached, new, before)]
    add x63 -> x0, other arithmetic: 60.7 us -> none  [add_states(): return earlier + later]
    all_to_all x0 -> x1, waiting for transfers between devices: none -> 15.6 us  [local(): rows = lax.all_to_all(jnp.broadcast_to(mine, (8,) + mine.shape), Z, 0, 0)]
    dot_general x14 -> x0, matrix products: 15.5 us -> none  [the longest x1 4.75 us: local(): jnp.dot(flat_normed, full_weight, preferred_element_type=jnp.float32)]
    pallas_call x0 -> x6, Pallas kernels: none -> 15.4 us  [the longest x1 5 us: project(): pl.pallas_call(project_kernel, grid=(8,), in_specs=[pl.BlockSpec((1, TOK,...]
    all_to_all x0 -> x1, starting transfers between devices: none -> 10.4 us  [local(): rows = lax.all_to_all(jnp.broadcast_to(mine, (8,) + mine.shape), Z, 0, 0)]
  transfers between devices with their start and end apart: 5 -> 3, of which waited for: 3 -> 1; matrix products, arithmetic and copies ran while one was open for 31% -> 1% of each run, Pallas kernels for 0% -> 7%
where the time goes in v1:
time: 156 us; the launch traced here: 155 us
  blocking collectives  92.7 us (59%)
  waiting for transfers between devices  15.6 us (10%)
  Pallas kernels  15.4 us (10%)
  between operations  14.1 us (9%)
  starting transfers between devices  10.5 us (7%)
  local copies, waits for them, and re-layouts  6.4 us (4%)
    all_to_all x2, blocking collectives, carried(): pieces = lax.all_to_all(state.reshape(64, 8, HEAD_DIM), CTX, 0, 0)  40.3 us
    all_to_all x2, blocking collectives, carried(): back = lax.all_to_all(sums.reshape(64, 8, HEAD_DIM), CTX, 0, 0)  37.3 us
    all_to_all x1, waiting for transfers between devices, local(): rows = lax.all_to_all(jnp.broadcast_to(mine, (8,) + mine.shape), Z, 0, 0)  15.6 us
    all_to_all x1, blocking collectives, local(): lax.all_to_all(jnp.broadcast_to(grad_out, (4,) + grad_out.shape), 'x', 0, 0)  10.6 us
    all_to_all x1, starting transfers between devices, local(): rows = lax.all_to_all(jnp.broadcast_to(mine, (8,) + mine.shape), Z, 0, 0)  10.4 us
    pallas_call x1, Pallas kernels, project(): pl.pallas_call(project_kernel, grid=(8,), in_specs=[pl.BlockSpec((1, TOK,...  5 us
    all_to_all x1, blocking collectives, local(): lax.all_to_all(jnp.broadcast_to(along_x, (2,) + along_x.shape), 'core', 0...  4.58 us
    unnamed x14, local copies, waits for them, and re-layouts  3.64 us
  transfers between devices with their start and end apart: 3, of which 1 were waited for; matrix products, arithmetic and copies ran while one was open for 1% of the time, Pallas kernels for 7%

profile of v1, /device:TPU:6, one launch (start us, length us, event | category | flops | bytes accessed | tf_op | source)
XLA Modules:
  0.0 154.8 jit_solution(5748094943481268326)
XLA Ops:
  7.2 1.7 %broadcast_in_dim.9 = bf16[8,64,512]{2,1,0:T(8,128)(2,1)} broadcast(bf16[64,512]{1,0:T(8,128)(2,1)} %bitcast.25), dimensions={1,2} | broadcast | bytes 589824 | tf_op jit(solution)/shard_map/broadcast_in_dim | solution.py:197
  8.8 10.4 %all-to-all-start = ((bf16[8,64,512]{2,1,0:T(8,128)(2,1)}), bf16[8,64,512]{2,1,0:T(8,128)(2,1)S(1)}, u32[]{:S(2)}, u32[]{:S(2)}) async-start(bf16[8,64,512]{2,1,0:T(8,128)(2,1)} %broadcast_in_dim.9), calls=%async_computation | async-start | bytes 1048576 | tf_op jit(solution)/shard_map/all_to_all | solution.py:197
  19.3 0.0 all-gather.2.cloned.1.call-start
  19.3 1.8 %local_state.1 = bf16[512,128]{1,0:T(8,128)(2,1)} custom-call(bf16[128,512]{1,0:T(8,128)(2,1)} %k_ref.5, bf16[128,512]{1,0:T(8,128)(2,1)} %v_ref.5), custom_call_target="tpu_custom_call" | custom-call | flops 16777216 | bytes 400000 | tf_op jit(solution)/shard_map/local_state/pallas_call | solution.py:49
  21.2 15.6 %all-to-all-done = bf16[8,64,512]{2,1,0:T(8,128)(2,1)S(1)} async-done(((bf16[8,64,512]{2,1,0:T(8,128)(2,1)}), bf16[8,64,512]{2,1,0:T(8,128)(2,1)S(1)}, u32[]{:S(2)}, u32[]{:S(2)}) %all-to-all-start) | async-done | bytes 524320 | tf_op jit(solution)/shard_map/all_to_all | solution.py:197
  36.8 0.8 copy-done.6
  37.6 0.0 all-gather.2.cloned.1.call-update
  37.6 0.0 reduce-scatter.2.cloned.1.call-start
  37.7 21.0 %all_to_all.35 = bf16[64,8,128]{2,1,0:T(8,128)(2,1)} all-to-all(bf16[64,8,128]{2,1,0:T(8,128)(2,1)} %bitcast.19), channel_id=1, replica_groups=mesh['y'=8,'z'=8,'x'=4,'core'=2] {'y','z'}, dimensions={0} | all-to-all | bytes 262144 | tf_op jit(solution)/shard_map/all_to_all | solution.py:85
  58.7 1.6 %scan_states.2 = bf16[512,128]{1,0:T(8,128)(2,1)} custom-call(bf16[512,128]{1,0:T(8,128)(2,1)} %bitcast.21), custom_call_target="tpu_custom_call" | custom-call | flops 65536 | bytes 300000 | tf_op jit(solution)/shard_map/scan_states/pallas_call | solution.py:76
  60.3 19.2 %all_to_all.36 = bf16[64,8,128]{2,1,0:T(8,128)(2,1)} all-to-all(bf16[64,8,128]{2,1,0:T(8,128)(2,1)} %bitcast.22), channel_id=1, replica_groups=mesh['y'=8,'z'=8,'x'=4,'core'=2] {'y','z'}, dimensions={0} | all-to-all | bytes 262144 | tf_op jit(solution)/shard_map/all_to_all | solution.py:87
  79.5 2.4 %attend.1 = (bf16[128,512]{1,0:T(8,128)(2,1)}, f32[128,512]{1,0:T(8,128)}, f32[128,512]{1,0:T(8,128)}, bf16[128,512]{1,0:T(8,128)(2,1)}) custom-call(bf16[128,512]{1,0:T(8,128)(2,1)} %q_ref.5, bf16[128,512]{1,0:T(8,128)(2,1)} %k_ref.5, bf16[128,512]{1,0:T(8,128)(2,1)} %v_ref.5, bf16[512,128]{1,0:T(8,128)(2,1)} %bitcast.17), custom_call_target="tpu_custom_call" | custom-call | flops 50331648 | bytes 1500000 | tf_op jit(solution)/shard_map/attend/pallas_call | solution.py:108
  82.0 1.0 broadcast_in_dim.10
  83.0 10.6 %all_to_all.37 = bf16[4,128,512]{2,1,0:T(8,128)(2,1)S(1)} all-to-all(bf16[4,128,512]{2,1,0:T(8,128)(2,1)S(1)} %broadcast_in_dim.10), channel_id=1, replica_groups=mesh['y'=8,'z'=8,'x'=4,'core'=2] {'x'}, dimensions={0} | all-to-all | bytes 1048576 | tf_op jit(solution)/shard_map/all_to_all | solution.py:204
  93.6 0.1 broadcast_in_dim.11
  93.6 4.6 %all_to_all.38 = bf16[2,4,128,512]{3,2,1,0:T(8,128)(2,1)S(1)} all-to-all(bf16[2,4,128,512]{3,2,1,0:T(8,128)(2,1)S(1)} %broadcast_in_dim.11), channel_id=1, replica_groups=mesh['y'=8,'z'=8,'x'=4,'core'=2] {'core'}, dimensions={0} | all-to-all | bytes 2097152 | tf_op jit(solution)/shard_map/all_to_all | solution.py:205
  98.3 2.2 %copy-done = bf16[8,512,512]{2,1,0:T(8,128)(2,1)S(1)} copy-done((bf16[8,512,512]{2,1,0:T(8,128)(2,1)S(1)}, bf16[8,512,512]{2,1,0:T(8,128)(2,1)}, u32[]{:S(2)}) %copy-start) | copy-done | bytes 4194328
  100.4 5.0 %project.1 = (bf16[8,128,512]{2,1,0:T(8,128)(2,1)}, bf16[128,512]{1,0:T(8,128)(2,1)S(1)}, bf16[512,128]{1,0:T(8,128)(2,1)S(1)}) custom-call(bf16[8,128,512]{2,1,0:T(8,128)(2,1)S(1)} %bitcast.14, bf16[4096,512]{1,0:T(8,128)(2,1)S(1)} %bitcast.13, bf16[128,512]{1,0:T(8,128)(2,1)S(1)} %copy-done.5, f32[128,512]{1,0:T(8,128)S(1)} %copy-done.2, ...), custom_call_target="tpu_custom_call" | custom-call | flops 1073741824 | bytes 8000000 | tf_op jit(solution)/shard_map/project/pallas_call | solution.py:145
  105.4 0.6 copy-done.4
  106.1 0.0 reduce-scatter.2.cloned.1.call-update
  106.1 19.2 %all_to_all.39 = bf16[64,8,128]{2,1,0:T(8,128)(2,1)} all-to-all(bf16[64,8,128]{2,1,0:T(8,128)(2,1)S(1)} %bitcast.15), channel_id=1, replica_groups=mesh['y'=8,'z'=8,'x'=4,'core'=2] {'y','z'}, dimensions={0} | all-to-all | bytes 262144 | tf_op jit(solution)/shard_map/all_to_all | solution.py:85
  125.3 1.6 %scan_states.3 = bf16[512,128]{1,0:T(8,128)(2,1)} custom-call(bf16[512,128]{1,0:T(8,128)(2,1)} %bitcast.23), custom_call_target="tpu_custom_call" | custom-call | flops 65536 | bytes 300000 | tf_op jit(solution)/shard_map/scan_states/pallas_call | solution.py:76
  126.9 18.1 %all_to_all.40 = bf16[64,8,128]{2,1,0:T(8,128)(2,1)} all-to-all(bf16[64,8,128]{2,1,0:T(8,128)(2,1)} %bitcast.24), channel_id=1, replica_groups=mesh['y'=8,'z'=8,'x'=4,'core'=2] {'y','z'}, dimensions={0} | all-to-all | bytes 262144 | tf_op jit(solution)/shard_map/all_to_all | solution.py:87
  145.0 2.9 %grads.1 = (bf16[128,512]{1,0:T(8,128)(2,1)}, bf16[128,512]{1,0:T(8,128)(2,1)}, bf16[128,512]{1,0:T(8,128)(2,1)}) custom-call(bf16[128,512]{1,0:T(8,128)(2,1)} %q_ref.5, bf16[128,512]{1,0:T(8,128)(2,1)} %k_ref.5, bf16[128,512]{1,0:T(8,128)(2,1)} %v_ref.5, bf16[128,512]{1,0:T(8,128)(2,1)} %get-tuple-element.26.p_ref, bf16[128,512]{1,0:T(8,128)(2,1)} %copy-done.4, ...), custom_call_target="tpu_custom_call" | custom-call | flops 117440512 | bytes 1500000 | tf_op jit(solution)/shard_map/grads/pallas_call | solution.py:183
  (13 shorter events, 0.0 us)
Async XLA Ops:
  8.8 89.4 %copy-start.1 = (bf16[128,512]{1,0:T(8,128)(2,1)S(1)}, bf16[128,512]{1,0:T(8,128)(2,1)}, u32[]{:S(2)}) copy-start(bf16[128,512]{1,0:T(8,128)(2,1)} %q_ref.5) | copy-start | bytes 393220
  8.8 27.9 %all-to-all-start = ((bf16[8,64,512]{2,1,0:T(8,128)(2,1)}), bf16[8,64,512]{2,1,0:T(8,128)(2,1)S(1)}, u32[]{:S(2)}, u32[]{:S(2)}) async-start(bf16[8,64,512]{2,1,0:T(8,128)(2,1)} %broadcast_in_dim.9), calls=%async_computation | async-start | bytes 1048576 | tf_op jit(solution)/shard_map/all_to_all | solution.py:197
  19.3 78.9 %all-gather.2.cloned.1.call-start = ((), (), s32[]{:S(2)}) async-start(), calls=%async_computation.8 | async-start | bytes 4718592 | tf_op jit(solution)/shard_map/all_gather | solution.py:200
  36.8 0.8 copy-start.6
  37.6 110.3 %reduce-scatter.2.cloned.1.call-start = ((), (), s32[]{:S(2)}) async-start(), calls=%async_computation.9 | async-start | bytes 1179648 | tf_op jit(solution)/shard_map/reduce_scatter | solution.py:209
  82.0 16.3 %copy-start.2 = (f32[128,512]{1,0:T(8,128)S(1)}, f32[128,512]{1,0:T(8,128)}, u32[]{:S(2)}) copy-start(f32[128,512]{1,0:T(8,128)} %get-tuple-element.23.normed_ref) | copy-start | bytes 786436
  82.0 16.3 %copy-start.3 = (f32[128,512]{1,0:T(8,128)S(1)}, f32[128,512]{1,0:T(8,128)}, u32[]{:S(2)}) copy-start(f32[128,512]{1,0:T(8,128)} %get-tuple-element.24.scale_ref) | copy-start | bytes 786436
  82.0 16.3 %copy-start.5 = (bf16[128,512]{1,0:T(8,128)(2,1)S(1)}, bf16[128,512]{1,0:T(8,128)(2,1)}, u32[]{:S(2)}) copy-start(bf16[128,512]{1,0:T(8,128)(2,1)} %get-tuple-element.22.flat_ref) | copy-start | bytes 393220
  98.2 2.2 %copy-start = (bf16[8,512,512]{2,1,0:T(8,128)(2,1)S(1)}, bf16[8,512,512]{2,1,0:T(8,128)(2,1)}, u32[]{:S(2)}) copy-start(bf16[8,512,512]{2,1,0:T(8,128)(2,1)} %all-gather.2.cloned.1.call-done) | copy-start | bytes 12582916
  105.4 0.6 copy-start.4
Sparse Core Ops, SparseCore 0:
  37.7 57.2 all-gather.1
  106.2 28.9 reduce-scatter.1

commit v2 on v1

--- a/solution.py
+++ b/solution.py
@@ -14,8 +14,7 @@
 EPSILON = 1e-06
 F32 = jnp.float32
 BF16 = jnp.bfloat16
-Z = ("z",)
-CTX = ("y", "z")
+CTX = ("yh", "yl", "z")
 
 NN = (((1,), (0,)), ((), ()))
 NT = (((1,), (1,)), ((), ()))
@@ -36,6 +35,10 @@
     return rows >= cols
 
 
+def small():
+    return pltpu.CompilerParams(vmem_limit_bytes=16 * 1024 * 1024)
+
+
 def cost(flops, nbytes):
     return pl.CostEstimate(flops=flops, bytes_accessed=nbytes, transcendentals=0)
 
@@ -50,6 +53,7 @@
         state_kernel,
         out_shape=jax.ShapeDtypeStruct((WIDTH, HEAD_DIM), BF16),
         cost_estimate=cost(2 * TOK * WIDTH * HEAD_DIM, 400000),
+        compiler_params=small(),
         name="local_state",
     )(keys, values)
 
@@ -77,6 +81,7 @@
         functools.partial(scan_kernel, reverse),
         out_shape=jax.ShapeDtypeStruct(pieces.shape, pieces.dtype),
         cost_estimate=cost(WIDTH * HEAD_DIM, 300000),
+        compiler_params=small(),
         name="scan_states",
     )(pieces)
 
@@ -109,62 +114,84 @@
         attend_kernel,
         out_shape=(flat, wide, wide, flat),
         cost_estimate=cost(6 * TOK * WIDTH * HEAD_DIM, 1500000),
+        compiler_params=small(),
         name="attend",
     )(queries, keys, values, before)
 
 
-def project_kernel(go_ref, w_ref, flat_ref, normed_ref, scale_ref, q_ref, part_ref, ga_ref, state_ref, gn_ref):
-    step = pl.program_id(0)
-    weight = w_ref[...]
-    part_ref[0] = mm(flat_ref[...], weight, NT).astype(BF16)
-    grad = mm(go_ref[0], weight, NN)
-
-    @pl.when(step == 0)
-    def _():
-        gn_ref[...] = grad
-
-    @pl.when(step > 0)
-    def _():
-        gn_ref[...] += grad
-
-    @pl.when(step == pl.num_programs(0) - 1)
-    def _():
-        for h in range(HEADS_DEV):
-            grad_normed, normed = gn_ref[:, head(h)], normed_ref[:, head(h)]
-            mean = jnp.mean(grad_normed * normed, axis=-1, keepdims=True)
-            ga = (scale_ref[:, head(h)] * (grad_normed - normed * mean)).astype(BF16)
-            ga_ref[:, head(h)] = ga
-            state_ref[head(h), :] = mm(q_ref[:, head(h)], ga, TN).astype(BF16)
-
-
-def project(grad_full, weight, flat, normed, scale, queries):
-    def group(j):
-        return 2 * (j % 4) + j // 4
-
-    whole = pl.BlockSpec((TOK, WIDTH), lambda j: (0, 0))
+def project_kernel(place_ref, w_ref, go0_ref, go1_ref, go2_ref, go3_ref, mine_ref, other_ref, part_ref, own_ref, send_ref, w_buf, a_buf, out_buf, w_sem, out_sem):
+    yl, x = place_ref[0], place_ref[1]
+    own = pl.ds(pl.multiple_of(yl * TOK, TOK), TOK)
+    other = pl.ds(pl.multiple_of((1 - yl) * TOK, TOK), TOK)
+    groups = [lax.rem(x + r, 4) for r in range(4)]
+    loads = [pltpu.make_async_copy(w_ref.at[:, groups[r]], w_buf.at[r], w_sem.at[r]) for r in range(4)]
+    stores = [pltpu.make_async_copy(out_buf.at[r], part_ref.at[groups[r]], out_sem.at[r]) for r in range(4)]
+    for load in loads:
+        load.start()
+    a_buf[own, :] = mine_ref[...]
+    a_buf[other, :] = other_ref[...]
+    normed = a_buf[...]
+    grad = jnp.zeros((2 * TOK, WIDTH), F32)
+    for r, go_ref in enumerate((go0_ref, go1_ref, go2_ref, go3_ref)):
+        loads[r].wait()
+        weight = w_buf[r].reshape(512, WIDTH)
+        grad = grad + mm(go_ref[...].reshape(2 * TOK, 512), weight, NN)
+        out_buf[r] = mm(normed, weight, NT).astype(BF16).reshape(2, TOK, 512)
+        stores[r].start()
+    first, second = grad[:TOK], grad[TOK:]
+    own_ref[...] = jnp.where(yl == 0, first, second)
+    send_ref[...] = jnp.where(yl == 0, second, first).astype(BF16)
+    for store in stores:
+        store.wait()
+
+
+def project(weight, grad_parts, mine, other):
+    vmem = pl.BlockSpec(memory_space=pltpu.VMEM)
+    hbm = pl.BlockSpec(memory_space=pltpu.HBM)
+    place = jnp.stack([lax.axis_index("yl"), lax.axis_index("x")]).astype(jnp.int32)
     return pl.pallas_call(
         project_kernel,
-        grid=(8,),
-        in_specs=[
-            pl.BlockSpec((1, TOK, 512), lambda j: (j, 0, 0)),
-            pl.BlockSpec((512, WIDTH), lambda j: (group(j), 0)),
-            whole, whole, whole, whole,
+        in_specs=[pl.BlockSpec(memory_space=pltpu.SMEM), hbm] + [vmem] * 6,
+        out_specs=(hbm, vmem, vmem),
+        out_shape=(
+            jax.ShapeDtypeStruct((4, 2, TOK, 512), BF16),
+            jax.ShapeDtypeStruct((TOK, WIDTH), F32),
+            jax.ShapeDtypeStruct((TOK, WIDTH), BF16),
+        ),
+        scratch_shapes=[
+            pltpu.VMEM((4, 8, 64, WIDTH), BF16),
+            pltpu.VMEM((2 * TOK, WIDTH), BF16),
+            pltpu.VMEM((4, 2, TOK, 512), BF16),
+            pltpu.SemaphoreType.DMA((4,)),
+            pltpu.SemaphoreType.DMA((4,)),
         ],
-        out_specs=(
-            pl.BlockSpec((1, TOK, 512), lambda j: (group(j), 0, 0)),
-            whole,
-            pl.BlockSpec((WIDTH, HEAD_DIM), lambda j: (0, 0)),
-        ),
+        compiler_params=small(),
+        cost_estimate=cost(4 * TOK * WIDTH * 4096, 6000000),
+        name="project",
+    )(place, weight, *grad_parts, mine, other)
+
+
+def grad_attended_kernel(own_ref, got_ref, normed_ref, scale_ref, q_ref, ga_ref, state_ref):
+    for h in range(HEADS_DEV):
+        grad_normed = own_ref[:, head(h)] + got_ref[:, head(h)].astype(F32)
+        normed = normed_ref[:, head(h)]
+        mean = jnp.mean(grad_normed * normed, axis=-1, keepdims=True)
+        ga = (scale_ref[:, head(h)] * (grad_normed - normed * mean)).astype(BF16)
+        ga_ref[:, head(h)] = ga
+        state_ref[head(h), :] = mm(q_ref[:, head(h)], ga, TN).astype(BF16)
+
+
+def grad_attended(own, got, normed, scale, queries):
+    return pl.pallas_call(
+        grad_attended_kernel,
         out_shape=(
-            jax.ShapeDtypeStruct((8, TOK, 512), BF16),
             jax.ShapeDtypeStruct((TOK, WIDTH), BF16),
             jax.ShapeDtypeStruct((WIDTH, HEAD_DIM), BF16),
         ),
-        scratch_shapes=[pltpu.VMEM((TOK, WIDTH), F32)],
-        compiler_params=pltpu.CompilerParams(vmem_limit_bytes=24 * 1024 * 1024),
-        cost_estimate=cost(4 * TOK * WIDTH * 4096, 8000000),
-        name="project",
-    )(grad_full, weight, flat, normed, scale, queries)
+        compiler_params=small(),
+        cost_estimate=cost(2 * TOK * WIDTH * HEAD_DIM, 1200000),
+        name="grad_attended",
+    )(own, got, normed, scale, queries)
 
 
 def grads_kernel(q_ref, k_ref, v_ref, p_ref, ga_ref, s_ref, g_ref, gq_ref, gk_ref, gv_ref):
@@ -184,6 +211,7 @@
         grads_kernel,
         out_shape=(flat, flat, flat),
         cost_estimate=cost(14 * TOK * WIDTH * HEAD_DIM, 1500000),
+        compiler_params=small(),
         name="grads",
     )(queries, keys, values, weights, ga, before, after)
 
@@ -192,28 +220,47 @@
     return lax.optimization_barrier((first, second))
 
 
+SWAP = [(0, 1), (1, 0)]
+TRANSPOSE = [(0, 0), (1, 2), (2, 1), (3, 3)]
+
+
+def repeated(value, times):
+    return jnp.broadcast_to(value, (times,) + value.shape)
+
+
+def shifted(value, step):
+    return lax.ppermute(value, "x", [((i + step) % 4, i) for i in range(4)])
+
+
 def local(queries, keys, values, out_weight, grad_out):
-    mine = out_weight.T
-    rows = lax.all_to_all(jnp.broadcast_to(mine, (8,) + mine.shape), Z, 0, 0)
+    grad_turned = lax.ppermute(grad_out, ("yl", "core"), TRANSPOSE)
+    rows = lax.all_to_all(repeated(out_weight.T, 4), "yh", 0, 0)
     state = local_state(keys, values)
     rows, state = tied(rows, state)
-    weight = lax.all_gather(rows.reshape(512, WIDTH), "y").reshape(4096, WIDTH)
+    weight = lax.all_gather(rows, "z")
+    grad_other = lax.ppermute(grad_turned, "core", SWAP)
+    core = lax.axis_index("core")
+    grad_own = jnp.stack(
+        [jnp.where(core == 0, grad_turned, grad_other), jnp.where(core == 0, grad_other, grad_turned)]
+    )
     before = carried(state, False)
     flat, normed, scale, weights = attend(queries, keys, values, before)
-    grad_out, flat = tied(grad_out, flat)
-    along_x = lax.all_to_all(jnp.broadcast_to(grad_out, (4,) + grad_out.shape), "x", 0, 0)
-    grad_full = lax.all_to_all(jnp.broadcast_to(along_x, (2,) + along_x.shape), "core", 0, 0)
-    parts, ga, grad_state = project(
-        grad_full.reshape(8, TOK, 512), weight, flat, normed, scale, queries
+    flat_other = lax.ppermute(flat, "yl", SWAP)
+    grad_parts = [grad_own] + [shifted(grad_own, r) for r in (1, 2, 3)]
+    parts, own, send = project(weight, grad_parts, flat, flat_other)
+    got = lax.ppermute(send, "yl", SWAP)
+    mixed_turned = lax.psum_scatter(
+        parts.reshape(8, TOK, 512), ("x", "core"), scatter_dimension=0, tiled=False
     )
-    mixed = lax.psum_scatter(parts, ("x", "core"), scatter_dimension=0, tiled=False)
+    ga, grad_state = grad_attended(own, got, normed, scale, queries)
     after = carried(grad_state, True)
     grad_query, grad_key, grad_value = grads(queries, keys, values, weights, ga, before, after)
+    mixed = lax.ppermute(mixed_turned, ("yl", "core"), TRANSPOSE)
     return mixed, grad_query, grad_key, grad_value
 
 
 def solution(mesh):
-    finer = Mesh(mesh.devices.reshape(8, 8, 4, 2), ("y", "z", "x", "core"))
+    finer = Mesh(mesh.devices.reshape(4, 2, 8, 4, 2), ("yh", "yl", "z", "x", "core"))
     spec = P(CTX, ("x", "core"))
     return jax.shard_map(
         local,

time: 156 us -> 145 us (0.929)
  blocking collectives: 92.7 us -> 22.8 us
  starting transfers between devices: 10.5 us -> 49.2 us
  waiting for transfers between devices: 15.6 us -> 42.5 us
  Pallas kernels: 15.4 us -> 8.1 us
    all_to_all x4 -> x0, blocking collectives: 52.4 us -> none  [the longest x2 37.3 us: carried(): back = lax.all_to_all(sums.reshape(64, 8, HEAD_DIM), CTX, 0, 0)]
    all_to_all x1 -> x4, starting transfers between devices: 10.4 us -> 30.3 us  [the longest x1 14 us: carried(): pieces = lax.all_to_all(state.reshape(64, 8, HEAD_DIM), CTX, 0, 0)]
    ppermute x0 -> x8, starting transfers between devices: none -> 18.8 us  [the longest x3 8.64 us: shifted(): return lax.ppermute(value, 'x', [((i + step) % 4, i) for i in range(4)])]
    all_to_all x1 -> x4, waiting for transfers between devices: 15.6 us -> 33.9 us  [the longest x2 15.3 us: carried(): back = lax.all_to_all(sums.reshape(64, 8, HEAD_DIM), CTX, 0, 0)]
    all_to_all x2 -> x1, blocking collectives: 40.3 us -> 22.8 us  [carried(): pieces = lax.all_to_all(state.reshape(64, 8, HEAD_DIM), CTX, 0, 0)]
    ppermute x0 -> x8, waiting for transfers between devices: none -> 8.52 us  [the longest x1 4.29 us: local(): got = lax.ppermute(send, 'yl', SWAP)]
    pallas_call x1, Pallas kernels: 2.44 us -> 0.5 us  [attend(): pl.pallas_call(attend_kernel, out_shape=(flat, wide, wide, flat), cost_es...]
    pallas_call x2, Pallas kernels: 3.26 us -> 1.45 us  [exclusive_scan(): pl.pallas_call(functools.partial(scan_kernel, reverse), out_shape=jax.Sha...]
  transfers between devices with their start and end apart: 3 -> 14, of which waited for: 1 -> 7; matrix products, arithmetic and copies ran while one was open for 1% -> 0% of each run, Pallas kernels for 7% -> 3%
where the time goes in v2:
time: 145 us; the launch traced here: 143 us
  starting transfers between devices  49.2 us (34%)
  waiting for transfers between devices  42.5 us (29%)
  blocking collectives  22.8 us (16%)
  between operations  14.2 us (10%)
  Pallas kernels  8.1 us (6%)
  local copies, waits for them, and re-layouts  6.38 us (4%)
    all_to_all x1, blocking collectives, carried(): pieces = lax.all_to_all(state.reshape(64, 8, HEAD_DIM), CTX, 0, 0)  22.8 us
    all_to_all x2, waiting for transfers between devices, carried(): back = lax.all_to_all(sums.reshape(64, 8, HEAD_DIM), CTX, 0, 0)  15.3 us
    all_to_all x1, starting transfers between devices, carried(): pieces = lax.all_to_all(state.reshape(64, 8, HEAD_DIM), CTX, 0, 0)  14 us
    all_to_all x1, waiting for transfers between devices, carried(): pieces = lax.all_to_all(state.reshape(64, 8, HEAD_DIM), CTX, 0, 0)  10.9 us
    all_to_all x2, starting transfers between devices, carried(): back = lax.all_to_all(sums.reshape(64, 8, HEAD_DIM), CTX, 0, 0)  9.24 us
    ppermute x3, starting transfers between devices, shifted(): return lax.ppermute(value, 'x', [((i + step) % 4, i) for i in range(4)])  8.64 us
    all_to_all x1, waiting for transfers between devices, local(): rows = lax.all_to_all(repeated(out_weight.T, 4), 'yh', 0, 0)  7.75 us
    all_to_all x1, starting transfers between devices, local(): rows = lax.all_to_all(repeated(out_weight.T, 4), 'yh', 0, 0)  7.09 us
  transfers between devices with their start and end apart: 14, of which 7 were waited for; matrix products, arithmetic and copies ran while one was open for 0% of the time, Pallas kernels for 3%

profile of v2, /device:TPU:6, one launch (start us, length us, event | category | flops | bytes accessed | tf_op | source)
XLA Modules:
  0.0 143.3 jit_solution(3022994084521947659)
XLA Ops:
  7.2 1.6 %broadcast_in_dim.3 = bf16[4,64,512]{2,1,0:T(8,128)(2,1)} broadcast(bf16[64,512]{1,0:T(8,128)(2,1)} %bitcast.25), dimensions={1,2} | broadcast | bytes 327680 | tf_op jit(solution)/shard_map/broadcast_in_dim | solution.py:228
  8.8 7.1 %all-to-all-start = ((bf16[4,64,512]{2,1,0:T(8,128)(2,1)}), bf16[4,64,512]{2,1,0:T(8,128)(2,1)S(1)}, u32[]{:S(2)}, u32[]{:S(2)}) async-start(bf16[4,64,512]{2,1,0:T(8,128)(2,1)} %broadcast_in_dim.3), calls=%async_computation | async-start | bytes 524288 | tf_op jit(solution)/shard_map/all_to_all | solution.py:237
  18.6 7.7 %all-to-all-done = bf16[4,64,512]{2,1,0:T(8,128)(2,1)S(1)} async-done(((bf16[4,64,512]{2,1,0:T(8,128)(2,1)}), bf16[4,64,512]{2,1,0:T(8,128)(2,1)S(1)}, u32[]{:S(2)}, u32[]{:S(2)}) %all-to-all-start) | async-done | bytes 262176 | tf_op jit(solution)/shard_map/all_to_all | solution.py:237
  27.1 1.6 %collective-permute-start = (bf16[128,512]{1,0:T(8,128)(2,1)}, bf16[128,512]{1,0:T(8,128)(2,1)S(1)}, u32[]{:S(2)}, u32[]{:S(2)}) collective-permute-start(bf16[128,512]{1,0:T(8,128)(2,1)} %param.9), channel_id=1, source_target_pairs={{0,0},{1,64},{64,1},{65,65},{2,2},{3,66},{66,3},{67,67},{4,4},{5,6... | collective-permute-start | bytes 393224 | tf_op jit(solution)/shard_map/ppermute | solution.py:236
  28.6 14.0 %all-to-all-start.1 = ((bf16[64,8,128]{2,1,0:T(8,128)(2,1)}), bf16[64,8,128]{2,1,0:T(8,128)(2,1)S(1)}, u32[]{:S(2)}, u32[]{:S(2)}) async-start(bf16[64,8,128]{2,1,0:T(8,128)(2,1)} %bitcast.6), calls=%async_computation.1 | async-start | bytes 262144 | tf_op jit(solution)/shard_map/all_to_all | solution.py:90
  42.6 1.9 %collective-permute-start.1 = (bf16[128,512]{1,0:T(8,128)(2,1)S(1)}, bf16[128,512]{1,0:T(8,128)(2,1)S(1)}, u32[]{:S(2)}, u32[]{:S(2)}) collective-permute-start(bf16[128,512]{1,0:T(8,128)(2,1)S(1)} %collective-permute-done), channel_id=1, source_target_pairs={{0,1},{1,0},{2,3},{3,2},{4,5},{5,4},{6,7},{7,6},{8,9},{9,8},{10,11... | collective-permute-start | bytes 393224 | tf_op jit(solution)/shard_map/ppermute | solution.py:241
  44.6 10.9 %all-to-all-done.1 = bf16[64,8,128]{2,1,0:T(8,128)(2,1)S(1)} async-done(((bf16[64,8,128]{2,1,0:T(8,128)(2,1)}), bf16[64,8,128]{2,1,0:T(8,128)(2,1)S(1)}, u32[]{:S(2)}, u32[]{:S(2)}) %all-to-all-start.1) | async-done | bytes 131104 | tf_op jit(solution)/shard_map/all_to_all | solution.py:90
  56.2 4.6 %all-to-all-start.2 = ((bf16[64,8,128]{2,1,0:T(8,128)(2,1)}), bf16[64,8,128]{2,1,0:T(8,128)(2,1)S(1)}, u32[]{:S(2)}, u32[]{:S(2)}) async-start(bf16[64,8,128]{2,1,0:T(8,128)(2,1)} %bitcast.8), calls=%async_computation.2 | async-start | bytes 262144 | tf_op jit(solution)/shard_map/all_to_all | solution.py:92
  61.0 2.4 %collective-permute-start.4 = (bf16[2,128,512]{2,1,0:T(8,128)(2,1)S(1)}, bf16[2,128,512]{2,1,0:T(8,128)(2,1)S(1)}, u32[]{:S(2)}, u32[]{:S(2)}) collective-permute-start(bf16[2,128,512]{2,1,0:T(8,128)(2,1)S(1)} %pad_maximum_fusion.go0_ref), channel_id=1, source_target_pairs={{6,0},{0,2},{2,4},{4,6},{7,1},{1,3},{3,5},{5,7},{14,8},{8,10},{10,... | collective-permute-start | bytes 786440 | tf_op jit(solution)/shard_map/ppermute | solution.py:232
  63.4 4.3 %collective-permute-start.3 = (bf16[2,128,512]{2,1,0:T(8,128)(2,1)S(1)}, bf16[2,128,512]{2,1,0:T(8,128)(2,1)S(1)}, u32[]{:S(2)}, u32[]{:S(2)}) collective-permute-start(bf16[2,128,512]{2,1,0:T(8,128)(2,1)S(1)} %pad_maximum_fusion.go0_ref), channel_id=1, source_target_pairs={{4,0},{6,2},{0,4},{2,6},{5,1},{7,3},{1,5},{3,7},{12,8},{14,10},{8,... | collective-permute-start | bytes 786440 | tf_op jit(solution)/shard_map/ppermute | solution.py:232
  67.7 1.9 %collective-permute-start.2 = (bf16[2,128,512]{2,1,0:T(8,128)(2,1)S(1)}, bf16[2,128,512]{2,1,0:T(8,128)(2,1)S(1)}, u32[]{:S(2)}, u32[]{:S(2)}) collective-permute-start(bf16[2,128,512]{2,1,0:T(8,128)(2,1)S(1)} %pad_maximum_fusion.go0_ref), channel_id=1, source_target_pairs={{2,0},{4,2},{6,4},{0,6},{3,1},{5,3},{7,5},{1,7},{10,8},{12,10},{14... | collective-permute-start | bytes 786440 | tf_op jit(solution)/shard_map/ppermute | solution.py:232
  69.6 4.1 %all-to-all-done.2 = bf16[64,8,128]{2,1,0:T(8,128)(2,1)S(1)} async-done(((bf16[64,8,128]{2,1,0:T(8,128)(2,1)}), bf16[64,8,128]{2,1,0:T(8,128)(2,1)S(1)}, u32[]{:S(2)}, u32[]{:S(2)}) %all-to-all-start.2) | async-done | bytes 131104 | tf_op jit(solution)/shard_map/all_to_all | solution.py:92
  74.2 2.6 %collective-permute-start.5 = (bf16[128,512]{1,0:T(8,128)(2,1)S(1)}, bf16[128,512]{1,0:T(8,128)(2,1)S(1)}, u32[]{:S(2)}, u32[]{:S(2)}) collective-permute-start(bf16[128,512]{1,0:T(8,128)(2,1)S(1)} %get-tuple-element.20.mine_ref), channel_id=1, source_target_pairs={{0,64},{64,0},{1,65},{65,1},{2,66},{66,2},{3,67},{67,3},{4,68},{68... | collective-permute-start | bytes 393224 | tf_op jit(solution)/shard_map/ppermute | solution.py:248
  76.9 2.2 %collective-permute-done.2.go1_ref = bf16[2,128,512]{2,1,0:T(8,128)(2,1)S(1)} collective-permute-done((bf16[2,128,512]{2,1,0:T(8,128)(2,1)S(1)}, bf16[2,128,512]{2,1,0:T(8,128)(2,1)S(1)}, u32[]{:S(2)}, u32[]{:S(2)}) %collective-permute-start.2) | collective-permute-done | bytes 262176 | tf_op jit(solution)/shard_map/ppermute | solution.py:232
  79.1 2.0 %collective-permute-done.5.other_ref = bf16[128,512]{1,0:T(8,128)(2,1)S(1)} collective-permute-done((bf16[128,512]{1,0:T(8,128)(2,1)S(1)}, bf16[128,512]{1,0:T(8,128)(2,1)S(1)}, u32[]{:S(2)}, u32[]{:S(2)}) %collective-permute-start.5) | collective-permute-done | bytes 131104 | tf_op jit(solution)/shard_map/ppermute | solution.py:248
  81.1 1.6 %copy-done.5 = bf16[32,64,512]{2,1,0:T(8,128)(2,1)S(1)} copy-done((bf16[32,64,512]{2,1,0:T(8,128)(2,1)S(1)}, bf16[32,64,512]{2,1,0:T(8,128)(2,1)}, u32[]{:S(2)}) %copy-start.5) | copy-done | bytes 2097176
  82.7 3.3 %project.1 = (bf16[4,2,128,512]{3,2,1,0:T(8,128)(2,1)}, f32[128,512]{1,0:T(8,128)S(1)}, bf16[128,512]{1,0:T(8,128)(2,1)S(1)}) custom-call(s32[2]{0:T(128)S(1)} %pad_add_fusion.place_ref, bf16[8,4,64,512]{3,2,1,0:T(8,128)(2,1)S(1)} %bitcast.24, bf16[2,128,512]{2,1,0:T(8,128)(2,1)S(1)} %pad_maximum_fusion.go0_ref, ...), custom_call_target="tpu_custom_call" | custom-call | flops 1073741824 | bytes 6000000 | tf_op jit(solution)/shard_map/project/pallas_call | solution.py:152
  86.0 2.6 %collective-permute-start.7 = (bf16[128,512]{1,0:T(8,128)(2,1)S(1)}, bf16[128,512]{1,0:T(8,128)(2,1)S(1)}, u32[]{:S(2)}, u32[]{:S(2)}) collective-permute-start(bf16[128,512]{1,0:T(8,128)(2,1)S(1)} %get-tuple-element.24), channel_id=1, source_target_pairs={{0,64},{64,0},{1,65},{65,1},{2,66},{66,2},{3,67},{67,3},{4,68},{68... | collective-permute-start | bytes 393224 | tf_op jit(solution)/shard_map/ppermute | solution.py:251
  88.6 4.3 %collective-permute-done.7.got_ref = bf16[128,512]{1,0:T(8,128)(2,1)S(1)} collective-permute-done((bf16[128,512]{1,0:T(8,128)(2,1)S(1)}, bf16[128,512]{1,0:T(8,128)(2,1)S(1)}, u32[]{:S(2)}, u32[]{:S(2)}) %collective-permute-start.7) | collective-permute-done | bytes 131104 | tf_op jit(solution)/shard_map/ppermute | solution.py:251
  93.2 22.8 %all_to_all.25 = bf16[64,8,128]{2,1,0:T(8,128)(2,1)S(1)} all-to-all(bf16[64,8,128]{2,1,0:T(8,128)(2,1)S(1)} %bitcast.23), channel_id=1, replica_groups=mesh['yh'=4,'yl'=2,'z'=8,'x'=4,'core'=2] {'yh','yl','z'}, dimensions={0} | all-to-all | bytes 262144 | tf_op jit(solution)/shard_map/all_to_all | solution.py:90
  116.8 4.6 %all-to-all-start.4 = ((bf16[64,8,128]{2,1,0:T(8,128)(2,1)}), bf16[64,8,128]{2,1,0:T(8,128)(2,1)S(1)}, u32[]{:S(2)}, u32[]{:S(2)}) async-start(bf16[64,8,128]{2,1,0:T(8,128)(2,1)} %bitcast.14), calls=%async_computation.5 | async-start | bytes 262144 | tf_op jit(solution)/shard_map/all_to_all | solution.py:92
  121.4 1.6 %collective-permute-start.6 = (bf16[128,512]{1,0:T(8,128)(2,1)}, bf16[128,512]{1,0:T(8,128)(2,1)S(1)}, u32[]{:S(2)}, u32[]{:S(2)}) collective-permute-start(bf16[128,512]{1,0:T(8,128)(2,1)} %bitcast.26), channel_id=1, source_target_pairs={{0,0},{1,64},{64,1},{65,65},{2,2},{3,66},{66,3},{67,67},{4,4},{5,6... | collective-permute-start | bytes 393224 | tf_op jit(solution)/shard_map/ppermute | solution.py:258
  123.0 11.2 %all-to-all-done.4 = bf16[64,8,128]{2,1,0:T(8,128)(2,1)S(1)} async-done(((bf16[64,8,128]{2,1,0:T(8,128)(2,1)}), bf16[64,8,128]{2,1,0:T(8,128)(2,1)S(1)}, u32[]{:S(2)}, u32[]{:S(2)}) %all-to-all-start.4) | async-done | bytes 131104 | tf_op jit(solution)/shard_map/all_to_all | solution.py:92
  134.1 1.7 %grads.1 = (bf16[128,512]{1,0:T(8,128)(2,1)}, bf16[128,512]{1,0:T(8,128)(2,1)}, bf16[128,512]{1,0:T(8,128)(2,1)}) custom-call(bf16[128,512]{1,0:T(8,128)(2,1)S(1)} %copy-done.4, bf16[128,512]{1,0:T(8,128)(2,1)S(1)} %copy-done.1, bf16[128,512]{1,0:T(8,128)(2,1)S(1)} %copy-done.3, bf16[128,512]{1,0:T(8,128)(2,1)S(1)} %get-tuple-element.22.p_ref, ...), custom_call_target="tpu_custom_call" | custom-call | flops 117440512 | bytes 1500000 | tf_op jit(solution)/shard_map/grads/pallas_call | solution.py:210
  (33 shorter events, 6.5 us)
Async XLA Ops:
  7.2 66.6 %copy-start.3 = (bf16[128,512]{1,0:T(8,128)(2,1)S(1)}, bf16[128,512]{1,0:T(8,128)(2,1)}, u32[]{:S(2)}) copy-start(bf16[128,512]{1,0:T(8,128)(2,1)} %v_ref.5) | copy-start | bytes 393220
  7.2 66.6 %copy-start.1 = (bf16[128,512]{1,0:T(8,128)(2,1)S(1)}, bf16[128,512]{1,0:T(8,128)(2,1)}, u32[]{:S(2)}) copy-start(bf16[128,512]{1,0:T(8,128)(2,1)} %k_ref.5) | copy-start | bytes 393220
  7.2 66.5 %copy-start.4 = (bf16[128,512]{1,0:T(8,128)(2,1)S(1)}, bf16[128,512]{1,0:T(8,128)(2,1)}, u32[]{:S(2)}) copy-start(bf16[128,512]{1,0:T(8,128)(2,1)} %q_ref.5) | copy-start | bytes 393220
  8.8 17.5 %all-to-all-start = ((bf16[4,64,512]{2,1,0:T(8,128)(2,1)}), bf16[4,64,512]{2,1,0:T(8,128)(2,1)S(1)}, u32[]{:S(2)}, u32[]{:S(2)}) async-start(bf16[4,64,512]{2,1,0:T(8,128)(2,1)} %broadcast_in_dim.3), calls=%async_computation | async-start | bytes 524288 | tf_op jit(solution)/shard_map/all_to_all | solution.py:237
  15.9 65.2 %all-gather.3.cloned.1.call-start = ((), (), s32[]{:S(2)}) async-start(), calls=%async_computation.7 | async-start | bytes 2359296 | tf_op jit(solution)/shard_map/all_gather | solution.py:240
  15.9 0.9 copy-start
  16.8 0.9 copy-start.2
  26.3 0.7 copy-start.6
  27.1 15.6 %collective-permute-start = (bf16[128,512]{1,0:T(8,128)(2,1)}, bf16[128,512]{1,0:T(8,128)(2,1)S(1)}, u32[]{:S(2)}, u32[]{:S(2)}) collective-permute-start(bf16[128,512]{1,0:T(8,128)(2,1)} %param.9), channel_id=1, source_target_pairs={{0,0},{1,64},{64,1},{65,65},{2,2},{3,66},{66,3},{67,67},{4,4},{5,6... | collective-permute-start | bytes 393224 | tf_op jit(solution)/shard_map/ppermute | solution.py:236
  28.6 26.9 %all-to-all-start.1 = ((bf16[64,8,128]{2,1,0:T(8,128)(2,1)}), bf16[64,8,128]{2,1,0:T(8,128)(2,1)S(1)}, u32[]{:S(2)}, u32[]{:S(2)}) async-start(bf16[64,8,128]{2,1,0:T(8,128)(2,1)} %bitcast.6), calls=%async_computation.1 | async-start | bytes 262144 | tf_op jit(solution)/shard_map/all_to_all | solution.py:90
  42.6 18.3 %collective-permute-start.1 = (bf16[128,512]{1,0:T(8,128)(2,1)S(1)}, bf16[128,512]{1,0:T(8,128)(2,1)S(1)}, u32[]{:S(2)}, u32[]{:S(2)}) collective-permute-start(bf16[128,512]{1,0:T(8,128)(2,1)S(1)} %collective-permute-done), channel_id=1, source_target_pairs={{0,1},{1,0},{2,3},{3,2},{4,5},{5,4},{6,7},{7,6},{8,9},{9,8},{10,11... | collective-permute-start | bytes 393224 | tf_op jit(solution)/shard_map/ppermute | solution.py:241
  56.2 17.5 %all-to-all-start.2 = ((bf16[64,8,128]{2,1,0:T(8,128)(2,1)}), bf16[64,8,128]{2,1,0:T(8,128)(2,1)S(1)}, u32[]{:S(2)}, u32[]{:S(2)}) async-start(bf16[64,8,128]{2,1,0:T(8,128)(2,1)} %bitcast.8), calls=%async_computation.2 | async-start | bytes 262144 | tf_op jit(solution)/shard_map/all_to_all | solution.py:92
  60.8 60.6 %reduce-scatter.2.cloned.1.call-start = ((), (), s32[]{:S(2)}) async-start(), calls=%async_computation.6 | async-start | bytes 1179648 | tf_op jit(solution)/shard_map/reduce_scatter | solution.py:252
  61.0 15.9 %collective-permute-start.4 = (bf16[2,128,512]{2,1,0:T(8,128)(2,1)S(1)}, bf16[2,128,512]{2,1,0:T(8,128)(2,1)S(1)}, u32[]{:S(2)}, u32[]{:S(2)}) collective-permute-start(bf16[2,128,512]{2,1,0:T(8,128)(2,1)S(1)} %pad_maximum_fusion.go0_ref), channel_id=1, source_target_pairs={{6,0},{0,2},{2,4},{4,6},{7,1},{1,3},{3,5},{5,7},{14,8},{8,10},{10,... | collective-permute-start | bytes 786440 | tf_op jit(solution)/shard_map/ppermute | solution.py:232
  63.4 13.5 %collective-permute-start.3 = (bf16[2,128,512]{2,1,0:T(8,128)(2,1)S(1)}, bf16[2,128,512]{2,1,0:T(8,128)(2,1)S(1)}, u32[]{:S(2)}, u32[]{:S(2)}) collective-permute-start(bf16[2,128,512]{2,1,0:T(8,128)(2,1)S(1)} %pad_maximum_fusion.go0_ref), channel_id=1, source_target_pairs={{4,0},{6,2},{0,4},{2,6},{5,1},{7,3},{1,5},{3,7},{12,8},{14,10},{8,... | collective-permute-start | bytes 786440 | tf_op jit(solution)/shard_map/ppermute | solution.py:232
  67.7 11.4 %collective-permute-start.2 = (bf16[2,128,512]{2,1,0:T(8,128)(2,1)S(1)}, bf16[2,128,512]{2,1,0:T(8,128)(2,1)S(1)}, u32[]{:S(2)}, u32[]{:S(2)}) collective-permute-start(bf16[2,128,512]{2,1,0:T(8,128)(2,1)S(1)} %pad_maximum_fusion.go0_ref), channel_id=1, source_target_pairs={{2,0},{4,2},{6,4},{0,6},{3,1},{5,3},{7,5},{1,7},{10,8},{12,10},{14... | collective-permute-start | bytes 786440 | tf_op jit(solution)/shard_map/ppermute | solution.py:232
  74.2 6.9 %collective-permute-start.5 = (bf16[128,512]{1,0:T(8,128)(2,1)S(1)}, bf16[128,512]{1,0:T(8,128)(2,1)S(1)}, u32[]{:S(2)}, u32[]{:S(2)}) collective-permute-start(bf16[128,512]{1,0:T(8,128)(2,1)S(1)} %get-tuple-element.20.mine_ref), channel_id=1, source_target_pairs={{0,64},{64,0},{1,65},{65,1},{2,66},{66,2},{3,67},{67,3},{4,68},{68... | collective-permute-start | bytes 393224 | tf_op jit(solution)/shard_map/ppermute | solution.py:248
  81.1 1.6 %copy-start.5 = (bf16[32,64,512]{2,1,0:T(8,128)(2,1)S(1)}, bf16[32,64,512]{2,1,0:T(8,128)(2,1)}, u32[]{:S(2)}) copy-start(bf16[32,64,512]{2,1,0:T(8,128)(2,1)} %all-gather.3.cloned.1.call-done) | copy-start | bytes 6291460
  86.0 6.9 %collective-permute-start.7 = (bf16[128,512]{1,0:T(8,128)(2,1)S(1)}, bf16[128,512]{1,0:T(8,128)(2,1)S(1)}, u32[]{:S(2)}, u32[]{:S(2)}) collective-permute-start(bf16[128,512]{1,0:T(8,128)(2,1)S(1)} %get-tuple-element.24), channel_id=1, source_target_pairs={{0,64},{64,0},{1,65},{65,1},{2,66},{66,2},{3,67},{67,3},{4,68},{68... | collective-permute-start | bytes 393224 | tf_op jit(solution)/shard_map/ppermute | solution.py:251
  116.8 17.4 %all-to-all-start.4 = ((bf16[64,8,128]{2,1,0:T(8,128)(2,1)}), bf16[64,8,128]{2,1,0:T(8,128)(2,1)S(1)}, u32[]{:S(2)}, u32[]{:S(2)}) async-start(bf16[64,8,128]{2,1,0:T(8,128)(2,1)} %bitcast.14), calls=%async_computation.5 | async-start | bytes 262144 | tf_op jit(solution)/shard_map/all_to_all | solution.py:92
  121.4 14.4 %collective-permute-start.6 = (bf16[128,512]{1,0:T(8,128)(2,1)}, bf16[128,512]{1,0:T(8,128)(2,1)S(1)}, u32[]{:S(2)}, u32[]{:S(2)}) collective-permute-start(bf16[128,512]{1,0:T(8,128)(2,1)} %bitcast.26), channel_id=1, source_target_pairs={{0,0},{1,64},{64,1},{65,65},{2,2},{3,66},{66,3},{67,67},{4,4},{5,6... | collective-permute-start | bytes 393224 | tf_op jit(solution)/shard_map/ppermute | solution.py:258
Sparse Core Ops, SparseCore 0:
  27.2 48.2 all-gather.2
  86.2 32.7 reduce-scatter.1

commit v3 on v2

v3 whole, which is shorter than its diff:
```python
import functools

import jax
import jax.numpy as jnp
from jax import lax
from jax.experimental import pallas as pl
from jax.experimental.pallas import tpu as pltpu
from jax.sharding import Mesh, PartitionSpec as P

HEAD_DIM = 128
HEADS_DEV = 4
TOK = 128
WIDTH = HEADS_DEV * HEAD_DIM
EPSILON = 1e-06
F32 = jnp.float32
BF16 = jnp.bfloat16
CTX = ("y", "zh", "zl")

NN = (((1,), (0,)), ((), ()))
NT = (((1,), (1,)), ((), ()))
TN = (((0,), (0,)), ((), ()))


def mm(a, b, dims):
    return lax.dot_general(a, b, dims, preferred_element_type=F32)


def head(h):
    return slice(h * HEAD_DIM, (h + 1) * HEAD_DIM)


def causal():
    rows = lax.broadcasted_iota(jnp.int32, (TOK, TOK), 0)
    cols = lax.broadcasted_iota(jnp.int32, (TOK, TOK), 1)
    return rows >= cols


def small():
    return pltpu.CompilerParams(vmem_limit_bytes=16 * 1024 * 1024)


def cost(flops, nbytes):
    return pl.CostEstimate(flops=flops, bytes_accessed=nbytes, transcendentals=0)


def blocks_of(value, parity):
    return jnp.concatenate(
        [value[:, 128 * j + 64 * parity : 128 * j + 64 * parity + 64] for j in range(4)], axis=1
    )


def vmem():
    return pl.BlockSpec(memory_space=pltpu.VMEM)


def hbm():
    return pl.BlockSpec(memory_space=pltpu.HBM)


def smem():
    return pl.BlockSpec(memory_space=pltpu.SMEM)


def in_hbm(value):
    return pltpu.with_memory_space_constraint(value, pltpu.HBM)


def state_kernel(k_ref, v_ref, out_ref):
    for h in range(HEADS_DEV):
        out_ref[head(h), :] = mm(k_ref[:, head(h)], v_ref[:, head(h)], TN).astype(BF16)


def local_state(keys, values):
    return pl.pallas_call(
        state_kernel,
        out_shape=jax.ShapeDtypeStruct((WIDTH, HEAD_DIM), BF16),
        compiler_params=small(),
        cost_estimate=cost(2 * TOK * WIDTH * HEAD_DIM, 400000),
        name="local_state",
    )(keys, values)


def split_kernel(place_ref, go_ref, keep_ref, send_ref):
    value = go_ref[...].astype(F32)
    even, odd = blocks_of(value, 0).astype(BF16), blocks_of(value, 1).astype(BF16)
    first = place_ref[0] == 0
    keep_ref[...] = jnp.where(first, even, odd)
    send_ref[...] = jnp.where(first, odd, even)


def split_columns(place, grad_out):
    half = jax.ShapeDtypeStruct((TOK, 256), BF16)
    return pl.pallas_call(
        split_kernel,
        in_specs=[smem(), vmem()],
        out_shape=(half, half),
        compiler_params=small(),
        cost_estimate=cost(TOK * WIDTH, 300000),
        name="split_columns",
    )(place, grad_out)


def scan_kernel(reverse, in_ref, out_ref):
    pairs = in_ref.shape[0] // 16
    total = jnp.zeros((8, HEAD_DIM), F32)
    order = range(pairs - 1, -1, -1) if reverse else range(pairs)
    for i in order:
        rows = slice(16 * i, 16 * i + 16)
        both = in_ref[rows, :].astype(F32)
        low, high = both[:8], both[8:]
        if reverse:
            then = total + high
            out_ref[rows, :] = jnp.concatenate([then, total], axis=0).astype(out_ref.dtype)
            total = then + low
        else:
            then = total + low
            out_ref[rows, :] = jnp.concatenate([total, then], axis=0).astype(out_ref.dtype)
            total = then + high


def exclusive_scan(pieces, reverse):
    return pl.pallas_call(
        functools.partial(scan_kernel, reverse),
        out_shape=jax.ShapeDtypeStruct(pieces.shape, pieces.dtype),
        cost_estimate=cost(WIDTH * HEAD_DIM, 300000),
        compiler_params=small(),
        name="scan_states",
    )(pieces)


def carried(state, reverse):
    pieces = lax.all_to_all(state.reshape(64, 8, HEAD_DIM), CTX, 0, 0)
    sums = exclusive_scan(pieces.reshape(WIDTH, HEAD_DIM), reverse)
    back = lax.all_to_all(sums.reshape(64, 8, HEAD_DIM), CTX, 0, 0)
    return back.reshape(WIDTH, HEAD_DIM)


def attend_kernel(q_ref, k_ref, v_ref, s_ref, flat_ref, normed_ref, scale_ref, p_ref):
    keep = causal()
    for h in range(HEADS_DEV):
        q, k, v = q_ref[:, head(h)], k_ref[:, head(h)], v_ref[:, head(h)]
        weights = jnp.where(keep, mm(q, k, NT), 0.0).astype(BF16)
        p_ref[:, head(h)] = weights
        attended = mm(weights, v, NN) + mm(q, s_ref[head(h), :], NN)
        scale = lax.rsqrt(jnp.mean(attended * attended, axis=-1, keepdims=True) + EPSILON)
        normed = attended * scale
        flat_ref[:, head(h)] = normed.astype(BF16)
        normed_ref[:, head(h)] = normed
        scale_ref[:, head(h)] = jnp.broadcast_to(scale, (TOK, HEAD_DIM))


def attend(queries, keys, values, before):
    flat = jax.ShapeDtypeStruct((TOK, WIDTH), BF16)
    wide = jax.ShapeDtypeStruct((TOK, WIDTH), F32)
    return pl.pallas_call(
        attend_kernel,
        out_shape=(flat, wide, wide, flat),
        cost_estimate=cost(6 * TOK * WIDTH * HEAD_DIM, 1500000),
        compiler_params=small(),
        name="attend",
    )(queries, keys, values, before)


def grad_normed_kernel(place_ref, w_ref, go0_ref, go1_ref, go3_ref, go2_ref, far_ref, own_ref, send_ref, w_buf, w_sem):
    x, core = place_ref[1], place_ref[2]
    groups = [2 * lax.rem(x + r, 4) + cs for r in (0, 1, 3, 2) for cs in (core, 1 - core)]
    pieces = [ref.at[i] for ref in (go0_ref, go1_ref, go3_ref) for i in range(2)] + [go2_ref, far_ref]
    loads = [pltpu.make_async_copy(w_ref.at[g], w_buf.at[g], w_sem.at[i]) for i, g in enumerate(groups)]
    for load in loads:
        load.start()
    grad = jnp.zeros((2 * TOK, WIDTH), F32)
    for i in range(8):
        loads[i].wait()
        grad = grad + mm(pieces[i][...].reshape(2 * TOK, 256), w_buf[groups[i]], NN)
    own_ref[...] = grad[:TOK]
    send_ref[...] = grad[TOK:].astype(BF16)


def grad_normed_parts(place, weight, grad_parts):
    return pl.pallas_call(
        grad_normed_kernel,
        in_specs=[smem(), hbm()] + [vmem()] * 5,
        out_specs=(vmem(), vmem(), vmem()),
        out_shape=(
            jax.ShapeDtypeStruct((TOK, WIDTH), F32),
            jax.ShapeDtypeStruct((TOK, WIDTH), BF16),
            jax.ShapeDtypeStruct((8, 256, WIDTH), BF16),
        ),
        scratch_shapes=[pltpu.SemaphoreType.DMA((8,))],
        compiler_params=small(),
        cost_estimate=cost(2 * TOK * WIDTH * 4096, 4000000),
        name="grad_normed",
    )(place, weight, *grad_parts)


def project_kernel(w_ref, own_ref, other_ref, part_ref, out_buf, out_sem):
    stores = [pltpu.make_async_copy(out_buf.at[g], part_ref.at[g], out_sem.at[g]) for g in range(8)]
    normed = jnp.concatenate([own_ref[...], other_ref[...]], axis=0)
    for g in range(8):
        out_buf[g] = mm(normed, w_ref[g], NT).astype(BF16).reshape(2, TOK, 256)
        stores[g].start()
    for store in stores:
        store.wait()


def project(weight, own, other):
    return pl.pallas_call(
        project_kernel,
        in_specs=[vmem()] * 3,
        out_specs=hbm(),
        out_shape=jax.ShapeDtypeStruct((8, 2, TOK, 256), BF16),
        scratch_shapes=[pltpu.VMEM((8, 2, TOK, 256), BF16), pltpu.SemaphoreType.DMA((8,))],
        compiler_params=small(),
        cost_estimate=cost(2 * TOK * WIDTH * 4096, 4000000),
        name="project",
    )(weight, own, other)


def grad_attended_kernel(own_ref, got_ref, normed_ref, scale_ref, q_ref, ga_ref, state_ref):
    for h in range(HEADS_DEV):
        grad_normed = own_ref[:, head(h)] + got_ref[:, head(h)].astype(F32)
        normed = normed_ref[:, head(h)]
        mean = jnp.mean(grad_normed * normed, axis=-1, keepdims=True)
        ga = (scale_ref[:, head(h)] * (grad_normed - normed * mean)).astype(BF16)
        ga_ref[:, head(h)] = ga
        state_ref[head(h), :] = mm(q_ref[:, head(h)], ga, TN).astype(BF16)


def grad_attended(own, got, normed, scale, queries):
    return pl.pallas_call(
        grad_attended_kernel,
        out_shape=(
            jax.ShapeDtypeStruct((TOK, WIDTH), BF16),
            jax.ShapeDtypeStruct((WIDTH, HEAD_DIM), BF16),
        ),
        compiler_params=small(),
        cost_estimate=cost(2 * TOK * WIDTH * HEAD_DIM, 1200000),
        name="grad_attended",
    )(own, got, normed, scale, queries)


def grads_block_kernel(q_ref, k_ref, v_ref, p_ref, ga_ref, s_ref, gq_ref, gk_ref, gv_ref):
    keep = causal()
    for h in range(HEADS_DEV):
        q, k, v, ga = q_ref[:, head(h)], k_ref[:, head(h)], v_ref[:, head(h)], ga_ref[:, head(h)]
        scores = jnp.where(keep, mm(ga, v, NT), 0.0).astype(BF16)
        gq_ref[:, head(h)] = (mm(scores, k, NN) + mm(ga, s_ref[head(h), :], NT)).astype(BF16)
        gk_ref[:, head(h)] = mm(scores, q, TN)
        gv_ref[:, head(h)] = mm(p_ref[:, head(h)], ga, TN)


def grads_block(queries, keys, values, weights, ga, before):
    flat = jax.ShapeDtypeStruct((TOK, WIDTH), BF16)
    wide = jax.ShapeDtypeStruct((TOK, WIDTH), F32)
    return pl.pallas_call(
        grads_block_kernel,
        out_shape=(flat, wide, wide),
        compiler_params=small(),
        cost_estimate=cost(10 * TOK * WIDTH * HEAD_DIM, 1500000),
        name="grads_block",
    )(queries, keys, values, weights, ga, before)


def finish_kernel(place_ref, k_ref, v_ref, g_ref, gk_in_ref, gv_in_ref, keep_ref, got_ref, mixed_ref, gk_ref, gv_ref):
    keep, got = keep_ref[...].astype(F32), got_ref[...].astype(F32)
    first = place_ref[0] == 0
    even, odd = jnp.where(first, keep, got), jnp.where(first, got, keep)
    for j in range(4):
        cols = slice(64 * j, 64 * j + 64)
        mixed_ref[:, head(j)] = jnp.concatenate([even[:, cols], odd[:, cols]], axis=1).astype(BF16)
    for h in range(HEADS_DEV):
        after = g_ref[head(h), :]
        gk_ref[:, head(h)] = (gk_in_ref[:, head(h)] + mm(v_ref[:, head(h)], after, NT)).astype(BF16)
        gv_ref[:, head(h)] = (gv_in_ref[:, head(h)] + mm(k_ref[:, head(h)], after, NN)).astype(BF16)


def finish(place, keys, values, after, grad_key, grad_value, keep, got):
    flat = jax.ShapeDtypeStruct((TOK, WIDTH), BF16)
    return pl.pallas_call(
        finish_kernel,
        in_specs=[smem()] + [vmem()] * 7,
        out_shape=(flat, flat, flat),
        compiler_params=small(),
        cost_estimate=cost(4 * TOK * WIDTH * HEAD_DIM, 1500000),
        name="finish",
    )(place, keys, values, after, grad_key, grad_value, keep, got)


def tied(first, second):
    return lax.optimization_barrier((first, second))


SWAP = [(0, 1), (1, 0)]


def repeated(value, times):
    return jnp.broadcast_to(value, (times,) + value.shape)


def shifted(value, axis, step):
    return lax.ppermute(value, axis, [((i + step) % 4, i) for i in range(4)])


def local(queries, keys, values, out_weight, grad_out):
    place = jnp.stack([lax.axis_index(n) for n in ("zl", "x", "core")]).astype(jnp.int32)
    rows = lax.all_to_all(repeated(out_weight.T, 4), "zh", 0, 0)
    grad_keep, grad_send = split_columns(place, in_hbm(grad_out))
    grad_got = lax.ppermute(grad_send, "zl", SWAP)
    state = local_state(in_hbm(keys), in_hbm(values))
    (grad_got, rows), state = tied((grad_got, rows), state)
    grad_pair = jnp.stack([grad_keep, grad_got])
    weight = lax.all_gather(rows, "y").reshape(8, 256, WIDTH)
    weight = in_hbm(weight)
    grad_cores = jnp.stack([grad_pair, lax.ppermute(grad_pair, "core", SWAP)])
    grad_far = shifted(grad_pair, "x", 2)
    grad_parts = [grad_cores] + [shifted(grad_cores, "x", r) for r in (1, 3)]
    grad_parts += [grad_far, lax.ppermute(grad_far, "core", SWAP)]
    before = carried(state, False)
    flat, normed, scale, weights = attend(queries, keys, values, before)
    flat_other = lax.ppermute(flat, "zl", SWAP)
    own, send, weight = grad_normed_parts(place, weight, grad_parts)
    flat, send = tied(flat, send)
    got = lax.ppermute(send, "zl", SWAP)
    parts = project(weight, flat, flat_other)
    mixed_pair = lax.psum_scatter(parts, ("x", "core"), scatter_dimension=0, tiled=False)
    ga, grad_state = grad_attended(own, got, normed, scale, queries)
    after = carried(grad_state, True)
    grad_query, grad_key, grad_value = grads_block(queries, keys, values, weights, ga, before)
    mixed_got = lax.ppermute(mixed_pair[1], "zl", SWAP)
    mixed, grad_key, grad_value = finish(
        place, keys, values, after, grad_key, grad_value, mixed_pair[0], mixed_got
    )
    return mixed, grad_query, grad_key, grad_value


def solution(mesh):
    finer = Mesh(mesh.devices.reshape(8, 4, 2, 4, 2), ("y", "zh", "zl", "x", "core"))
    spec = P(CTX, ("x", "core"))
    return jax.shard_map(
        local,
        mesh=finer,
        in_specs=(spec, spec, spec, P(("x", "core"), CTX), spec),
        out_specs=(spec, spec, spec, spec),
        check_vma=False,
    )
```

time: 145 us -> 140 us (0.966)
  waiting for transfers between devices: 42.5 us -> 31.5 us
  starting transfers between devices: 49.2 us -> 55.4 us
  Pallas kernels: 8.1 us -> 12.2 us
  local copies, waits for them, and re-layouts: 6.38 us -> 3.21 us
  blocking collectives: 22.8 us -> 21.2 us
    ppermute x8 -> x9, starting transfers between devices: 18.8 us -> 25.2 us  [the longest x3 9.24 us: shifted(): return lax.ppermute(value, axis, [((i + step) % 4, i) for i in range(4)])]
    all_to_all x1, waiting for transfers between devices: 7.75 us -> 2.66 us  [local(): rows = lax.all_to_all(repeated(out_weight.T, 4), 'zh', 0, 0)]
    all_to_all x1, starting transfers between devices: 14 us -> 9.9 us  [carried(): pieces = lax.all_to_all(state.reshape(64, 8, HEAD_DIM), CTX, 0, 0)]
    unnamed x15 -> x8, local copies, waits for them, and re-layouts: 4.77 us -> 0.73 us
    all_to_all x1, waiting for transfers between devices: 10.9 us -> 7.33 us  [carried(): pieces = lax.all_to_all(state.reshape(64, 8, HEAD_DIM), CTX, 0, 0)]
    all_to_all x1, starting transfers between devices: 7.09 us -> 10.3 us  [local(): rows = lax.all_to_all(repeated(out_weight.T, 4), 'zh', 0, 0)]
    pallas_call x2 -> x5, Pallas kernels: 4.99 us -> 8.09 us  [the longest x1 2.63 us: grad_normed_parts(): pl.pallas_call(grad_normed_kernel, in_specs=[smem(), hbm()] + [vmem()] *...]
    all_to_all x2, waiting for transfers between devices: 15.3 us -> 13 us  [carried(): back = lax.all_to_all(sums.reshape(64, 8, HEAD_DIM), CTX, 0, 0)]
  transfers between devices with their start and end apart: 14 -> 15, of which waited for: 7 -> 7; matrix products, arithmetic and copies ran while one was open for 0% -> 1% of each run, Pallas kernels for 3% -> 7%
where the time goes in v3:
time: 140 us; the launch traced here: 138 us
  starting transfers between devices  55.4 us (40%)
  waiting for transfers between devices  31.5 us (22%)
  blocking collectives  21.2 us (15%)
  between operations  14.3 us (10%)
  Pallas kernels  12.2 us (9%)
  local copies, waits for them, and re-layouts  3.21 us (2%)
    all_to_all x1, blocking collectives, carried(): pieces = lax.all_to_all(state.reshape(64, 8, HEAD_DIM), CTX, 0, 0)  21.2 us
    all_to_all x2, waiting for transfers between devices, carried(): back = lax.all_to_all(sums.reshape(64, 8, HEAD_DIM), CTX, 0, 0)  13 us
    all_to_all x1, starting transfers between devices, local(): rows = lax.all_to_all(repeated(out_weight.T, 4), 'zh', 0, 0)  10.3 us
    all_to_all x2, starting transfers between devices, carried(): back = lax.all_to_all(sums.reshape(64, 8, HEAD_DIM), CTX, 0, 0)  9.99 us
    all_to_all x1, starting transfers between devices, carried(): pieces = lax.all_to_all(state.reshape(64, 8, HEAD_DIM), CTX, 0, 0)  9.9 us
    ppermute x3, starting transfers between devices, shifted(): return lax.ppermute(value, axis, [((i + step) % 4, i) for i in range(4)])  9.24 us
    all_to_all x1, waiting for transfers between devices, carried(): pieces = lax.all_to_all(state.reshape(64, 8, HEAD_DIM), CTX, 0, 0)  7.33 us
    ppermute x1, waiting for transfers between devices, local(): got = lax.ppermute(send, 'zl', SWAP)  4.18 us
  transfers between devices with their start and end apart: 15, of which 7 were waited for; matrix products, arithmetic and copies ran while one was open for 1% of the time, Pallas kernels for 7%

profile of v3, /device:TPU:6, one launch (start us, length us, event | category | flops | bytes accessed | tf_op | source)
XLA Modules:
  0.0 137.9 jit_solution(16603985607528565969)
XLA Ops:
  7.2 1.6 %broadcast_in_dim.3 = bf16[4,64,512]{2,1,0:T(8,128)(2,1)} broadcast(bf16[64,512]{1,0:T(8,128)(2,1)} %bitcast.31), dimensions={1,2} | broadcast | bytes 327680 | tf_op jit(solution)/shard_map/broadcast_in_dim | solution.py:297
  8.8 10.3 %all-to-all-start = ((bf16[4,64,512]{2,1,0:T(8,128)(2,1)}), bf16[4,64,512]{2,1,0:T(8,128)(2,1)S(1)}, u32[]{:S(2)}, u32[]{:S(2)}) async-start(bf16[4,64,512]{2,1,0:T(8,128)(2,1)} %broadcast_in_dim.3), calls=%async_computation | async-start | bytes 524288 | tf_op jit(solution)/shard_map/all_to_all | solution.py:306
  20.2 3.4 %collective-permute-start = (bf16[128,256]{1,0:T(8,128)(2,1)S(1)}, bf16[128,256]{1,0:T(8,128)(2,1)S(1)}, u32[]{:S(2)}, u32[]{:S(2)}) collective-permute-start(bf16[128,256]{1,0:T(8,128)(2,1)S(1)} %get-tuple-element.26), channel_id=1, source_target_pairs={{0,8},{8,0},{1,9},{9,1},{2,10},{10,2},{3,11},{11,3},{4,12},{12,4},... | collective-permute-start | bytes 196616 | tf_op jit(solution)/shard_map/ppermute | solution.py:308
  23.6 1.8 %local_state.1 = bf16[512,128]{1,0:T(8,128)(2,1)} custom-call(bf16[128,512]{1,0:T(8,128)(2,1)} %k_ref.7, bf16[128,512]{1,0:T(8,128)(2,1)} %v_ref.7), custom_call_target="tpu_custom_call" | custom-call | flops 16777216 | bytes 400000 | tf_op jit(solution)/shard_map/local_state/pallas_call | solution.py:74
  25.4 2.7 %collective-permute-done = bf16[128,256]{1,0:T(8,128)(2,1)S(1)} collective-permute-done((bf16[128,256]{1,0:T(8,128)(2,1)S(1)}, bf16[128,256]{1,0:T(8,128)(2,1)S(1)}, u32[]{:S(2)}, u32[]{:S(2)}) %collective-permute-start) | collective-permute-done | bytes 65568 | tf_op jit(solution)/shard_map/ppermute | solution.py:308
  28.2 2.7 %all-to-all-done = bf16[4,64,512]{2,1,0:T(8,128)(2,1)S(1)} async-done(((bf16[4,64,512]{2,1,0:T(8,128)(2,1)}), bf16[4,64,512]{2,1,0:T(8,128)(2,1)S(1)}, u32[]{:S(2)}, u32[]{:S(2)}) %all-to-all-start) | async-done | bytes 262176 | tf_op jit(solution)/shard_map/all_to_all | solution.py:306
  31.6 9.9 %all-to-all-start.1 = ((bf16[64,8,128]{2,1,0:T(8,128)(2,1)}), bf16[64,8,128]{2,1,0:T(8,128)(2,1)S(1)}, u32[]{:S(2)}, u32[]{:S(2)}) async-start(bf16[64,8,128]{2,1,0:T(8,128)(2,1)} %bitcast.9), calls=%async_computation.1 | async-start | bytes 262144 | tf_op jit(solution)/shard_map/all_to_all | solution.py:132
  41.5 1.9 %collective-permute-start.1 = (bf16[2,128,256]{2,1,0:T(8,128)(2,1)S(1)}, bf16[2,128,256]{2,1,0:T(8,128)(2,1)S(1)}, u32[]{:S(2)}, u32[]{:S(2)}) collective-permute-start(bf16[2,128,256]{2,1,0:T(8,128)(2,1)S(1)} %get-tuple-element.51), channel_id=1, source_target_pairs={{0,1},{1,0},{2,3},{3,2},{4,5},{5,4},{6,7},{7,6},{8,9},{9,8},{10,11... | collective-permute-start | bytes 393224 | tf_op jit(solution)/shard_map/ppermute | solution.py:314
  43.4 3.3 %collective-permute-start.4 = (bf16[2,128,256]{2,1,0:T(8,128)(2,1)S(1)}, bf16[2,128,256]{2,1,0:T(8,128)(2,1)S(1)}, u32[]{:S(2)}, u32[]{:S(2)}) collective-permute-start(bf16[2,128,256]{2,1,0:T(8,128)(2,1)S(1)} %get-tuple-element.51), channel_id=1, source_target_pairs={{4,0},{6,2},{0,4},{2,6},{5,1},{7,3},{1,5},{3,7},{12,8},{14,10},{8,... | collective-permute-start | bytes 393224 | tf_op jit(solution)/shard_map/ppermute | solution.py:301
  46.7 7.3 %all-to-all-done.1 = bf16[64,8,128]{2,1,0:T(8,128)(2,1)S(1)} async-done(((bf16[64,8,128]{2,1,0:T(8,128)(2,1)}), bf16[64,8,128]{2,1,0:T(8,128)(2,1)S(1)}, u32[]{:S(2)}, u32[]{:S(2)}) %all-to-all-start.1) | async-done | bytes 131104 | tf_op jit(solution)/shard_map/all_to_all | solution.py:132
  54.8 5.4 %all-to-all-start.2 = ((bf16[64,8,128]{2,1,0:T(8,128)(2,1)}), bf16[64,8,128]{2,1,0:T(8,128)(2,1)S(1)}, u32[]{:S(2)}, u32[]{:S(2)}) async-start(bf16[64,8,128]{2,1,0:T(8,128)(2,1)} %bitcast.11), calls=%async_computation.2 | async-start | bytes 262144 | tf_op jit(solution)/shard_map/all_to_all | solution.py:134
  60.3 4.0 %collective-permute-start.3 = (bf16[2,2,128,256]{3,2,1,0:T(8,128)(2,1)S(1)}, bf16[2,2,128,256]{3,2,1,0:T(8,128)(2,1)S(1)}, u32[]{:S(2)}, u32[]{:S(2)}) collective-permute-start(bf16[2,2,128,256]{3,2,1,0:T(8,128)(2,1)S(1)} %pad_maximum_fusion.go0_ref), channel_id=1, source_target_pairs={{6,0},{0,2},{2,4},{4,6},{7,1},{1,3},{3,5},{5,7},{14,8},{8,10},{10,... | collective-permute-start | bytes 786440 | tf_op jit(solution)/shard_map/ppermute | solution.py:301
  64.3 1.9 %collective-permute-start.2 = (bf16[2,2,128,256]{3,2,1,0:T(8,128)(2,1)S(1)}, bf16[2,2,128,256]{3,2,1,0:T(8,128)(2,1)S(1)}, u32[]{:S(2)}, u32[]{:S(2)}) collective-permute-start(bf16[2,2,128,256]{3,2,1,0:T(8,128)(2,1)S(1)} %pad_maximum_fusion.go0_ref), channel_id=1, source_target_pairs={{2,0},{4,2},{6,4},{0,6},{3,1},{5,3},{7,5},{1,7},{10,8},{12,10},{14... | collective-permute-start | bytes 786440 | tf_op jit(solution)/shard_map/ppermute | solution.py:301
  66.2 1.9 %collective-permute-start.5 = (bf16[2,128,256]{2,1,0:T(8,128)(2,1)S(1)}, bf16[2,128,256]{2,1,0:T(8,128)(2,1)S(1)}, u32[]{:S(2)}, u32[]{:S(2)}) collective-permute-start(bf16[2,128,256]{2,1,0:T(8,128)(2,1)S(1)} %collective-permute-done.4.go2_ref), channel_id=1, source_target_pairs={{0,1},{1,0},{2,3},{3,2},{4,5},{5,4},{6,7},{7,6},{8,9},{9,8},{10,11... | collective-permute-start | bytes 393224 | tf_op jit(solution)/shard_map/ppermute | solution.py:317
  68.2 6.0 %all-to-all-done.2 = bf16[64,8,128]{2,1,0:T(8,128)(2,1)S(1)} async-done(((bf16[64,8,128]{2,1,0:T(8,128)(2,1)}), bf16[64,8,128]{2,1,0:T(8,128)(2,1)S(1)}, u32[]{:S(2)}, u32[]{:S(2)}) %all-to-all-start.2) | async-done | bytes 131104 | tf_op jit(solution)/shard_map/all_to_all | solution.py:134
  74.7 2.7 %collective-permute-start.7 = (bf16[128,512]{1,0:T(8,128)(2,1)S(1)}, bf16[128,512]{1,0:T(8,128)(2,1)S(1)}, u32[]{:S(2)}, u32[]{:S(2)}) collective-permute-start(bf16[128,512]{1,0:T(8,128)(2,1)S(1)} %get-tuple-element.43.own_ref), channel_id=1, source_target_pairs={{0,8},{8,0},{1,9},{9,1},{2,10},{10,2},{3,11},{11,3},{4,12},{12,4},... | collective-permute-start | bytes 393224 | tf_op jit(solution)/shard_map/ppermute | solution.py:320
  77.4 2.6 %grad_normed.1 = (f32[128,512]{1,0:T(8,128)S(1)}, bf16[128,512]{1,0:T(8,128)(2,1)S(1)}, bf16[8,256,512]{2,1,0:T(8,128)(2,1)S(1)}) custom-call(s32[3]{0:T(128)S(1)} %pad_add_fusion.place_ref, bf16[8,256,512]{2,1,0:T(8,128)(2,1)} %bitcast.29, bf16[2,2,128,256]{3,2,1,0:T(8,128)(2,1)S(1)} %pad_maximum_fusion.go0_ref, ...), custom_call_target="tpu_custom_call" | custom-call | flops 536870912 | bytes 4000000 | tf_op jit(solution)/shard_map/grad_normed/pallas_call | solution.py:180
  81.5 1.5 %project.1 = bf16[8,2,128,256]{3,2,1,0:T(8,128)(2,1)} custom-call(bf16[8,256,512]{2,1,0:T(8,128)(2,1)S(1)} %get-tuple-element.42.w_ref, bf16[128,512]{1,0:T(8,128)(2,1)S(1)} %get-tuple-element.43.own_ref, bf16[128,512]{1,0:T(8,128)(2,1)S(1)} %collective-permute-done.7.other_ref), custom_call_target="tpu_custom_call" | custom-call | flops 536870912 | bytes 4000000 | tf_op jit(solution)/shard_map/project/pallas_call | solution.py:207
  83.1 2.7 %collective-permute-start.6 = (bf16[128,512]{1,0:T(8,128)(2,1)S(1)}, bf16[128,512]{1,0:T(8,128)(2,1)S(1)}, u32[]{:S(2)}, u32[]{:S(2)}) collective-permute-start(bf16[128,512]{1,0:T(8,128)(2,1)S(1)} %get-tuple-element.34), channel_id=1, source_target_pairs={{0,8},{8,0},{1,9},{9,1},{2,10},{10,2},{3,11},{11,3},{4,12},{12,4},... | collective-permute-start | bytes 393224 | tf_op jit(solution)/shard_map/ppermute | solution.py:323
  85.8 4.2 %collective-permute-done.6.got_ref = bf16[128,512]{1,0:T(8,128)(2,1)S(1)} collective-permute-done((bf16[128,512]{1,0:T(8,128)(2,1)S(1)}, bf16[128,512]{1,0:T(8,128)(2,1)S(1)}, u32[]{:S(2)}, u32[]{:S(2)}) %collective-permute-start.6) | collective-permute-done | bytes 131104 | tf_op jit(solution)/shard_map/ppermute | solution.py:323
  90.3 21.2 %all_to_all.25 = bf16[64,8,128]{2,1,0:T(8,128)(2,1)S(1)} all-to-all(bf16[64,8,128]{2,1,0:T(8,128)(2,1)S(1)} %bitcast.27), channel_id=1, replica_groups=mesh['y'=8,'zh'=4,'zl'=2,'x'=4,'core'=2] {'y','zh','zl'}, dimensions={0} | all-to-all | bytes 262144 | tf_op jit(solution)/shard_map/all_to_all | solution.py:132
  112.2 4.6 %all-to-all-start.4 = ((bf16[64,8,128]{2,1,0:T(8,128)(2,1)}), bf16[64,8,128]{2,1,0:T(8,128)(2,1)S(1)}, u32[]{:S(2)}, u32[]{:S(2)}) async-start(bf16[64,8,128]{2,1,0:T(8,128)(2,1)} %bitcast.15), calls=%async_computation.4 | async-start | bytes 262144 | tf_op jit(solution)/shard_map/all_to_all | solution.py:134
  117.8 3.4 %collective-permute-start.8 = (bf16[128,256]{1,0:T(8,128)(2,1)S(1)}, bf16[128,256]{1,0:T(8,128)(2,1)S(1)}, u32[]{:S(2)}, u32[]{:S(2)}) collective-permute-start(bf16[128,256]{1,0:T(8,128)(2,1)S(1)} %get-tuple-element.48), channel_id=1, source_target_pairs={{0,8},{8,0},{1,9},{9,1},{2,10},{10,2},{3,11},{11,3},{4,12},{12,4},... | collective-permute-start | bytes 196616 | tf_op jit(solution)/shard_map/ppermute | solution.py:329
  122.5 7.1 %all-to-all-done.4 = bf16[64,8,128]{2,1,0:T(8,128)(2,1)S(1)} async-done(((bf16[64,8,128]{2,1,0:T(8,128)(2,1)}), bf16[64,8,128]{2,1,0:T(8,128)(2,1)S(1)}, u32[]{:S(2)}, u32[]{:S(2)}) %all-to-all-start.4) | async-done | bytes 131104 | tf_op jit(solution)/shard_map/all_to_all | solution.py:134
  (32 shorter events, 9.5 us)
Async XLA Ops:
  7.2 67.0 %copy-start.1 = (bf16[128,512]{1,0:T(8,128)(2,1)S(1)}, bf16[128,512]{1,0:T(8,128)(2,1)}, u32[]{:S(2)}) copy-start(bf16[128,512]{1,0:T(8,128)(2,1)} %v_ref.7) | copy-start | bytes 393220
  7.2 67.0 %copy-start = (bf16[128,512]{1,0:T(8,128)(2,1)S(1)}, bf16[128,512]{1,0:T(8,128)(2,1)}, u32[]{:S(2)}) copy-start(bf16[128,512]{1,0:T(8,128)(2,1)} %k_ref.7) | copy-start | bytes 393220
  7.2 67.0 %copy-start.2 = (bf16[128,512]{1,0:T(8,128)(2,1)S(1)}, bf16[128,512]{1,0:T(8,128)(2,1)}, u32[]{:S(2)}) copy-start(bf16[128,512]{1,0:T(8,128)(2,1)} %q_ref.5) | copy-start | bytes 393220
  8.8 22.0 %all-to-all-start = ((bf16[4,64,512]{2,1,0:T(8,128)(2,1)}), bf16[4,64,512]{2,1,0:T(8,128)(2,1)S(1)}, u32[]{:S(2)}, u32[]{:S(2)}) async-start(bf16[4,64,512]{2,1,0:T(8,128)(2,1)} %broadcast_in_dim.3), calls=%async_computation | async-start | bytes 524288 | tf_op jit(solution)/shard_map/all_to_all | solution.py:306
  19.1 58.3 %all-gather.3.cloned.1.call-start = ((), (), s32[]{:S(2)}) async-start(), calls=%async_computation.7 | async-start | bytes 2359296 | tf_op jit(solution)/shard_map/all_gather | solution.py:312
  20.2 7.9 %collective-permute-start = (bf16[128,256]{1,0:T(8,128)(2,1)S(1)}, bf16[128,256]{1,0:T(8,128)(2,1)S(1)}, u32[]{:S(2)}, u32[]{:S(2)}) collective-permute-start(bf16[128,256]{1,0:T(8,128)(2,1)S(1)} %get-tuple-element.26), channel_id=1, source_target_pairs={{0,8},{8,0},{1,9},{9,1},{2,10},{10,2},{3,11},{11,3},{4,12},{12,4},... | collective-permute-start | bytes 196616 | tf_op jit(solution)/shard_map/ppermute | solution.py:308
  30.8 0.7 copy-start.3
  31.6 22.5 %all-to-all-start.1 = ((bf16[64,8,128]{2,1,0:T(8,128)(2,1)}), bf16[64,8,128]{2,1,0:T(8,128)(2,1)S(1)}, u32[]{:S(2)}, u32[]{:S(2)}) async-start(bf16[64,8,128]{2,1,0:T(8,128)(2,1)} %bitcast.9), calls=%async_computation.1 | async-start | bytes 262144 | tf_op jit(solution)/shard_map/all_to_all | solution.py:132
  41.5 18.7 %collective-permute-start.1 = (bf16[2,128,256]{2,1,0:T(8,128)(2,1)S(1)}, bf16[2,128,256]{2,1,0:T(8,128)(2,1)S(1)}, u32[]{:S(2)}, u32[]{:S(2)}) collective-permute-start(bf16[2,128,256]{2,1,0:T(8,128)(2,1)S(1)} %get-tuple-element.51), channel_id=1, source_target_pairs={{0,1},{1,0},{2,3},{3,2},{4,5},{5,4},{6,7},{7,6},{8,9},{9,8},{10,11... | collective-permute-start | bytes 393224 | tf_op jit(solution)/shard_map/ppermute | solution.py:314
  43.4 22.8 %collective-permute-start.4 = (bf16[2,128,256]{2,1,0:T(8,128)(2,1)S(1)}, bf16[2,128,256]{2,1,0:T(8,128)(2,1)S(1)}, u32[]{:S(2)}, u32[]{:S(2)}) collective-permute-start(bf16[2,128,256]{2,1,0:T(8,128)(2,1)S(1)} %get-tuple-element.51), channel_id=1, source_target_pairs={{4,0},{6,2},{0,4},{2,6},{5,1},{7,3},{1,5},{3,7},{12,8},{14,10},{8,... | collective-permute-start | bytes 393224 | tf_op jit(solution)/shard_map/ppermute | solution.py:301
  54.8 19.3 %all-to-all-start.2 = ((bf16[64,8,128]{2,1,0:T(8,128)(2,1)}), bf16[64,8,128]{2,1,0:T(8,128)(2,1)S(1)}, u32[]{:S(2)}, u32[]{:S(2)}) async-start(bf16[64,8,128]{2,1,0:T(8,128)(2,1)} %bitcast.11), calls=%async_computation.2 | async-start | bytes 262144 | tf_op jit(solution)/shard_map/all_to_all | solution.py:134
  60.2 56.7 %reduce-scatter.2.cloned.1.call-start = ((), (), s32[]{:S(2)}) async-start(), calls=%async_computation.6 | async-start | bytes 1179648 | tf_op jit(solution)/shard_map/reduce_scatter | solution.py:325
  60.3 17.1 %collective-permute-start.3 = (bf16[2,2,128,256]{3,2,1,0:T(8,128)(2,1)S(1)}, bf16[2,2,128,256]{3,2,1,0:T(8,128)(2,1)S(1)}, u32[]{:S(2)}, u32[]{:S(2)}) collective-permute-start(bf16[2,2,128,256]{3,2,1,0:T(8,128)(2,1)S(1)} %pad_maximum_fusion.go0_ref), channel_id=1, source_target_pairs={{6,0},{0,2},{2,4},{4,6},{7,1},{1,3},{3,5},{5,7},{14,8},{8,10},{10,... | collective-permute-start | bytes 786440 | tf_op jit(solution)/shard_map/ppermute | solution.py:301
  64.3 13.1 %collective-permute-start.2 = (bf16[2,2,128,256]{3,2,1,0:T(8,128)(2,1)S(1)}, bf16[2,2,128,256]{3,2,1,0:T(8,128)(2,1)S(1)}, u32[]{:S(2)}, u32[]{:S(2)}) collective-permute-start(bf16[2,2,128,256]{3,2,1,0:T(8,128)(2,1)S(1)} %pad_maximum_fusion.go0_ref), channel_id=1, source_target_pairs={{2,0},{4,2},{6,4},{0,6},{3,1},{5,3},{7,5},{1,7},{10,8},{12,10},{14... | collective-permute-start | bytes 786440 | tf_op jit(solution)/shard_map/ppermute | solution.py:301
  66.2 11.1 %collective-permute-start.5 = (bf16[2,128,256]{2,1,0:T(8,128)(2,1)S(1)}, bf16[2,128,256]{2,1,0:T(8,128)(2,1)S(1)}, u32[]{:S(2)}, u32[]{:S(2)}) collective-permute-start(bf16[2,128,256]{2,1,0:T(8,128)(2,1)S(1)} %collective-permute-done.4.go2_ref), channel_id=1, source_target_pairs={{0,1},{1,0},{2,3},{3,2},{4,5},{5,4},{6,7},{7,6},{8,9},{9,8},{10,11... | collective-permute-start | bytes 393224 | tf_op jit(solution)/shard_map/ppermute | solution.py:317
  74.7 6.9 %collective-permute-start.7 = (bf16[128,512]{1,0:T(8,128)(2,1)S(1)}, bf16[128,512]{1,0:T(8,128)(2,1)S(1)}, u32[]{:S(2)}, u32[]{:S(2)}) collective-permute-start(bf16[128,512]{1,0:T(8,128)(2,1)S(1)} %get-tuple-element.43.own_ref), channel_id=1, source_target_pairs={{0,8},{8,0},{1,9},{9,1},{2,10},{10,2},{3,11},{11,3},{4,12},{12,4},... | collective-permute-start | bytes 393224 | tf_op jit(solution)/shard_map/ppermute | solution.py:320
  83.1 6.9 %collective-permute-start.6 = (bf16[128,512]{1,0:T(8,128)(2,1)S(1)}, bf16[128,512]{1,0:T(8,128)(2,1)S(1)}, u32[]{:S(2)}, u32[]{:S(2)}) collective-permute-start(bf16[128,512]{1,0:T(8,128)(2,1)S(1)} %get-tuple-element.34), channel_id=1, source_target_pairs={{0,8},{8,0},{1,9},{9,1},{2,10},{10,2},{3,11},{11,3},{4,12},{12,4},... | collective-permute-start | bytes 393224 | tf_op jit(solution)/shard_map/ppermute | solution.py:323
  112.2 17.4 %all-to-all-start.4 = ((bf16[64,8,128]{2,1,0:T(8,128)(2,1)}), bf16[64,8,128]{2,1,0:T(8,128)(2,1)S(1)}, u32[]{:S(2)}, u32[]{:S(2)}) async-start(bf16[64,8,128]{2,1,0:T(8,128)(2,1)} %bitcast.15), calls=%async_computation.4 | async-start | bytes 262144 | tf_op jit(solution)/shard_map/all_to_all | solution.py:134
  117.8 11.8 %collective-permute-start.8 = (bf16[128,256]{1,0:T(8,128)(2,1)S(1)}, bf16[128,256]{1,0:T(8,128)(2,1)S(1)}, u32[]{:S(2)}, u32[]{:S(2)}) collective-permute-start(bf16[128,256]{1,0:T(8,128)(2,1)S(1)} %get-tuple-element.48), channel_id=1, source_target_pairs={{0,8},{8,0},{1,9},{9,1},{2,10},{10,2},{3,11},{11,3},{4,12},{12,4},... | collective-permute-start | bytes 196616 | tf_op jit(solution)/shard_map/ppermute | solution.py:329
Sparse Core Ops, SparseCore 0:
  31.7 43.8 all-gather.2
  83.2 30.8 reduce-scatter.1

commit v4 on v3

--- a/solution.py
+++ b/solution.py
@@ -173,7 +173,7 @@
         loads[i].wait()
         grad = grad + mm(pieces[i][...].reshape(2 * TOK, 256), w_buf[groups[i]], NN)
     own_ref[...] = grad[:TOK]
-    send_ref[...] = grad[TOK:].astype(BF16)
+    send_ref[...] = grad[TOK:]
 
 
 def grad_normed_parts(place, weight, grad_parts):
@@ -183,7 +183,7 @@
         out_specs=(vmem(), vmem(), vmem()),
         out_shape=(
             jax.ShapeDtypeStruct((TOK, WIDTH), F32),
-            jax.ShapeDtypeStruct((TOK, WIDTH), BF16),
+            jax.ShapeDtypeStruct((TOK, WIDTH), F32),
             jax.ShapeDtypeStruct((8, 256, WIDTH), BF16),
         ),
         scratch_shapes=[pltpu.SemaphoreType.DMA((8,))],
@@ -211,14 +211,14 @@
         out_shape=jax.ShapeDtypeStruct((8, 2, TOK, 256), BF16),
         scratch_shapes=[pltpu.VMEM((8, 2, TOK, 256), BF16), pltpu.SemaphoreType.DMA((8,))],
         compiler_params=small(),
-        cost_estimate=cost(2 * TOK * WIDTH * 4096, 4000000),
+        cost_estimate=cost(10000000000, 40000000),
         name="project",
     )(weight, own, other)
 
 
 def grad_attended_kernel(own_ref, got_ref, normed_ref, scale_ref, q_ref, ga_ref, state_ref):
     for h in range(HEADS_DEV):
-        grad_normed = own_ref[:, head(h)] + got_ref[:, head(h)].astype(F32)
+        grad_normed = own_ref[:, head(h)] + got_ref[:, head(h)]
         normed = normed_ref[:, head(h)]
         mean = jnp.mean(grad_normed * normed, axis=-1, keepdims=True)
         ga = (scale_ref[:, head(h)] * (grad_normed - normed * mean)).astype(BF16)
@@ -234,7 +234,7 @@
             jax.ShapeDtypeStruct((WIDTH, HEAD_DIM), BF16),
         ),
         compiler_params=small(),
-        cost_estimate=cost(2 * TOK * WIDTH * HEAD_DIM, 1200000),
+        cost_estimate=cost(30000000000, 100000000),
         name="grad_attended",
     )(own, got, normed, scale, queries)
 

time: 140 us -> 139 us (level)
  waiting for transfers between devices: 31.5 us -> 29.3 us
  blocking collectives: 21.2 us -> 23.1 us
    all_to_all x1, blocking collectives: 21.2 us -> 23.1 us  [carried(): pieces = lax.all_to_all(state.reshape(64, 8, HEAD_DIM), CTX, 0, 0)]
    ppermute x1, waiting for transfers between devices: 1.48 us -> 0.01 us  [local(): flat_other = lax.ppermute(flat, 'zl', SWAP)]
  transfers between devices with their start and end apart: 15 -> 15, of which waited for: 7 -> 6; matrix products, arithmetic and copies ran while one was open for 1% -> 1% of each run, Pallas kernels for 7% -> 8%
where the time goes in v4:
time: 139 us; the launch traced here: 138 us
  starting transfers between devices  55.9 us (40%)
  waiting for transfers between devices  29.3 us (21%)
  blocking collectives  23.1 us (17%)
  between operations  14.3 us (10%)
  Pallas kernels  12.2 us (9%)
  local copies, waits for them, and re-layouts  3.21 us (2%)
    all_to_all x1, blocking collectives, carried(): pieces = lax.all_to_all(state.reshape(64, 8, HEAD_DIM), CTX, 0, 0)  23.1 us
    all_to_all x2, waiting for transfers between devices, carried(): back = lax.all_to_all(sums.reshape(64, 8, HEAD_DIM), CTX, 0, 0)  13 us
    all_to_all x1, starting transfers between devices, local(): rows = lax.all_to_all(repeated(out_weight.T, 4), 'zh', 0, 0)  10.3 us
    all_to_all x2, starting transfers between devices, carried(): back = lax.all_to_all(sums.reshape(64, 8, HEAD_DIM), CTX, 0, 0)  9.99 us
    all_to_all x1, starting transfers between devices, carried(): pieces = lax.all_to_all(state.reshape(64, 8, HEAD_DIM), CTX, 0, 0)  9.9 us
    ppermute x3, starting transfers between devices, shifted(): return lax.ppermute(value, axis, [((i + step) % 4, i) for i in range(4)])  9.24 us
    all_to_all x1, waiting for transfers between devices, carried(): pieces = lax.all_to_all(state.reshape(64, 8, HEAD_DIM), CTX, 0, 0)  7.33 us
    ppermute x1, waiting for transfers between devices, local(): got = lax.ppermute(send, 'zl', SWAP)  3.49 us
  transfers between devices with their start and end apart: 15, of which 6 were waited for; matrix products, arithmetic and copies ran while one was open for 1% of the time, Pallas kernels for 8%

profile of v4, /device:TPU:6, one launch (start us, length us, event | category | flops | bytes accessed | tf_op | source)
XLA Modules:
  0.0 138.2 jit_solution(11890631359335991116)
XLA Ops:
  7.2 1.6 %broadcast_in_dim.3 = bf16[4,64,512]{2,1,0:T(8,128)(2,1)} broadcast(bf16[64,512]{1,0:T(8,128)(2,1)} %bitcast.31), dimensions={1,2} | broadcast | bytes 327680 | tf_op jit(solution)/shard_map/broadcast_in_dim | solution.py:297
  8.8 10.3 %all-to-all-start = ((bf16[4,64,512]{2,1,0:T(8,128)(2,1)}), bf16[4,64,512]{2,1,0:T(8,128)(2,1)S(1)}, u32[]{:S(2)}, u32[]{:S(2)}) async-start(bf16[4,64,512]{2,1,0:T(8,128)(2,1)} %broadcast_in_dim.3), calls=%async_computation | async-start | bytes 524288 | tf_op jit(solution)/shard_map/all_to_all | solution.py:306
  20.2 3.4 %collective-permute-start = (bf16[128,256]{1,0:T(8,128)(2,1)S(1)}, bf16[128,256]{1,0:T(8,128)(2,1)S(1)}, u32[]{:S(2)}, u32[]{:S(2)}) collective-permute-start(bf16[128,256]{1,0:T(8,128)(2,1)S(1)} %get-tuple-element.26), channel_id=1, source_target_pairs={{0,8},{8,0},{1,9},{9,1},{2,10},{10,2},{3,11},{11,3},{4,12},{12,4},... | collective-permute-start | bytes 196616 | tf_op jit(solution)/shard_map/ppermute | solution.py:308
  23.6 1.8 %local_state.1 = bf16[512,128]{1,0:T(8,128)(2,1)} custom-call(bf16[128,512]{1,0:T(8,128)(2,1)} %k_ref.7, bf16[128,512]{1,0:T(8,128)(2,1)} %v_ref.7), custom_call_target="tpu_custom_call" | custom-call | flops 16777216 | bytes 400000 | tf_op jit(solution)/shard_map/local_state/pallas_call | solution.py:74
  25.4 2.7 %collective-permute-done = bf16[128,256]{1,0:T(8,128)(2,1)S(1)} collective-permute-done((bf16[128,256]{1,0:T(8,128)(2,1)S(1)}, bf16[128,256]{1,0:T(8,128)(2,1)S(1)}, u32[]{:S(2)}, u32[]{:S(2)}) %collective-permute-start) | collective-permute-done | bytes 65568 | tf_op jit(solution)/shard_map/ppermute | solution.py:308
  28.2 2.7 %all-to-all-done = bf16[4,64,512]{2,1,0:T(8,128)(2,1)S(1)} async-done(((bf16[4,64,512]{2,1,0:T(8,128)(2,1)}), bf16[4,64,512]{2,1,0:T(8,128)(2,1)S(1)}, u32[]{:S(2)}, u32[]{:S(2)}) %all-to-all-start) | async-done | bytes 262176 | tf_op jit(solution)/shard_map/all_to_all | solution.py:306
  31.6 9.9 %all-to-all-start.1 = ((bf16[64,8,128]{2,1,0:T(8,128)(2,1)}), bf16[64,8,128]{2,1,0:T(8,128)(2,1)S(1)}, u32[]{:S(2)}, u32[]{:S(2)}) async-start(bf16[64,8,128]{2,1,0:T(8,128)(2,1)} %bitcast.9), calls=%async_computation.1 | async-start | bytes 262144 | tf_op jit(solution)/shard_map/all_to_all | solution.py:132
  41.5 1.9 %collective-permute-start.1 = (bf16[2,128,256]{2,1,0:T(8,128)(2,1)S(1)}, bf16[2,128,256]{2,1,0:T(8,128)(2,1)S(1)}, u32[]{:S(2)}, u32[]{:S(2)}) collective-permute-start(bf16[2,128,256]{2,1,0:T(8,128)(2,1)S(1)} %get-tuple-element.51), channel_id=1, source_target_pairs={{0,1},{1,0},{2,3},{3,2},{4,5},{5,4},{6,7},{7,6},{8,9},{9,8},{10,11... | collective-permute-start | bytes 393224 | tf_op jit(solution)/shard_map/ppermute | solution.py:314
  43.4 3.3 %collective-permute-start.4 = (bf16[2,128,256]{2,1,0:T(8,128)(2,1)S(1)}, bf16[2,128,256]{2,1,0:T(8,128)(2,1)S(1)}, u32[]{:S(2)}, u32[]{:S(2)}) collective-permute-start(bf16[2,128,256]{2,1,0:T(8,128)(2,1)S(1)} %get-tuple-element.51), channel_id=1, source_target_pairs={{4,0},{6,2},{0,4},{2,6},{5,1},{7,3},{1,5},{3,7},{12,8},{14,10},{8,... | collective-permute-start | bytes 393224 | tf_op jit(solution)/shard_map/ppermute | solution.py:301
  46.7 7.3 %all-to-all-done.1 = bf16[64,8,128]{2,1,0:T(8,128)(2,1)S(1)} async-done(((bf16[64,8,128]{2,1,0:T(8,128)(2,1)}), bf16[64,8,128]{2,1,0:T(8,128)(2,1)S(1)}, u32[]{:S(2)}, u32[]{:S(2)}) %all-to-all-start.1) | async-done | bytes 131104 | tf_op jit(solution)/shard_map/all_to_all | solution.py:132
  54.8 5.4 %all-to-all-start.2 = ((bf16[64,8,128]{2,1,0:T(8,128)(2,1)}), bf16[64,8,128]{2,1,0:T(8,128)(2,1)S(1)}, u32[]{:S(2)}, u32[]{:S(2)}) async-start(bf16[64,8,128]{2,1,0:T(8,128)(2,1)} %bitcast.11), calls=%async_computation.2 | async-start | bytes 262144 | tf_op jit(solution)/shard_map/all_to_all | solution.py:134
  60.3 4.0 %collective-permute-start.3 = (bf16[2,2,128,256]{3,2,1,0:T(8,128)(2,1)S(1)}, bf16[2,2,128,256]{3,2,1,0:T(8,128)(2,1)S(1)}, u32[]{:S(2)}, u32[]{:S(2)}) collective-permute-start(bf16[2,2,128,256]{3,2,1,0:T(8,128)(2,1)S(1)} %pad_maximum_fusion.go0_ref), channel_id=1, source_target_pairs={{6,0},{0,2},{2,4},{4,6},{7,1},{1,3},{3,5},{5,7},{14,8},{8,10},{10,... | collective-permute-start | bytes 786440 | tf_op jit(solution)/shard_map/ppermute | solution.py:301
  64.3 1.9 %collective-permute-start.2 = (bf16[2,2,128,256]{3,2,1,0:T(8,128)(2,1)S(1)}, bf16[2,2,128,256]{3,2,1,0:T(8,128)(2,1)S(1)}, u32[]{:S(2)}, u32[]{:S(2)}) collective-permute-start(bf16[2,2,128,256]{3,2,1,0:T(8,128)(2,1)S(1)} %pad_maximum_fusion.go0_ref), channel_id=1, source_target_pairs={{2,0},{4,2},{6,4},{0,6},{3,1},{5,3},{7,5},{1,7},{10,8},{12,10},{14... | collective-permute-start | bytes 786440 | tf_op jit(solution)/shard_map/ppermute | solution.py:301
  66.2 1.9 %collective-permute-start.5 = (bf16[2,128,256]{2,1,0:T(8,128)(2,1)S(1)}, bf16[2,128,256]{2,1,0:T(8,128)(2,1)S(1)}, u32[]{:S(2)}, u32[]{:S(2)}) collective-permute-start(bf16[2,128,256]{2,1,0:T(8,128)(2,1)S(1)} %collective-permute-done.4.go2_ref), channel_id=1, source_target_pairs={{0,1},{1,0},{2,3},{3,2},{4,5},{5,4},{6,7},{7,6},{8,9},{9,8},{10,11... | collective-permute-start | bytes 393224 | tf_op jit(solution)/shard_map/ppermute | solution.py:317
  68.2 6.0 %all-to-all-done.2 = bf16[64,8,128]{2,1,0:T(8,128)(2,1)S(1)} async-done(((bf16[64,8,128]{2,1,0:T(8,128)(2,1)}), bf16[64,8,128]{2,1,0:T(8,128)(2,1)S(1)}, u32[]{:S(2)}, u32[]{:S(2)}) %all-to-all-start.2) | async-done | bytes 131104 | tf_op jit(solution)/shard_map/all_to_all | solution.py:134
  74.7 2.7 %collective-permute-start.7 = (bf16[128,512]{1,0:T(8,128)(2,1)S(1)}, bf16[128,512]{1,0:T(8,128)(2,1)S(1)}, u32[]{:S(2)}, u32[]{:S(2)}) collective-permute-start(bf16[128,512]{1,0:T(8,128)(2,1)S(1)} %get-tuple-element.43.own_ref), channel_id=1, source_target_pairs={{0,8},{8,0},{1,9},{9,1},{2,10},{10,2},{3,11},{11,3},{4,12},{12,4},... | collective-permute-start | bytes 393224 | tf_op jit(solution)/shard_map/ppermute | solution.py:320
  77.4 2.6 %grad_normed.1 = (f32[128,512]{1,0:T(8,128)S(1)}, f32[128,512]{1,0:T(8,128)S(1)}, bf16[8,256,512]{2,1,0:T(8,128)(2,1)S(1)}) custom-call(s32[3]{0:T(128)S(1)} %pad_add_fusion.place_ref, bf16[8,256,512]{2,1,0:T(8,128)(2,1)} %bitcast.29, bf16[2,2,128,256]{3,2,1,0:T(8,128)(2,1)S(1)} %pad_maximum_fusion.go0_ref, ...), custom_call_target="tpu_custom_call" | custom-call | flops 536870912 | bytes 4000000 | tf_op jit(solution)/shard_map/grad_normed/pallas_call | solution.py:180
  80.0 3.2 %collective-permute-start.6 = (f32[128,512]{1,0:T(8,128)S(1)}, f32[128,512]{1,0:T(8,128)S(1)}, u32[]{:S(2)}, u32[]{:S(2)}) collective-permute-start(f32[128,512]{1,0:T(8,128)S(1)} %get-tuple-element.34), channel_id=1, source_target_pairs={{0,8},{8,0},{1,9},{9,1},{2,10},{10,2},{3,11},{11,3},{4,12},{12,4},... | collective-permute-start | bytes 786440 | tf_op jit(solution)/shard_map/ppermute | solution.py:323
  83.2 1.6 %project.1 = bf16[8,2,128,256]{3,2,1,0:T(8,128)(2,1)} custom-call(bf16[8,256,512]{2,1,0:T(8,128)(2,1)S(1)} %get-tuple-element.42.w_ref, bf16[128,512]{1,0:T(8,128)(2,1)S(1)} %get-tuple-element.43.own_ref, bf16[128,512]{1,0:T(8,128)(2,1)S(1)} %collective-permute-done.7.other_ref), custom_call_target="tpu_custom_call" | custom-call | flops 10000000000 | bytes 40000000 | tf_op jit(solution)/shard_map/project/pallas_call | solution.py:207
  84.8 3.5 %collective-permute-done.6.got_ref = f32[128,512]{1,0:T(8,128)S(1)} collective-permute-done((f32[128,512]{1,0:T(8,128)S(1)}, f32[128,512]{1,0:T(8,128)S(1)}, u32[]{:S(2)}, u32[]{:S(2)}) %collective-permute-start.6) | collective-permute-done | bytes 262176 | tf_op jit(solution)/shard_map/ppermute | solution.py:323
  88.6 23.1 %all_to_all.25 = bf16[64,8,128]{2,1,0:T(8,128)(2,1)S(1)} all-to-all(bf16[64,8,128]{2,1,0:T(8,128)(2,1)S(1)} %bitcast.27), channel_id=1, replica_groups=mesh['y'=8,'zh'=4,'zl'=2,'x'=4,'core'=2] {'y','zh','zl'}, dimensions={0} | all-to-all | bytes 262144 | tf_op jit(solution)/shard_map/all_to_all | solution.py:132
  112.4 4.6 %all-to-all-start.4 = ((bf16[64,8,128]{2,1,0:T(8,128)(2,1)}), bf16[64,8,128]{2,1,0:T(8,128)(2,1)S(1)}, u32[]{:S(2)}, u32[]{:S(2)}) async-start(bf16[64,8,128]{2,1,0:T(8,128)(2,1)} %bitcast.15), calls=%async_computation.4 | async-start | bytes 262144 | tf_op jit(solution)/shard_map/all_to_all | solution.py:134
  118.0 3.4 %collective-permute-start.8 = (bf16[128,256]{1,0:T(8,128)(2,1)S(1)}, bf16[128,256]{1,0:T(8,128)(2,1)S(1)}, u32[]{:S(2)}, u32[]{:S(2)}) collective-permute-start(bf16[128,256]{1,0:T(8,128)(2,1)S(1)} %get-tuple-element.48), channel_id=1, source_target_pairs={{0,8},{8,0},{1,9},{9,1},{2,10},{10,2},{3,11},{11,3},{4,12},{12,4},... | collective-permute-start | bytes 196616 | tf_op jit(solution)/shard_map/ppermute | solution.py:329
  122.8 7.1 %all-to-all-done.4 = bf16[64,8,128]{2,1,0:T(8,128)(2,1)S(1)} async-done(((bf16[64,8,128]{2,1,0:T(8,128)(2,1)}), bf16[64,8,128]{2,1,0:T(8,128)(2,1)S(1)}, u32[]{:S(2)}, u32[]{:S(2)}) %all-to-all-start.4) | async-done | bytes 131104 | tf_op jit(solution)/shard_map/all_to_all | solution.py:134
  (32 shorter events, 8.0 us)
Async XLA Ops:
  7.2 67.0 %copy-start.1 = (bf16[128,512]{1,0:T(8,128)(2,1)S(1)}, bf16[128,512]{1,0:T(8,128)(2,1)}, u32[]{:S(2)}) copy-start(bf16[128,512]{1,0:T(8,128)(2,1)} %v_ref.7) | copy-start | bytes 393220
  7.2 67.0 %copy-start = (bf16[128,512]{1,0:T(8,128)(2,1)S(1)}, bf16[128,512]{1,0:T(8,128)(2,1)}, u32[]{:S(2)}) copy-start(bf16[128,512]{1,0:T(8,128)(2,1)} %k_ref.7) | copy-start | bytes 393220
  7.2 67.0 %copy-start.2 = (bf16[128,512]{1,0:T(8,128)(2,1)S(1)}, bf16[128,512]{1,0:T(8,128)(2,1)}, u32[]{:S(2)}) copy-start(bf16[128,512]{1,0:T(8,128)(2,1)} %q_ref.5) | copy-start | bytes 393220
  8.8 22.0 %all-to-all-start = ((bf16[4,64,512]{2,1,0:T(8,128)(2,1)}), bf16[4,64,512]{2,1,0:T(8,128)(2,1)S(1)}, u32[]{:S(2)}, u32[]{:S(2)}) async-start(bf16[4,64,512]{2,1,0:T(8,128)(2,1)} %broadcast_in_dim.3), calls=%async_computation | async-start | bytes 524288 | tf_op jit(solution)/shard_map/all_to_all | solution.py:306
  19.1 58.3 %all-gather.3.cloned.1.call-start = ((), (), s32[]{:S(2)}) async-start(), calls=%async_computation.7 | async-start | bytes 2359296 | tf_op jit(solution)/shard_map/all_gather | solution.py:312
  20.2 7.9 %collective-permute-start = (bf16[128,256]{1,0:T(8,128)(2,1)S(1)}, bf16[128,256]{1,0:T(8,128)(2,1)S(1)}, u32[]{:S(2)}, u32[]{:S(2)}) collective-permute-start(bf16[128,256]{1,0:T(8,128)(2,1)S(1)} %get-tuple-element.26), channel_id=1, source_target_pairs={{0,8},{8,0},{1,9},{9,1},{2,10},{10,2},{3,11},{11,3},{4,12},{12,4},... | collective-permute-start | bytes 196616 | tf_op jit(solution)/shard_map/ppermute | solution.py:308
  30.8 0.7 copy-start.3
  31.6 22.5 %all-to-all-start.1 = ((bf16[64,8,128]{2,1,0:T(8,128)(2,1)}), bf16[64,8,128]{2,1,0:T(8,128)(2,1)S(1)}, u32[]{:S(2)}, u32[]{:S(2)}) async-start(bf16[64,8,128]{2,1,0:T(8,128)(2,1)} %bitcast.9), calls=%async_computation.1 | async-start | bytes 262144 | tf_op jit(solution)/shard_map/all_to_all | solution.py:132
  41.5 18.7 %collective-permute-start.1 = (bf16[2,128,256]{2,1,0:T(8,128)(2,1)S(1)}, bf16[2,128,256]{2,1,0:T(8,128)(2,1)S(1)}, u32[]{:S(2)}, u32[]{:S(2)}) collective-permute-start(bf16[2,128,256]{2,1,0:T(8,128)(2,1)S(1)} %get-tuple-element.51), channel_id=1, source_target_pairs={{0,1},{1,0},{2,3},{3,2},{4,5},{5,4},{6,7},{7,6},{8,9},{9,8},{10,11... | collective-permute-start | bytes 393224 | tf_op jit(solution)/shard_map/ppermute | solution.py:314
  43.4 22.8 %collective-permute-start.4 = (bf16[2,128,256]{2,1,0:T(8,128)(2,1)S(1)}, bf16[2,128,256]{2,1,0:T(8,128)(2,1)S(1)}, u32[]{:S(2)}, u32[]{:S(2)}) collective-permute-start(bf16[2,128,256]{2,1,0:T(8,128)(2,1)S(1)} %get-tuple-element.51), channel_id=1, source_target_pairs={{4,0},{6,2},{0,4},{2,6},{5,1},{7,3},{1,5},{3,7},{12,8},{14,10},{8,... | collective-permute-start | bytes 393224 | tf_op jit(solution)/shard_map/ppermute | solution.py:301
  54.8 19.3 %all-to-all-start.2 = ((bf16[64,8,128]{2,1,0:T(8,128)(2,1)}), bf16[64,8,128]{2,1,0:T(8,128)(2,1)S(1)}, u32[]{:S(2)}, u32[]{:S(2)}) async-start(bf16[64,8,128]{2,1,0:T(8,128)(2,1)} %bitcast.11), calls=%async_computation.2 | async-start | bytes 262144 | tf_op jit(solution)/shard_map/all_to_all | solution.py:134
  60.2 56.9 %reduce-scatter.2.cloned.1.call-start = ((), (), s32[]{:S(2)}) async-start(), calls=%async_computation.6 | async-start | bytes 1179648 | tf_op jit(solution)/shard_map/reduce_scatter | solution.py:325
  60.3 17.1 %collective-permute-start.3 = (bf16[2,2,128,256]{3,2,1,0:T(8,128)(2,1)S(1)}, bf16[2,2,128,256]{3,2,1,0:T(8,128)(2,1)S(1)}, u32[]{:S(2)}, u32[]{:S(2)}) collective-permute-start(bf16[2,2,128,256]{3,2,1,0:T(8,128)(2,1)S(1)} %pad_maximum_fusion.go0_ref), channel_id=1, source_target_pairs={{6,0},{0,2},{2,4},{4,6},{7,1},{1,3},{3,5},{5,7},{14,8},{8,10},{10,... | collective-permute-start | bytes 786440 | tf_op jit(solution)/shard_map/ppermute | solution.py:301
  64.3 13.1 %collective-permute-start.2 = (bf16[2,2,128,256]{3,2,1,0:T(8,128)(2,1)S(1)}, bf16[2,2,128,256]{3,2,1,0:T(8,128)(2,1)S(1)}, u32[]{:S(2)}, u32[]{:S(2)}) collective-permute-start(bf16[2,2,128,256]{3,2,1,0:T(8,128)(2,1)S(1)} %pad_maximum_fusion.go0_ref), channel_id=1, source_target_pairs={{2,0},{4,2},{6,4},{0,6},{3,1},{5,3},{7,5},{1,7},{10,8},{12,10},{14... | collective-permute-start | bytes 786440 | tf_op jit(solution)/shard_map/ppermute | solution.py:301
  66.2 11.1 %collective-permute-start.5 = (bf16[2,128,256]{2,1,0:T(8,128)(2,1)S(1)}, bf16[2,128,256]{2,1,0:T(8,128)(2,1)S(1)}, u32[]{:S(2)}, u32[]{:S(2)}) collective-permute-start(bf16[2,128,256]{2,1,0:T(8,128)(2,1)S(1)} %collective-permute-done.4.go2_ref), channel_id=1, source_target_pairs={{0,1},{1,0},{2,3},{3,2},{4,5},{5,4},{6,7},{7,6},{8,9},{9,8},{10,11... | collective-permute-start | bytes 393224 | tf_op jit(solution)/shard_map/ppermute | solution.py:317
  74.7 8.6 %collective-permute-start.7 = (bf16[128,512]{1,0:T(8,128)(2,1)S(1)}, bf16[128,512]{1,0:T(8,128)(2,1)S(1)}, u32[]{:S(2)}, u32[]{:S(2)}) collective-permute-start(bf16[128,512]{1,0:T(8,128)(2,1)S(1)} %get-tuple-element.43.own_ref), channel_id=1, source_target_pairs={{0,8},{8,0},{1,9},{9,1},{2,10},{10,2},{3,11},{11,3},{4,12},{12,4},... | collective-permute-start | bytes 393224 | tf_op jit(solution)/shard_map/ppermute | solution.py:320
  80.0 8.3 %collective-permute-start.6 = (f32[128,512]{1,0:T(8,128)S(1)}, f32[128,512]{1,0:T(8,128)S(1)}, u32[]{:S(2)}, u32[]{:S(2)}) collective-permute-start(f32[128,512]{1,0:T(8,128)S(1)} %get-tuple-element.34), channel_id=1, source_target_pairs={{0,8},{8,0},{1,9},{9,1},{2,10},{10,2},{3,11},{11,3},{4,12},{12,4},... | collective-permute-start | bytes 786440 | tf_op jit(solution)/shard_map/ppermute | solution.py:323
  112.4 17.4 %all-to-all-start.4 = ((bf16[64,8,128]{2,1,0:T(8,128)(2,1)}), bf16[64,8,128]{2,1,0:T(8,128)(2,1)S(1)}, u32[]{:S(2)}, u32[]{:S(2)}) async-start(bf16[64,8,128]{2,1,0:T(8,128)(2,1)} %bitcast.15), calls=%async_computation.4 | async-start | bytes 262144 | tf_op jit(solution)/shard_map/all_to_all | solution.py:134
  118.0 11.8 %collective-permute-start.8 = (bf16[128,256]{1,0:T(8,128)(2,1)S(1)}, bf16[128,256]{1,0:T(8,128)(2,1)S(1)}, u32[]{:S(2)}, u32[]{:S(2)}) collective-permute-start(bf16[128,256]{1,0:T(8,128)(2,1)S(1)} %get-tuple-element.48), channel_id=1, source_target_pairs={{0,8},{8,0},{1,9},{9,1},{2,10},{10,2},{3,11},{11,3},{4,12},{12,4},... | collective-permute-start | bytes 196616 | tf_op jit(solution)/shard_map/ppermute | solution.py:329
Sparse Core Ops, SparseCore 0:
  31.7 43.8 all-gather.2
  84.9 31.6 reduce-scatter.1

commit v5 on v4

--- a/solution.py
+++ b/solution.py
@@ -135,7 +135,7 @@
     return back.reshape(WIDTH, HEAD_DIM)
 
 
-def attend_kernel(q_ref, k_ref, v_ref, s_ref, flat_ref, normed_ref, scale_ref, p_ref):
+def attend_kernel(q_ref, k_ref, v_ref, s_ref, pair_ref, normed_ref, scale_ref, p_ref):
     keep = causal()
     for h in range(HEADS_DEV):
         q, k, v = q_ref[:, head(h)], k_ref[:, head(h)], v_ref[:, head(h)]
@@ -144,7 +144,8 @@
         attended = mm(weights, v, NN) + mm(q, s_ref[head(h), :], NN)
         scale = lax.rsqrt(jnp.mean(attended * attended, axis=-1, keepdims=True) + EPSILON)
         normed = attended * scale
-        flat_ref[:, head(h)] = normed.astype(BF16)
+        pair_ref[0, :, head(h)] = normed.astype(BF16)
+        pair_ref[1, :, head(h)] = (q.astype(F32) * scale).astype(BF16)
         normed_ref[:, head(h)] = normed
         scale_ref[:, head(h)] = jnp.broadcast_to(scale, (TOK, HEAD_DIM))
 
@@ -154,9 +155,9 @@
     wide = jax.ShapeDtypeStruct((TOK, WIDTH), F32)
     return pl.pallas_call(
         attend_kernel,
-        out_shape=(flat, wide, wide, flat),
+        out_shape=(jax.ShapeDtypeStruct((2, TOK, WIDTH), BF16), wide, wide, flat),
+        compiler_params=small(),
         cost_estimate=cost(6 * TOK * WIDTH * HEAD_DIM, 1500000),
-        compiler_params=small(),
         name="attend",
     )(queries, keys, values, before)
 
@@ -195,7 +196,7 @@
 
 def project_kernel(w_ref, own_ref, other_ref, part_ref, out_buf, out_sem):
     stores = [pltpu.make_async_copy(out_buf.at[g], part_ref.at[g], out_sem.at[g]) for g in range(8)]
-    normed = jnp.concatenate([own_ref[...], other_ref[...]], axis=0)
+    normed = jnp.concatenate([own_ref[0], other_ref[0]], axis=0)
     for g in range(8):
         out_buf[g] = mm(normed, w_ref[g], NT).astype(BF16).reshape(2, TOK, 256)
         stores[g].start()
@@ -211,54 +212,83 @@
         out_shape=jax.ShapeDtypeStruct((8, 2, TOK, 256), BF16),
         scratch_shapes=[pltpu.VMEM((8, 2, TOK, 256), BF16), pltpu.SemaphoreType.DMA((8,))],
         compiler_params=small(),
-        cost_estimate=cost(10000000000, 40000000),
+        cost_estimate=cost(2 * TOK * WIDTH * 4096, 4000000),
         name="project",
     )(weight, own, other)
 
 
-def grad_attended_kernel(own_ref, got_ref, normed_ref, scale_ref, q_ref, ga_ref, state_ref):
+def grad_states_kernel(own_ref, send_ref, normed_ref, scale_ref, q_ref, other_ref, out_ref):
+    terms = [], []
+    for h in range(HEADS_DEV):
+        part, normed = own_ref[:, head(h)], normed_ref[:, head(h)]
+        mean = jnp.mean(part * normed, axis=-1, keepdims=True)
+        part = (scale_ref[:, head(h)] * (part - normed * mean)).astype(BF16)
+        terms[0].append(mm(q_ref[:, head(h)], part, TN))
+        part, normed = send_ref[:, head(h)], other_ref[0, :, head(h)].astype(F32)
+        mean = jnp.mean(part * normed, axis=-1, keepdims=True)
+        part = (part - normed * mean).astype(BF16)
+        terms[1].append(mm(other_ref[1, :, head(h)], part, TN))
+    own, other = [jnp.concatenate(term, axis=0).reshape(64, 8, HEAD_DIM) for term in terms]
+    out_ref[...] = jnp.concatenate([own, other], axis=1).astype(BF16)
+
+
+def grad_states(own, send, normed, scale, queries, other):
+    return pl.pallas_call(
+        grad_states_kernel,
+        out_shape=jax.ShapeDtypeStruct((64, 16, HEAD_DIM), BF16),
+        compiler_params=small(),
+        cost_estimate=cost(4 * TOK * WIDTH * HEAD_DIM, 1500000),
+        name="grad_states",
+    )(own, send, normed, scale, queries, other)
+
+
+def scan_pairs_kernel(in_ref, out_ref):
+    total = jnp.zeros((8, HEAD_DIM), F32)
+    for i in range(in_ref.shape[0] // 32 - 1, -1, -1):
+        even = in_ref[32 * i : 32 * i + 16, :].astype(F32)
+        odd = in_ref[32 * i + 16 : 32 * i + 32, :].astype(F32)
+        then = total + (odd[:8] + even[8:])
+        out_ref[16 * i : 16 * i + 16, :] = jnp.concatenate([then, total], axis=0).astype(BF16)
+        total = then + (even[:8] + odd[8:])
+
+
+def later_states(states):
+    pieces = lax.all_to_all(states, CTX, 0, 0)
+    sums = pl.pallas_call(
+        scan_pairs_kernel,
+        out_shape=jax.ShapeDtypeStruct((WIDTH, HEAD_DIM), BF16),
+        compiler_params=small(),
+        cost_estimate=cost(2 * WIDTH * HEAD_DIM, 500000),
+        name="scan_pairs",
+    )(pieces.reshape(2 * WIDTH, HEAD_DIM))
+    back = lax.all_to_all(sums.reshape(64, 8, HEAD_DIM), CTX, 0, 0)
+    return back.reshape(WIDTH, HEAD_DIM)
+
+
+def grads_block_kernel(q_ref, k_ref, v_ref, p_ref, own_ref, got_ref, normed_ref, scale_ref, s_ref, gq_ref, gk_ref, gv_ref):
+    keep = causal()
     for h in range(HEADS_DEV):
         grad_normed = own_ref[:, head(h)] + got_ref[:, head(h)]
         normed = normed_ref[:, head(h)]
         mean = jnp.mean(grad_normed * normed, axis=-1, keepdims=True)
         ga = (scale_ref[:, head(h)] * (grad_normed - normed * mean)).astype(BF16)
-        ga_ref[:, head(h)] = ga
-        state_ref[head(h), :] = mm(q_ref[:, head(h)], ga, TN).astype(BF16)
-
-
-def grad_attended(own, got, normed, scale, queries):
-    return pl.pallas_call(
-        grad_attended_kernel,
-        out_shape=(
-            jax.ShapeDtypeStruct((TOK, WIDTH), BF16),
-            jax.ShapeDtypeStruct((WIDTH, HEAD_DIM), BF16),
-        ),
-        compiler_params=small(),
-        cost_estimate=cost(30000000000, 100000000),
-        name="grad_attended",
-    )(own, got, normed, scale, queries)
-
-
-def grads_block_kernel(q_ref, k_ref, v_ref, p_ref, ga_ref, s_ref, gq_ref, gk_ref, gv_ref):
-    keep = causal()
-    for h in range(HEADS_DEV):
-        q, k, v, ga = q_ref[:, head(h)], k_ref[:, head(h)], v_ref[:, head(h)], ga_ref[:, head(h)]
+        q, k, v = q_ref[:, head(h)], k_ref[:, head(h)], v_ref[:, head(h)]
         scores = jnp.where(keep, mm(ga, v, NT), 0.0).astype(BF16)
         gq_ref[:, head(h)] = (mm(scores, k, NN) + mm(ga, s_ref[head(h), :], NT)).astype(BF16)
         gk_ref[:, head(h)] = mm(scores, q, TN)
         gv_ref[:, head(h)] = mm(p_ref[:, head(h)], ga, TN)
 
 
-def grads_block(queries, keys, values, weights, ga, before):
+def grads_block(queries, keys, values, weights, own, got, normed, scale, before):
     flat = jax.ShapeDtypeStruct((TOK, WIDTH), BF16)
     wide = jax.ShapeDtypeStruct((TOK, WIDTH), F32)
     return pl.pallas_call(
         grads_block_kernel,
         out_shape=(flat, wide, wide),
         compiler_params=small(),
-        cost_estimate=cost(10 * TOK * WIDTH * HEAD_DIM, 1500000),
+        cost_estimate=cost(10 * TOK * WIDTH * HEAD_DIM, 2500000),
         name="grads_block",
-    )(queries, keys, values, weights, ga, before)
+    )(queries, keys, values, weights, own, got, normed, scale, before)
 
 
 def finish_kernel(place_ref, k_ref, v_ref, g_ref, gk_in_ref, gv_in_ref, keep_ref, got_ref, mixed_ref, gk_ref, gv_ref):
@@ -316,16 +346,16 @@
     grad_parts = [grad_cores] + [shifted(grad_cores, "x", r) for r in (1, 3)]
     grad_parts += [grad_far, lax.ppermute(grad_far, "core", SWAP)]
     before = carried(state, False)
-    flat, normed, scale, weights = attend(queries, keys, values, before)
-    flat_other = lax.ppermute(flat, "zl", SWAP)
+    pair, normed, scale, weights = attend(queries, keys, values, before)
+    other = lax.ppermute(pair, "zl", SWAP)
     own, send, weight = grad_normed_parts(place, weight, grad_parts)
-    flat, send = tied(flat, send)
+    parts = project(weight, pair, other)
+    mixed_pair = lax.psum_scatter(parts, ("x", "core"), scatter_dimension=0, tiled=False)
+    after = later_states(grad_states(own, send, normed, scale, queries, other))
     got = lax.ppermute(send, "zl", SWAP)
-    parts = project(weight, flat, flat_other)
-    mixed_pair = lax.psum_scatter(parts, ("x", "core"), scatter_dimension=0, tiled=False)
-    ga, grad_state = grad_attended(own, got, normed, scale, queries)
-    after = carried(grad_state, True)
-    grad_query, grad_key, grad_value = grads_block(queries, keys, values, weights, ga, before)
+    grad_query, grad_key, grad_value = grads_block(
+        queries, keys, values, weights, own, got, normed, scale, before
+    )
     mixed_got = lax.ppermute(mixed_pair[1], "zl", SWAP)
     mixed, grad_key, grad_value = finish(
         place, keys, values, after, grad_key, grad_value, mixed_pair[0], mixed_got

time: 139 us -> 138 us (level); the launches traced: 138 us -> 135 us
  blocking collectives: 23.1 us -> 0 us
  starting transfers between devices: 55.9 us -> 66.1 us
  waiting for transfers between devices: 29.3 us -> 38.2 us
    all_to_all x1 -> x0, blocking collectives: 23.1 us -> none  [carried(): pieces = lax.all_to_all(state.reshape(64, 8, HEAD_DIM), CTX, 0, 0)]
    all_to_all x0 -> x2, waiting for transfers between devices: none -> 15.8 us  [the longest x1 10.7 us: later_states(): pieces = lax.all_to_all(states, CTX, 0, 0)]
    all_to_all x0 -> x2, starting transfers between devices: none -> 15 us  [the longest x1 10.4 us: later_states(): pieces = lax.all_to_all(states, CTX, 0, 0)]
    all_to_all x2 -> x1, waiting for transfers between devices: 13 us -> 3.31 us  [carried(): back = lax.all_to_all(sums.reshape(64, 8, HEAD_DIM), CTX, 0, 0)]
    all_to_all x2 -> x1, starting transfers between devices: 9.99 us -> 4.62 us  [carried(): back = lax.all_to_all(sums.reshape(64, 8, HEAD_DIM), CTX, 0, 0)]
    ppermute x1, waiting for transfers between devices: 3.49 us -> 0.01 us  [local(): got = lax.ppermute(send, 'zl', SWAP)]
    all_to_all x1, waiting for transfers between devices: 7.33 us -> 10.7 us  [carried(): pieces = lax.all_to_all(state.reshape(64, 8, HEAD_DIM), CTX, 0, 0)]
    reduce_scatter x1, waiting for transfers between devices: 0.02 us -> 1.62 us  [local(): lax.psum_scatter(parts, ('x', 'core'), scatter_dimension=0, tiled=False)]
  transfers between devices with their start and end apart: 15 -> 16, of which waited for: 6 -> 8; matrix products, arithmetic and copies ran while one was open for 1% -> 1% of each run, Pallas kernels for 8% -> 7%
where the time goes in v5:
time: 138 us; the launch traced here: 135 us
  starting transfers between devices  66.1 us (48%)
  waiting for transfers between devices  38.2 us (28%)
  between operations  14.3 us (10%)
  Pallas kernels  13.1 us (9%)
  local copies, waits for them, and re-layouts  3.2 us (2%)
    all_to_all x1, waiting for transfers between devices, later_states(): pieces = lax.all_to_all(states, CTX, 0, 0)  10.7 us
    all_to_all x1, waiting for transfers between devices, carried(): pieces = lax.all_to_all(state.reshape(64, 8, HEAD_DIM), CTX, 0, 0)  10.7 us
    all_to_all x1, starting transfers between devices, later_states(): pieces = lax.all_to_all(states, CTX, 0, 0)  10.4 us
    all_to_all x1, starting transfers between devices, local(): rows = lax.all_to_all(repeated(out_weight.T, 4), 'zh', 0, 0)  10.3 us
    all_to_all x1, starting transfers between devices, carried(): pieces = lax.all_to_all(state.reshape(64, 8, HEAD_DIM), CTX, 0, 0)  9.9 us
    ppermute x3, starting transfers between devices, shifted(): return lax.ppermute(value, axis, [((i + step) % 4, i) for i in range(4)])  9.24 us
    all_to_all x1, waiting for transfers between devices, later_states(): back = lax.all_to_all(sums.reshape(64, 8, HEAD_DIM), CTX, 0, 0)  5.09 us
    all_to_all x1, starting transfers between devices, later_states(): back = lax.all_to_all(sums.reshape(64, 8, HEAD_DIM), CTX, 0, 0)  4.62 us
  transfers between devices with their start and end apart: 16, of which 8 were waited for; matrix products, arithmetic and copies ran while one was open for 1% of the time, Pallas kernels for 7%

profile of v5, /device:TPU:6, one launch (start us, length us, event | category | flops | bytes accessed | tf_op | source)
XLA Modules:
  0.0 135.0 jit_solution(4249273442739384721)
XLA Ops:
  7.2 1.6 %broadcast_in_dim.3 = bf16[4,64,512]{2,1,0:T(8,128)(2,1)} broadcast(bf16[64,512]{1,0:T(8,128)(2,1)} %bitcast.29), dimensions={1,2} | broadcast | bytes 327680 | tf_op jit(solution)/shard_map/broadcast_in_dim | solution.py:327
  8.8 10.3 %all-to-all-start = ((bf16[4,64,512]{2,1,0:T(8,128)(2,1)}), bf16[4,64,512]{2,1,0:T(8,128)(2,1)S(1)}, u32[]{:S(2)}, u32[]{:S(2)}) async-start(bf16[4,64,512]{2,1,0:T(8,128)(2,1)} %broadcast_in_dim.3), calls=%async_computation | async-start | bytes 524288 | tf_op jit(solution)/shard_map/all_to_all | solution.py:336
  20.2 3.4 %collective-permute-start = (bf16[128,256]{1,0:T(8,128)(2,1)S(1)}, bf16[128,256]{1,0:T(8,128)(2,1)S(1)}, u32[]{:S(2)}, u32[]{:S(2)}) collective-permute-start(bf16[128,256]{1,0:T(8,128)(2,1)S(1)} %get-tuple-element.22), channel_id=1, source_target_pairs={{0,8},{8,0},{1,9},{9,1},{2,10},{10,2},{3,11},{11,3},{4,12},{12,4},... | collective-permute-start | bytes 196616 | tf_op jit(solution)/shard_map/ppermute | solution.py:338
  23.6 1.8 %local_state.1 = bf16[512,128]{1,0:T(8,128)(2,1)} custom-call(bf16[128,512]{1,0:T(8,128)(2,1)} %k_ref.7, bf16[128,512]{1,0:T(8,128)(2,1)} %v_ref.7), custom_call_target="tpu_custom_call" | custom-call | flops 16777216 | bytes 400000 | tf_op jit(solution)/shard_map/local_state/pallas_call | solution.py:74
  25.4 2.7 %collective-permute-done = bf16[128,256]{1,0:T(8,128)(2,1)S(1)} collective-permute-done((bf16[128,256]{1,0:T(8,128)(2,1)S(1)}, bf16[128,256]{1,0:T(8,128)(2,1)S(1)}, u32[]{:S(2)}, u32[]{:S(2)}) %collective-permute-start) | collective-permute-done | bytes 65568 | tf_op jit(solution)/shard_map/ppermute | solution.py:338
  28.1 2.7 %all-to-all-done = bf16[4,64,512]{2,1,0:T(8,128)(2,1)S(1)} async-done(((bf16[4,64,512]{2,1,0:T(8,128)(2,1)}), bf16[4,64,512]{2,1,0:T(8,128)(2,1)S(1)}, u32[]{:S(2)}, u32[]{:S(2)}) %all-to-all-start) | async-done | bytes 262176 | tf_op jit(solution)/shard_map/all_to_all | solution.py:336
  31.5 9.9 %all-to-all-start.1 = ((bf16[64,8,128]{2,1,0:T(8,128)(2,1)}), bf16[64,8,128]{2,1,0:T(8,128)(2,1)S(1)}, u32[]{:S(2)}, u32[]{:S(2)}) async-start(bf16[64,8,128]{2,1,0:T(8,128)(2,1)} %bitcast.9), calls=%async_computation.1 | async-start | bytes 262144 | tf_op jit(solution)/shard_map/all_to_all | solution.py:132
  41.5 1.9 %collective-permute-start.1 = (bf16[2,128,256]{2,1,0:T(8,128)(2,1)S(1)}, bf16[2,128,256]{2,1,0:T(8,128)(2,1)S(1)}, u32[]{:S(2)}, u32[]{:S(2)}) collective-permute-start(bf16[2,128,256]{2,1,0:T(8,128)(2,1)S(1)} %get-tuple-element.43), channel_id=1, source_target_pairs={{0,1},{1,0},{2,3},{3,2},{4,5},{5,4},{6,7},{7,6},{8,9},{9,8},{10,11... | collective-permute-start | bytes 393224 | tf_op jit(solution)/shard_map/ppermute | solution.py:344
  43.4 10.7 %all-to-all-done.1 = bf16[64,8,128]{2,1,0:T(8,128)(2,1)S(1)} async-done(((bf16[64,8,128]{2,1,0:T(8,128)(2,1)}), bf16[64,8,128]{2,1,0:T(8,128)(2,1)S(1)}, u32[]{:S(2)}, u32[]{:S(2)}) %all-to-all-start.1) | async-done | bytes 131104 | tf_op jit(solution)/shard_map/all_to_all | solution.py:132
  54.8 4.6 %all-to-all-start.2 = ((bf16[64,8,128]{2,1,0:T(8,128)(2,1)}), bf16[64,8,128]{2,1,0:T(8,128)(2,1)S(1)}, u32[]{:S(2)}, u32[]{:S(2)}) async-start(bf16[64,8,128]{2,1,0:T(8,128)(2,1)} %bitcast.11), calls=%async_computation.2 | async-start | bytes 262144 | tf_op jit(solution)/shard_map/all_to_all | solution.py:134
  59.5 3.3 %collective-permute-start.4 = (bf16[2,128,256]{2,1,0:T(8,128)(2,1)S(1)}, bf16[2,128,256]{2,1,0:T(8,128)(2,1)S(1)}, u32[]{:S(2)}, u32[]{:S(2)}) collective-permute-start(bf16[2,128,256]{2,1,0:T(8,128)(2,1)S(1)} %get-tuple-element.43), channel_id=1, source_target_pairs={{4,0},{6,2},{0,4},{2,6},{5,1},{7,3},{1,5},{3,7},{12,8},{14,10},{8,... | collective-permute-start | bytes 393224 | tf_op jit(solution)/shard_map/ppermute | solution.py:331
  62.8 4.0 %collective-permute-start.3 = (bf16[2,2,128,256]{3,2,1,0:T(8,128)(2,1)S(1)}, bf16[2,2,128,256]{3,2,1,0:T(8,128)(2,1)S(1)}, u32[]{:S(2)}, u32[]{:S(2)}) collective-permute-start(bf16[2,2,128,256]{3,2,1,0:T(8,128)(2,1)S(1)} %pad_maximum_fusion.go0_ref), channel_id=1, source_target_pairs={{6,0},{0,2},{2,4},{4,6},{7,1},{1,3},{3,5},{5,7},{14,8},{8,10},{10,... | collective-permute-start | bytes 786440 | tf_op jit(solution)/shard_map/ppermute | solution.py:331
  66.8 1.9 %collective-permute-start.2 = (bf16[2,2,128,256]{3,2,1,0:T(8,128)(2,1)S(1)}, bf16[2,2,128,256]{3,2,1,0:T(8,128)(2,1)S(1)}, u32[]{:S(2)}, u32[]{:S(2)}) collective-permute-start(bf16[2,2,128,256]{3,2,1,0:T(8,128)(2,1)S(1)} %pad_maximum_fusion.go0_ref), channel_id=1, source_target_pairs={{2,0},{4,2},{6,4},{0,6},{3,1},{5,3},{7,5},{1,7},{10,8},{12,10},{14... | collective-permute-start | bytes 786440 | tf_op jit(solution)/shard_map/ppermute | solution.py:331
  68.8 3.3 %all-to-all-done.2 = bf16[64,8,128]{2,1,0:T(8,128)(2,1)S(1)} async-done(((bf16[64,8,128]{2,1,0:T(8,128)(2,1)}), bf16[64,8,128]{2,1,0:T(8,128)(2,1)S(1)}, u32[]{:S(2)}, u32[]{:S(2)}) %all-to-all-start.2) | async-done | bytes 131104 | tf_op jit(solution)/shard_map/all_to_all | solution.py:134
  72.6 2.7 %collective-permute-start.6 = (bf16[2,128,512]{2,1,0:T(8,128)(2,1)S(1)}, bf16[2,128,512]{2,1,0:T(8,128)(2,1)S(1)}, u32[]{:S(2)}, u32[]{:S(2)}) collective-permute-start(bf16[2,128,512]{2,1,0:T(8,128)(2,1)S(1)} %get-tuple-element.31.own_ref), channel_id=1, source_target_pairs={{0,8},{8,0},{1,9},{9,1},{2,10},{10,2},{3,11},{11,3},{4,12},{12,4},... | collective-permute-start | bytes 786440 | tf_op jit(solution)/shard_map/ppermute | solution.py:350
  75.4 1.9 %collective-permute-start.5 = (bf16[2,128,256]{2,1,0:T(8,128)(2,1)S(1)}, bf16[2,128,256]{2,1,0:T(8,128)(2,1)S(1)}, u32[]{:S(2)}, u32[]{:S(2)}) collective-permute-start(bf16[2,128,256]{2,1,0:T(8,128)(2,1)S(1)} %collective-permute-done.4.go2_ref), channel_id=1, source_target_pairs={{0,1},{1,0},{2,3},{3,2},{4,5},{5,4},{6,7},{7,6},{8,9},{9,8},{10,11... | collective-permute-start | bytes 393224 | tf_op jit(solution)/shard_map/ppermute | solution.py:347
  78.6 2.6 %grad_normed.1 = (f32[128,512]{1,0:T(8,128)S(1)}, f32[128,512]{1,0:T(8,128)S(1)}, bf16[8,256,512]{2,1,0:T(8,128)(2,1)S(1)}) custom-call(s32[3]{0:T(128)S(1)} %pad_add_fusion.place_ref, bf16[8,256,512]{2,1,0:T(8,128)(2,1)} %bitcast.27, bf16[2,2,128,256]{3,2,1,0:T(8,128)(2,1)S(1)} %pad_maximum_fusion.go0_ref, ...), custom_call_target="tpu_custom_call" | custom-call | flops 536870912 | bytes 4000000 | tf_op jit(solution)/shard_map/grad_normed/pallas_call | solution.py:181
  84.0 10.4 %all-to-all-start.3 = ((bf16[64,16,128]{2,1,0:T(8,128)(2,1)}), bf16[64,16,128]{2,1,0:T(8,128)(2,1)S(1)}, u32[]{:S(2)}, u32[]{:S(2)}) async-start(bf16[64,16,128]{2,1,0:T(8,128)(2,1)} %grad_states.1), calls=%async_computation.3 | async-start | bytes 524288 | tf_op jit(solution)/shard_map/all_to_all | solution.py:256
  94.4 3.5 %collective-permute-start.7 = (f32[128,512]{1,0:T(8,128)S(1)}, f32[128,512]{1,0:T(8,128)S(1)}, u32[]{:S(2)}, u32[]{:S(2)}) collective-permute-start(f32[128,512]{1,0:T(8,128)S(1)} %get-tuple-element.27.send_ref), channel_id=1, source_target_pairs={{0,8},{8,0},{1,9},{9,1},{2,10},{10,2},{3,11},{11,3},{4,12},{12,4},... | collective-permute-start | bytes 786440 | tf_op jit(solution)/shard_map/ppermute | solution.py:355
  97.9 10.7 %all-to-all-done.3 = bf16[64,16,128]{2,1,0:T(8,128)(2,1)S(1)} async-done(((bf16[64,16,128]{2,1,0:T(8,128)(2,1)}), bf16[64,16,128]{2,1,0:T(8,128)(2,1)S(1)}, u32[]{:S(2)}, u32[]{:S(2)}) %all-to-all-start.3) | async-done | bytes 262176 | tf_op jit(solution)/shard_map/all_to_all | solution.py:256
  109.3 4.6 %all-to-all-start.4 = ((bf16[64,8,128]{2,1,0:T(8,128)(2,1)}), bf16[64,8,128]{2,1,0:T(8,128)(2,1)S(1)}, u32[]{:S(2)}, u32[]{:S(2)}) async-start(bf16[64,8,128]{2,1,0:T(8,128)(2,1)} %bitcast.14), calls=%async_computation.4 | async-start | bytes 262144 | tf_op jit(solution)/shard_map/all_to_all | solution.py:264
  114.0 1.6 %reduce-scatter.2.cloned.1.call-done = bf16[1,2,128,256]{3,2,1,0:T(8,128)(2,1)} async-done(((bf16[8,2,128,256]{3,2,1,0:T(8,128)(2,1)}), bf16[1,2,128,256]{3,2,1,0:T(8,128)(2,1)}) %reduce-scatter.2.cloned.1.call-update) | async-done | bytes 131088 | tf_op jit(solution)/shard_map/reduce_scatter | solution.py:353
  116.5 3.6 %collective-permute-start.8 = (bf16[128,256]{1,0:T(8,128)(2,1)S(1)}, bf16[128,256]{1,0:T(8,128)(2,1)S(1)}, u32[]{:S(2)}, u32[]{:S(2)}) collective-permute-start(bf16[128,256]{1,0:T(8,128)(2,1)S(1)} %get-tuple-element.40), channel_id=1, source_target_pairs={{0,8},{8,0},{1,9},{9,1},{2,10},{10,2},{3,11},{11,3},{4,12},{12,4},... | collective-permute-start | bytes 196616 | tf_op jit(solution)/shard_map/ppermute | solution.py:359
  121.5 5.1 %all-to-all-done.4 = bf16[64,8,128]{2,1,0:T(8,128)(2,1)S(1)} async-done(((bf16[64,8,128]{2,1,0:T(8,128)(2,1)}), bf16[64,8,128]{2,1,0:T(8,128)(2,1)S(1)}, u32[]{:S(2)}, u32[]{:S(2)}) %all-to-all-start.4) | async-done | bytes 131104 | tf_op jit(solution)/shard_map/all_to_all | solution.py:264
  (33 shorter events, 11.8 us)
Async XLA Ops:
  7.2 64.9 %copy-start.1 = (bf16[128,512]{1,0:T(8,128)(2,1)S(1)}, bf16[128,512]{1,0:T(8,128)(2,1)}, u32[]{:S(2)}) copy-start(bf16[128,512]{1,0:T(8,128)(2,1)} %v_ref.7) | copy-start | bytes 393220
  7.2 64.9 %copy-start = (bf16[128,512]{1,0:T(8,128)(2,1)S(1)}, bf16[128,512]{1,0:T(8,128)(2,1)}, u32[]{:S(2)}) copy-start(bf16[128,512]{1,0:T(8,128)(2,1)} %k_ref.7) | copy-start | bytes 393220
  7.2 64.9 %copy-start.2 = (bf16[128,512]{1,0:T(8,128)(2,1)S(1)}, bf16[128,512]{1,0:T(8,128)(2,1)}, u32[]{:S(2)}) copy-start(bf16[128,512]{1,0:T(8,128)(2,1)} %q_ref.5) | copy-start | bytes 393220
  8.8 22.0 %all-to-all-start = ((bf16[4,64,512]{2,1,0:T(8,128)(2,1)}), bf16[4,64,512]{2,1,0:T(8,128)(2,1)S(1)}, u32[]{:S(2)}, u32[]{:S(2)}) async-start(bf16[4,64,512]{2,1,0:T(8,128)(2,1)} %broadcast_in_dim.3), calls=%async_computation | async-start | bytes 524288 | tf_op jit(solution)/shard_map/all_to_all | solution.py:336
  19.1 59.5 %all-gather.3.cloned.1.call-start = ((), (), s32[]{:S(2)}) async-start(), calls=%async_computation.7 | async-start | bytes 2359296 | tf_op jit(solution)/shard_map/all_gather | solution.py:342
  20.2 7.9 %collective-permute-start = (bf16[128,256]{1,0:T(8,128)(2,1)S(1)}, bf16[128,256]{1,0:T(8,128)(2,1)S(1)}, u32[]{:S(2)}, u32[]{:S(2)}) collective-permute-start(bf16[128,256]{1,0:T(8,128)(2,1)S(1)} %get-tuple-element.22), channel_id=1, source_target_pairs={{0,8},{8,0},{1,9},{9,1},{2,10},{10,2},{3,11},{11,3},{4,12},{12,4},... | collective-permute-start | bytes 196616 | tf_op jit(solution)/shard_map/ppermute | solution.py:338
  30.8 0.7 copy-start.3
  31.5 22.5 %all-to-all-start.1 = ((bf16[64,8,128]{2,1,0:T(8,128)(2,1)}), bf16[64,8,128]{2,1,0:T(8,128)(2,1)S(1)}, u32[]{:S(2)}, u32[]{:S(2)}) async-start(bf16[64,8,128]{2,1,0:T(8,128)(2,1)} %bitcast.9), calls=%async_computation.1 | async-start | bytes 262144 | tf_op jit(solution)/shard_map/all_to_all | solution.py:132
  41.5 21.3 %collective-permute-start.1 = (bf16[2,128,256]{2,1,0:T(8,128)(2,1)S(1)}, bf16[2,128,256]{2,1,0:T(8,128)(2,1)S(1)}, u32[]{:S(2)}, u32[]{:S(2)}) collective-permute-start(bf16[2,128,256]{2,1,0:T(8,128)(2,1)S(1)} %get-tuple-element.43), channel_id=1, source_target_pairs={{0,1},{1,0},{2,3},{3,2},{4,5},{5,4},{6,7},{7,6},{8,9},{9,8},{10,11... | collective-permute-start | bytes 393224 | tf_op jit(solution)/shard_map/ppermute | solution.py:344
  54.8 17.3 %all-to-all-start.2 = ((bf16[64,8,128]{2,1,0:T(8,128)(2,1)}), bf16[64,8,128]{2,1,0:T(8,128)(2,1)S(1)}, u32[]{:S(2)}, u32[]{:S(2)}) async-start(bf16[64,8,128]{2,1,0:T(8,128)(2,1)} %bitcast.11), calls=%async_computation.2 | async-start | bytes 262144 | tf_op jit(solution)/shard_map/all_to_all | solution.py:134
  59.4 56.2 %reduce-scatter.2.cloned.1.call-start = ((), (), s32[]{:S(2)}) async-start(), calls=%async_computation.6 | async-start | bytes 1179648 | tf_op jit(solution)/shard_map/reduce_scatter | solution.py:353
  59.5 15.9 %collective-permute-start.4 = (bf16[2,128,256]{2,1,0:T(8,128)(2,1)S(1)}, bf16[2,128,256]{2,1,0:T(8,128)(2,1)S(1)}, u32[]{:S(2)}, u32[]{:S(2)}) collective-permute-start(bf16[2,128,256]{2,1,0:T(8,128)(2,1)S(1)} %get-tuple-element.43), channel_id=1, source_target_pairs={{4,0},{6,2},{0,4},{2,6},{5,1},{7,3},{1,5},{3,7},{12,8},{14,10},{8,... | collective-permute-start | bytes 393224 | tf_op jit(solution)/shard_map/ppermute | solution.py:331
  62.8 15.8 %collective-permute-start.3 = (bf16[2,2,128,256]{3,2,1,0:T(8,128)(2,1)S(1)}, bf16[2,2,128,256]{3,2,1,0:T(8,128)(2,1)S(1)}, u32[]{:S(2)}, u32[]{:S(2)}) collective-permute-start(bf16[2,2,128,256]{3,2,1,0:T(8,128)(2,1)S(1)} %pad_maximum_fusion.go0_ref), channel_id=1, source_target_pairs={{6,0},{0,2},{2,4},{4,6},{7,1},{1,3},{3,5},{5,7},{14,8},{8,10},{10,... | collective-permute-start | bytes 786440 | tf_op jit(solution)/shard_map/ppermute | solution.py:331
  66.8 11.8 %collective-permute-start.2 = (bf16[2,2,128,256]{3,2,1,0:T(8,128)(2,1)S(1)}, bf16[2,2,128,256]{3,2,1,0:T(8,128)(2,1)S(1)}, u32[]{:S(2)}, u32[]{:S(2)}) collective-permute-start(bf16[2,2,128,256]{3,2,1,0:T(8,128)(2,1)S(1)} %pad_maximum_fusion.go0_ref), channel_id=1, source_target_pairs={{2,0},{4,2},{6,4},{0,6},{3,1},{5,3},{7,5},{1,7},{10,8},{12,10},{14... | collective-permute-start | bytes 786440 | tf_op jit(solution)/shard_map/ppermute | solution.py:331
  72.6 8.7 %collective-permute-start.6 = (bf16[2,128,512]{2,1,0:T(8,128)(2,1)S(1)}, bf16[2,128,512]{2,1,0:T(8,128)(2,1)S(1)}, u32[]{:S(2)}, u32[]{:S(2)}) collective-permute-start(bf16[2,128,512]{2,1,0:T(8,128)(2,1)S(1)} %get-tuple-element.31.own_ref), channel_id=1, source_target_pairs={{0,8},{8,0},{1,9},{9,1},{2,10},{10,2},{3,11},{11,3},{4,12},{12,4},... | collective-permute-start | bytes 786440 | tf_op jit(solution)/shard_map/ppermute | solution.py:350
  75.4 3.2 %collective-permute-start.5 = (bf16[2,128,256]{2,1,0:T(8,128)(2,1)S(1)}, bf16[2,128,256]{2,1,0:T(8,128)(2,1)S(1)}, u32[]{:S(2)}, u32[]{:S(2)}) collective-permute-start(bf16[2,128,256]{2,1,0:T(8,128)(2,1)S(1)} %collective-permute-done.4.go2_ref), channel_id=1, source_target_pairs={{0,1},{1,0},{2,3},{3,2},{4,5},{5,4},{6,7},{7,6},{8,9},{9,8},{10,11... | collective-permute-start | bytes 393224 | tf_op jit(solution)/shard_map/ppermute | solution.py:347
  84.0 24.6 %all-to-all-start.3 = ((bf16[64,16,128]{2,1,0:T(8,128)(2,1)}), bf16[64,16,128]{2,1,0:T(8,128)(2,1)S(1)}, u32[]{:S(2)}, u32[]{:S(2)}) async-start(bf16[64,16,128]{2,1,0:T(8,128)(2,1)} %grad_states.1), calls=%async_computation.3 | async-start | bytes 524288 | tf_op jit(solution)/shard_map/all_to_all | solution.py:256
  94.4 25.7 %collective-permute-start.7 = (f32[128,512]{1,0:T(8,128)S(1)}, f32[128,512]{1,0:T(8,128)S(1)}, u32[]{:S(2)}, u32[]{:S(2)}) collective-permute-start(f32[128,512]{1,0:T(8,128)S(1)} %get-tuple-element.27.send_ref), channel_id=1, source_target_pairs={{0,8},{8,0},{1,9},{9,1},{2,10},{10,2},{3,11},{11,3},{4,12},{12,4},... | collective-permute-start | bytes 786440 | tf_op jit(solution)/shard_map/ppermute | solution.py:355
  109.3 17.3 %all-to-all-start.4 = ((bf16[64,8,128]{2,1,0:T(8,128)(2,1)}), bf16[64,8,128]{2,1,0:T(8,128)(2,1)S(1)}, u32[]{:S(2)}, u32[]{:S(2)}) async-start(bf16[64,8,128]{2,1,0:T(8,128)(2,1)} %bitcast.14), calls=%async_computation.4 | async-start | bytes 262144 | tf_op jit(solution)/shard_map/all_to_all | solution.py:264
  116.5 10.2 %collective-permute-start.8 = (bf16[128,256]{1,0:T(8,128)(2,1)S(1)}, bf16[128,256]{1,0:T(8,128)(2,1)S(1)}, u32[]{:S(2)}, u32[]{:S(2)}) collective-permute-start(bf16[128,256]{1,0:T(8,128)(2,1)S(1)} %get-tuple-element.40), channel_id=1, source_target_pairs={{0,8},{8,0},{1,9},{9,1},{2,10},{10,2},{3,11},{11,3},{4,12},{12,4},... | collective-permute-start | bytes 196616 | tf_op jit(solution)/shard_map/ppermute | solution.py:359
Sparse Core Ops, SparseCore 0:
  31.7 43.9 all-gather.2
  83.0 32.5 reduce-scatter.1

commit v6 on v5

--- a/solution.py
+++ b/solution.py
@@ -347,6 +347,7 @@
     grad_parts += [grad_far, lax.ppermute(grad_far, "core", SWAP)]
     before = carried(state, False)
     pair, normed, scale, weights = attend(queries, keys, values, before)
+    pair, grad_parts[-1] = tied(pair, grad_parts[-1])
     other = lax.ppermute(pair, "zl", SWAP)
     own, send, weight = grad_normed_parts(place, weight, grad_parts)
     parts = project(weight, pair, other)

time: 138 us -> 138 us (level); the launches traced: 135 us -> 137 us
  waiting for transfers between devices: 38.2 us -> 40.8 us
    ppermute x1, waiting for transfers between devices: 0.01 us -> 3.96 us  [local(): other = lax.ppermute(pair, 'zl', SWAP)]
    all_to_all x1, waiting for transfers between devices: 10.7 us -> 7.33 us  [carried(): pieces = lax.all_to_all(state.reshape(64, 8, HEAD_DIM), CTX, 0, 0)]
    all_to_all x1, waiting for transfers between devices: 3.31 us -> 5.89 us  [carried(): back = lax.all_to_all(sums.reshape(64, 8, HEAD_DIM), CTX, 0, 0)]
    all_to_all x1, starting transfers between devices: 10.4 us -> 8.76 us  [later_states(): pieces = lax.all_to_all(states, CTX, 0, 0)]
  transfers between devices with their start and end apart: 16 -> 16, of which waited for: 8 -> 9; matrix products, arithmetic and copies ran while one was open for 1% -> 1% of each run, Pallas kernels for 7% -> 7%
where the time goes in v6:
time: 138 us; the launch traced here: 137 us
  starting transfers between devices  65.5 us (47%)
  waiting for transfers between devices  40.8 us (30%)
  between operations  14.3 us (10%)
  Pallas kernels  13.1 us (9%)
  local copies, waits for them, and re-layouts  3.2 us (2%)
    all_to_all x1, waiting for transfers between devices, later_states(): pieces = lax.all_to_all(states, CTX, 0, 0)  11.2 us
    all_to_all x1, starting transfers between devices, local(): rows = lax.all_to_all(repeated(out_weight.T, 4), 'zh', 0, 0)  10.3 us
    all_to_all x1, starting transfers between devices, carried(): pieces = lax.all_to_all(state.reshape(64, 8, HEAD_DIM), CTX, 0, 0)  9.9 us
    ppermute x3, starting transfers between devices, shifted(): return lax.ppermute(value, axis, [((i + step) % 4, i) for i in range(4)])  9.24 us
    all_to_all x1, starting transfers between devices, later_states(): pieces = lax.all_to_all(states, CTX, 0, 0)  8.76 us
    all_to_all x1, waiting for transfers between devices, carried(): pieces = lax.all_to_all(state.reshape(64, 8, HEAD_DIM), CTX, 0, 0)  7.33 us
    all_to_all x1, waiting for transfers between devices, carried(): back = lax.all_to_all(sums.reshape(64, 8, HEAD_DIM), CTX, 0, 0)  5.89 us
    all_to_all x1, waiting for transfers between devices, later_states(): back = lax.all_to_all(sums.reshape(64, 8, HEAD_DIM), CTX, 0, 0)  5.58 us
  transfers between devices with their start and end apart: 16, of which 9 were waited for; matrix products, arithmetic and copies ran while one was open for 1% of the time, Pallas kernels for 7%

profile of v6, /device:TPU:6, one launch (start us, length us, event | category | flops | bytes accessed | tf_op | source)
XLA Modules:
  0.0 136.9 jit_solution(7575021661193020584)
XLA Ops:
  7.2 1.6 %broadcast_in_dim.3 = bf16[4,64,512]{2,1,0:T(8,128)(2,1)} broadcast(bf16[64,512]{1,0:T(8,128)(2,1)} %bitcast.29), dimensions={1,2} | broadcast | bytes 327680 | tf_op jit(solution)/shard_map/broadcast_in_dim | solution.py:327
  8.8 10.3 %all-to-all-start = ((bf16[4,64,512]{2,1,0:T(8,128)(2,1)}), bf16[4,64,512]{2,1,0:T(8,128)(2,1)S(1)}, u32[]{:S(2)}, u32[]{:S(2)}) async-start(bf16[4,64,512]{2,1,0:T(8,128)(2,1)} %broadcast_in_dim.3), calls=%async_computation | async-start | bytes 524288 | tf_op jit(solution)/shard_map/all_to_all | solution.py:336
  20.2 3.4 %collective-permute-start = (bf16[128,256]{1,0:T(8,128)(2,1)S(1)}, bf16[128,256]{1,0:T(8,128)(2,1)S(1)}, u32[]{:S(2)}, u32[]{:S(2)}) collective-permute-start(bf16[128,256]{1,0:T(8,128)(2,1)S(1)} %get-tuple-element.24), channel_id=1, source_target_pairs={{0,8},{8,0},{1,9},{9,1},{2,10},{10,2},{3,11},{11,3},{4,12},{12,4},... | collective-permute-start | bytes 196616 | tf_op jit(solution)/shard_map/ppermute | solution.py:338
  23.6 1.8 %local_state.1 = bf16[512,128]{1,0:T(8,128)(2,1)} custom-call(bf16[128,512]{1,0:T(8,128)(2,1)} %k_ref.7, bf16[128,512]{1,0:T(8,128)(2,1)} %v_ref.7), custom_call_target="tpu_custom_call" | custom-call | flops 16777216 | bytes 400000 | tf_op jit(solution)/shard_map/local_state/pallas_call | solution.py:74
  25.4 2.7 %collective-permute-done = bf16[128,256]{1,0:T(8,128)(2,1)S(1)} collective-permute-done((bf16[128,256]{1,0:T(8,128)(2,1)S(1)}, bf16[128,256]{1,0:T(8,128)(2,1)S(1)}, u32[]{:S(2)}, u32[]{:S(2)}) %collective-permute-start) | collective-permute-done | bytes 65568 | tf_op jit(solution)/shard_map/ppermute | solution.py:338
  28.1 2.7 %all-to-all-done = bf16[4,64,512]{2,1,0:T(8,128)(2,1)S(1)} async-done(((bf16[4,64,512]{2,1,0:T(8,128)(2,1)}), bf16[4,64,512]{2,1,0:T(8,128)(2,1)S(1)}, u32[]{:S(2)}, u32[]{:S(2)}) %all-to-all-start) | async-done | bytes 262176 | tf_op jit(solution)/shard_map/all_to_all | solution.py:336
  31.5 9.9 %all-to-all-start.1 = ((bf16[64,8,128]{2,1,0:T(8,128)(2,1)}), bf16[64,8,128]{2,1,0:T(8,128)(2,1)S(1)}, u32[]{:S(2)}, u32[]{:S(2)}) async-start(bf16[64,8,128]{2,1,0:T(8,128)(2,1)} %bitcast.9), calls=%async_computation.1 | async-start | bytes 262144 | tf_op jit(solution)/shard_map/all_to_all | solution.py:132
  41.5 3.3 %collective-permute-start.4 = (bf16[2,128,256]{2,1,0:T(8,128)(2,1)S(1)}, bf16[2,128,256]{2,1,0:T(8,128)(2,1)S(1)}, u32[]{:S(2)}, u32[]{:S(2)}) collective-permute-start(bf16[2,128,256]{2,1,0:T(8,128)(2,1)S(1)} %get-tuple-element.47), channel_id=1, source_target_pairs={{4,0},{6,2},{0,4},{2,6},{5,1},{7,3},{1,5},{3,7},{12,8},{14,10},{8,... | collective-permute-start | bytes 393224 | tf_op jit(solution)/shard_map/ppermute | solution.py:331
  44.8 1.9 %collective-permute-start.1 = (bf16[2,128,256]{2,1,0:T(8,128)(2,1)S(1)}, bf16[2,128,256]{2,1,0:T(8,128)(2,1)S(1)}, u32[]{:S(2)}, u32[]{:S(2)}) collective-permute-start(bf16[2,128,256]{2,1,0:T(8,128)(2,1)S(1)} %get-tuple-element.47), channel_id=1, source_target_pairs={{0,1},{1,0},{2,3},{3,2},{4,5},{5,4},{6,7},{7,6},{8,9},{9,8},{10,11... | collective-permute-start | bytes 393224 | tf_op jit(solution)/shard_map/ppermute | solution.py:344
  46.7 7.3 %all-to-all-done.1 = bf16[64,8,128]{2,1,0:T(8,128)(2,1)S(1)} async-done(((bf16[64,8,128]{2,1,0:T(8,128)(2,1)}), bf16[64,8,128]{2,1,0:T(8,128)(2,1)S(1)}, u32[]{:S(2)}, u32[]{:S(2)}) %all-to-all-start.1) | async-done | bytes 131104 | tf_op jit(solution)/shard_map/all_to_all | solution.py:132
  54.8 5.4 %all-to-all-start.2 = ((bf16[64,8,128]{2,1,0:T(8,128)(2,1)}), bf16[64,8,128]{2,1,0:T(8,128)(2,1)S(1)}, u32[]{:S(2)}, u32[]{:S(2)}) async-start(bf16[64,8,128]{2,1,0:T(8,128)(2,1)} %bitcast.11), calls=%async_computation.2 | async-start | bytes 262144 | tf_op jit(solution)/shard_map/all_to_all | solution.py:134
  60.2 2.1 %collective-permute-start.5 = (bf16[2,128,256]{2,1,0:T(8,128)(2,1)S(1)}, bf16[2,128,256]{2,1,0:T(8,128)(2,1)S(1)}, u32[]{:S(2)}, u32[]{:S(2)}) collective-permute-start(bf16[2,128,256]{2,1,0:T(8,128)(2,1)S(1)} %collective-permute-done.4.go2_ref), channel_id=1, source_target_pairs={{0,1},{1,0},{2,3},{3,2},{4,5},{5,4},{6,7},{7,6},{8,9},{9,8},{10,11... | collective-permute-start | bytes 393224 | tf_op jit(solution)/shard_map/ppermute | solution.py:347
  62.4 4.0 %collective-permute-start.3 = (bf16[2,2,128,256]{3,2,1,0:T(8,128)(2,1)S(1)}, bf16[2,2,128,256]{3,2,1,0:T(8,128)(2,1)S(1)}, u32[]{:S(2)}, u32[]{:S(2)}) collective-permute-start(bf16[2,2,128,256]{3,2,1,0:T(8,128)(2,1)S(1)} %pad_maximum_fusion.go0_ref), channel_id=1, source_target_pairs={{6,0},{0,2},{2,4},{4,6},{7,1},{1,3},{3,5},{5,7},{14,8},{8,10},{10,... | collective-permute-start | bytes 786440 | tf_op jit(solution)/shard_map/ppermute | solution.py:331
  66.4 1.9 %collective-permute-start.2 = (bf16[2,2,128,256]{3,2,1,0:T(8,128)(2,1)S(1)}, bf16[2,2,128,256]{3,2,1,0:T(8,128)(2,1)S(1)}, u32[]{:S(2)}, u32[]{:S(2)}) collective-permute-start(bf16[2,2,128,256]{3,2,1,0:T(8,128)(2,1)S(1)} %pad_maximum_fusion.go0_ref), channel_id=1, source_target_pairs={{2,0},{4,2},{6,4},{0,6},{3,1},{5,3},{7,5},{1,7},{10,8},{12,10},{14... | collective-permute-start | bytes 786440 | tf_op jit(solution)/shard_map/ppermute | solution.py:331
  68.4 5.9 %all-to-all-done.2 = bf16[64,8,128]{2,1,0:T(8,128)(2,1)S(1)} async-done(((bf16[64,8,128]{2,1,0:T(8,128)(2,1)}), bf16[64,8,128]{2,1,0:T(8,128)(2,1)S(1)}, u32[]{:S(2)}, u32[]{:S(2)}) %all-to-all-start.2) | async-done | bytes 131104 | tf_op jit(solution)/shard_map/all_to_all | solution.py:134
  74.8 2.7 %collective-permute-start.6 = (bf16[2,128,512]{2,1,0:T(8,128)(2,1)S(1)}, bf16[2,128,512]{2,1,0:T(8,128)(2,1)S(1)}, u32[]{:S(2)}, u32[]{:S(2)}) collective-permute-start(bf16[2,128,512]{2,1,0:T(8,128)(2,1)S(1)} %get-tuple-element.35.own_ref), channel_id=1, source_target_pairs={{0,8},{8,0},{1,9},{9,1},{2,10},{10,2},{3,11},{11,3},{4,12},{12,4},... | collective-permute-start | bytes 786440 | tf_op jit(solution)/shard_map/ppermute | solution.py:351
  77.8 2.6 %grad_normed.1 = (f32[128,512]{1,0:T(8,128)S(1)}, f32[128,512]{1,0:T(8,128)S(1)}, bf16[8,256,512]{2,1,0:T(8,128)(2,1)S(1)}) custom-call(s32[3]{0:T(128)S(1)} %pad_add_fusion.place_ref, bf16[8,256,512]{2,1,0:T(8,128)(2,1)} %bitcast.27, bf16[2,2,128,256]{3,2,1,0:T(8,128)(2,1)S(1)} %pad_maximum_fusion.go0_ref, ...), custom_call_target="tpu_custom_call" | custom-call | flops 536870912 | bytes 4000000 | tf_op jit(solution)/shard_map/grad_normed/pallas_call | solution.py:181
  80.4 4.0 %collective-permute-done.6.other_ref = bf16[2,128,512]{2,1,0:T(8,128)(2,1)S(1)} collective-permute-done((bf16[2,128,512]{2,1,0:T(8,128)(2,1)S(1)}, bf16[2,128,512]{2,1,0:T(8,128)(2,1)S(1)}, u32[]{:S(2)}, u32[]{:S(2)}) %collective-permute-start.6) | collective-permute-done | bytes 262176 | tf_op jit(solution)/shard_map/ppermute | solution.py:351
  87.1 8.8 %all-to-all-start.3 = ((bf16[64,16,128]{2,1,0:T(8,128)(2,1)}), bf16[64,16,128]{2,1,0:T(8,128)(2,1)S(1)}, u32[]{:S(2)}, u32[]{:S(2)}) async-start(bf16[64,16,128]{2,1,0:T(8,128)(2,1)} %grad_states.1), calls=%async_computation.3 | async-start | bytes 524288 | tf_op jit(solution)/shard_map/all_to_all | solution.py:256
  95.8 3.5 %collective-permute-start.7 = (f32[128,512]{1,0:T(8,128)S(1)}, f32[128,512]{1,0:T(8,128)S(1)}, u32[]{:S(2)}, u32[]{:S(2)}) collective-permute-start(f32[128,512]{1,0:T(8,128)S(1)} %get-tuple-element.32.send_ref), channel_id=1, source_target_pairs={{0,8},{8,0},{1,9},{9,1},{2,10},{10,2},{3,11},{11,3},{4,12},{12,4},... | collective-permute-start | bytes 786440 | tf_op jit(solution)/shard_map/ppermute | solution.py:356
  99.3 11.2 %all-to-all-done.3 = bf16[64,16,128]{2,1,0:T(8,128)(2,1)S(1)} async-done(((bf16[64,16,128]{2,1,0:T(8,128)(2,1)}), bf16[64,16,128]{2,1,0:T(8,128)(2,1)S(1)}, u32[]{:S(2)}, u32[]{:S(2)}) %all-to-all-start.3) | async-done | bytes 262176 | tf_op jit(solution)/shard_map/all_to_all | solution.py:256
  111.2 4.6 %all-to-all-start.4 = ((bf16[64,8,128]{2,1,0:T(8,128)(2,1)}), bf16[64,8,128]{2,1,0:T(8,128)(2,1)S(1)}, u32[]{:S(2)}, u32[]{:S(2)}) async-start(bf16[64,8,128]{2,1,0:T(8,128)(2,1)} %bitcast.14), calls=%async_computation.4 | async-start | bytes 262144 | tf_op jit(solution)/shard_map/all_to_all | solution.py:264
  117.9 3.6 %collective-permute-start.8 = (bf16[128,256]{1,0:T(8,128)(2,1)S(1)}, bf16[128,256]{1,0:T(8,128)(2,1)S(1)}, u32[]{:S(2)}, u32[]{:S(2)}) collective-permute-start(bf16[128,256]{1,0:T(8,128)(2,1)S(1)} %get-tuple-element.44), channel_id=1, source_target_pairs={{0,8},{8,0},{1,9},{9,1},{2,10},{10,2},{3,11},{11,3},{4,12},{12,4},... | collective-permute-start | bytes 196616 | tf_op jit(solution)/shard_map/ppermute | solution.py:360
  123.0 5.6 %all-to-all-done.4 = bf16[64,8,128]{2,1,0:T(8,128)(2,1)S(1)} async-done(((bf16[64,8,128]{2,1,0:T(8,128)(2,1)}), bf16[64,8,128]{2,1,0:T(8,128)(2,1)S(1)}, u32[]{:S(2)}, u32[]{:S(2)}) %all-to-all-start.4) | async-done | bytes 131104 | tf_op jit(solution)/shard_map/all_to_all | solution.py:264
  (33 shorter events, 11.8 us)
Async XLA Ops:
  7.2 67.1 %copy-start.1 = (bf16[128,512]{1,0:T(8,128)(2,1)S(1)}, bf16[128,512]{1,0:T(8,128)(2,1)}, u32[]{:S(2)}) copy-start(bf16[128,512]{1,0:T(8,128)(2,1)} %v_ref.7) | copy-start | bytes 393220
  7.2 67.1 %copy-start = (bf16[128,512]{1,0:T(8,128)(2,1)S(1)}, bf16[128,512]{1,0:T(8,128)(2,1)}, u32[]{:S(2)}) copy-start(bf16[128,512]{1,0:T(8,128)(2,1)} %k_ref.7) | copy-start | bytes 393220
  7.2 67.1 %copy-start.2 = (bf16[128,512]{1,0:T(8,128)(2,1)S(1)}, bf16[128,512]{1,0:T(8,128)(2,1)}, u32[]{:S(2)}) copy-start(bf16[128,512]{1,0:T(8,128)(2,1)} %q_ref.5) | copy-start | bytes 393220
  8.8 22.0 %all-to-all-start = ((bf16[4,64,512]{2,1,0:T(8,128)(2,1)}), bf16[4,64,512]{2,1,0:T(8,128)(2,1)S(1)}, u32[]{:S(2)}, u32[]{:S(2)}) async-start(bf16[4,64,512]{2,1,0:T(8,128)(2,1)} %broadcast_in_dim.3), calls=%async_computation | async-start | bytes 524288 | tf_op jit(solution)/shard_map/all_to_all | solution.py:336
  19.1 58.7 %all-gather.3.cloned.1.call-start = ((), (), s32[]{:S(2)}) async-start(), calls=%async_computation.7 | async-start | bytes 2359296 | tf_op jit(solution)/shard_map/all_gather | solution.py:342
  20.2 7.9 %collective-permute-start = (bf16[128,256]{1,0:T(8,128)(2,1)S(1)}, bf16[128,256]{1,0:T(8,128)(2,1)S(1)}, u32[]{:S(2)}, u32[]{:S(2)}) collective-permute-start(bf16[128,256]{1,0:T(8,128)(2,1)S(1)} %get-tuple-element.24), channel_id=1, source_target_pairs={{0,8},{8,0},{1,9},{9,1},{2,10},{10,2},{3,11},{11,3},{4,12},{12,4},... | collective-permute-start | bytes 196616 | tf_op jit(solution)/shard_map/ppermute | solution.py:338
  30.8 0.7 copy-start.3
  31.5 22.5 %all-to-all-start.1 = ((bf16[64,8,128]{2,1,0:T(8,128)(2,1)}), bf16[64,8,128]{2,1,0:T(8,128)(2,1)S(1)}, u32[]{:S(2)}, u32[]{:S(2)}) async-start(bf16[64,8,128]{2,1,0:T(8,128)(2,1)} %bitcast.9), calls=%async_computation.1 | async-start | bytes 262144 | tf_op jit(solution)/shard_map/all_to_all | solution.py:132
  41.5 18.7 %collective-permute-start.4 = (bf16[2,128,256]{2,1,0:T(8,128)(2,1)S(1)}, bf16[2,128,256]{2,1,0:T(8,128)(2,1)S(1)}, u32[]{:S(2)}, u32[]{:S(2)}) collective-permute-start(bf16[2,128,256]{2,1,0:T(8,128)(2,1)S(1)} %get-tuple-element.47), channel_id=1, source_target_pairs={{4,0},{6,2},{0,4},{2,6},{5,1},{7,3},{1,5},{3,7},{12,8},{14,10},{8,... | collective-permute-start | bytes 393224 | tf_op jit(solution)/shard_map/ppermute | solution.py:331
  44.8 17.6 %collective-permute-start.1 = (bf16[2,128,256]{2,1,0:T(8,128)(2,1)S(1)}, bf16[2,128,256]{2,1,0:T(8,128)(2,1)S(1)}, u32[]{:S(2)}, u32[]{:S(2)}) collective-permute-start(bf16[2,128,256]{2,1,0:T(8,128)(2,1)S(1)} %get-tuple-element.47), channel_id=1, source_target_pairs={{0,1},{1,0},{2,3},{3,2},{4,5},{5,4},{6,7},{7,6},{8,9},{9,8},{10,11... | collective-permute-start | bytes 393224 | tf_op jit(solution)/shard_map/ppermute | solution.py:344
  54.8 19.4 %all-to-all-start.2 = ((bf16[64,8,128]{2,1,0:T(8,128)(2,1)}), bf16[64,8,128]{2,1,0:T(8,128)(2,1)S(1)}, u32[]{:S(2)}, u32[]{:S(2)}) async-start(bf16[64,8,128]{2,1,0:T(8,128)(2,1)} %bitcast.11), calls=%async_computation.2 | async-start | bytes 262144 | tf_op jit(solution)/shard_map/all_to_all | solution.py:134
  60.2 56.8 %reduce-scatter.2.cloned.1.call-start = ((), (), s32[]{:S(2)}) async-start(), calls=%async_computation.6 | async-start | bytes 1179648 | tf_op jit(solution)/shard_map/reduce_scatter | solution.py:354
  60.2 14.5 %collective-permute-start.5 = (bf16[2,128,256]{2,1,0:T(8,128)(2,1)S(1)}, bf16[2,128,256]{2,1,0:T(8,128)(2,1)S(1)}, u32[]{:S(2)}, u32[]{:S(2)}) collective-permute-start(bf16[2,128,256]{2,1,0:T(8,128)(2,1)S(1)} %collective-permute-done.4.go2_ref), channel_id=1, source_target_pairs={{0,1},{1,0},{2,3},{3,2},{4,5},{5,4},{6,7},{7,6},{8,9},{9,8},{10,11... | collective-permute-start | bytes 393224 | tf_op jit(solution)/shard_map/ppermute | solution.py:347
  62.4 15.1 %collective-permute-start.3 = (bf16[2,2,128,256]{3,2,1,0:T(8,128)(2,1)S(1)}, bf16[2,2,128,256]{3,2,1,0:T(8,128)(2,1)S(1)}, u32[]{:S(2)}, u32[]{:S(2)}) collective-permute-start(bf16[2,2,128,256]{3,2,1,0:T(8,128)(2,1)S(1)} %pad_maximum_fusion.go0_ref), channel_id=1, source_target_pairs={{6,0},{0,2},{2,4},{4,6},{7,1},{1,3},{3,5},{5,7},{14,8},{8,10},{10,... | collective-permute-start | bytes 786440 | tf_op jit(solution)/shard_map/ppermute | solution.py:331
  66.4 11.3 %collective-permute-start.2 = (bf16[2,2,128,256]{3,2,1,0:T(8,128)(2,1)S(1)}, bf16[2,2,128,256]{3,2,1,0:T(8,128)(2,1)S(1)}, u32[]{:S(2)}, u32[]{:S(2)}) collective-permute-start(bf16[2,2,128,256]{3,2,1,0:T(8,128)(2,1)S(1)} %pad_maximum_fusion.go0_ref), channel_id=1, source_target_pairs={{2,0},{4,2},{6,4},{0,6},{3,1},{5,3},{7,5},{1,7},{10,8},{12,10},{14... | collective-permute-start | bytes 786440 | tf_op jit(solution)/shard_map/ppermute | solution.py:331
  74.8 9.6 %collective-permute-start.6 = (bf16[2,128,512]{2,1,0:T(8,128)(2,1)S(1)}, bf16[2,128,512]{2,1,0:T(8,128)(2,1)S(1)}, u32[]{:S(2)}, u32[]{:S(2)}) collective-permute-start(bf16[2,128,512]{2,1,0:T(8,128)(2,1)S(1)} %get-tuple-element.35.own_ref), channel_id=1, source_target_pairs={{0,8},{8,0},{1,9},{9,1},{2,10},{10,2},{3,11},{11,3},{4,12},{12,4},... | collective-permute-start | bytes 786440 | tf_op jit(solution)/shard_map/ppermute | solution.py:351
  87.1 23.5 %all-to-all-start.3 = ((bf16[64,16,128]{2,1,0:T(8,128)(2,1)}), bf16[64,16,128]{2,1,0:T(8,128)(2,1)S(1)}, u32[]{:S(2)}, u32[]{:S(2)}) async-start(bf16[64,16,128]{2,1,0:T(8,128)(2,1)} %grad_states.1), calls=%async_computation.3 | async-start | bytes 524288 | tf_op jit(solution)/shard_map/all_to_all | solution.py:256
  95.8 25.7 %collective-permute-start.7 = (f32[128,512]{1,0:T(8,128)S(1)}, f32[128,512]{1,0:T(8,128)S(1)}, u32[]{:S(2)}, u32[]{:S(2)}) collective-permute-start(f32[128,512]{1,0:T(8,128)S(1)} %get-tuple-element.32.send_ref), channel_id=1, source_target_pairs={{0,8},{8,0},{1,9},{9,1},{2,10},{10,2},{3,11},{11,3},{4,12},{12,4},... | collective-permute-start | bytes 786440 | tf_op jit(solution)/shard_map/ppermute | solution.py:356
  111.2 17.3 %all-to-all-start.4 = ((bf16[64,8,128]{2,1,0:T(8,128)(2,1)}), bf16[64,8,128]{2,1,0:T(8,128)(2,1)S(1)}, u32[]{:S(2)}, u32[]{:S(2)}) async-start(bf16[64,8,128]{2,1,0:T(8,128)(2,1)} %bitcast.14), calls=%async_computation.4 | async-start | bytes 262144 | tf_op jit(solution)/shard_map/all_to_all | solution.py:264
  117.9 10.7 %collective-permute-start.8 = (bf16[128,256]{1,0:T(8,128)(2,1)S(1)}, bf16[128,256]{1,0:T(8,128)(2,1)S(1)}, u32[]{:S(2)}, u32[]{:S(2)}) collective-permute-start(bf16[128,256]{1,0:T(8,128)(2,1)S(1)} %get-tuple-element.44), channel_id=1, source_target_pairs={{0,8},{8,0},{1,9},{9,1},{2,10},{10,2},{3,11},{11,3},{4,12},{12,4},... | collective-permute-start | bytes 196616 | tf_op jit(solution)/shard_map/ppermute | solution.py:360
Sparse Core Ops, SparseCore 0:
  31.7 43.9 all-gather.2
  86.0 30.9 reduce-scatter.1
